TPU v7x, 32 devices: a whole 2x2x4 slice. The times are simulated.
32 devices in a mesh: tile: 8 (over z, x), ens: 4 (over y, core).
Axes of the slice: x: 2, y: 2, z: 4, core: 2. Of those that a mesh axis runs over, the one named last changes fastest.
Arguments:
- features: bfloat16 [4, 8, 16, 16, 256], P('ens', 'tile'), may hold values from -6 to 6
- cotangent: bfloat16 [4, 8, 16, 16, 256], P('ens', 'tile'), may hold values from -6 to 6
- kernel: float32 [49, 256], replicated, may hold values from -0.875 to 0.875
- weight_in: bfloat16 [256, 1024], replicated, may hold values from -0.375 to 0.375
- weight_out: bfloat16 [1024, 256], replicated, may hold values from -0.1875 to 0.1875
- tile_neighbour: int32 [8, 4], P('tile'), may hold values from 0 to 7, as said below
- edge_code: int32 [8, 4], P('tile'), may hold values from 0 to 7, as said below
Outputs:
- grad_features: bfloat16 [4, 8, 16, 16, 256], P('ens', 'tile')
- grad_kernel: float32 [49, 256], replicated
- grad_weight_in: float32 [256, 1024], replicated
- grad_weight_out: float32 [1024, 256], replicated
Inputs may be any that keep to these rules, and one draw needn't show every extreme that they name: `tile_neighbour`: tile t is held by index t // 1 of tile; every neighbour of tile t is held by that same index, the one before it or the one after it, cyclically. edge_code % 4 names the neighbour's edge (0 top, 1 bottom, 2 left, 3 right); 4 or more means reversed along the edge.
All inputs are finite; a program needn't handle non-finite values.
Results may differ from a plain program's by a relative error of at most 0.015.
Values may be sent and summed in bfloat16 or wider, within the bound.
No kernel may reach another device: no remote copies, remote signals or barrier semaphores. Data moves between devices by JAX's collectives and lax.ppermute only.
A program may use at most 64 MiB of HBM per device.

v0:
```python
import jax
import jax.numpy as jnp
from jax import lax
from jax.sharding import PartitionSpec as P

C = 256
KERNEL_TAPS = 7
DILATION_STEP = 2
HALO = 6


def from_behind(x, axis, by):
    length = lax.axis_size(axis)
    return lax.ppermute(x, axis, [(i, (i + by) % length) for i in range(length)])


def pad_axis(values, from_end, before, later):
    widths = [(0, 0)] * values.ndim
    widths[values.ndim - from_end] = (before, later)
    return jnp.pad(values, widths)


def edge_strips(field_in, depth_rows):
    top_side = field_in[..., :depth_rows, :, :]
    bottom_side = jnp.flip(field_in[..., -depth_rows:, :, :], -3)
    left_side = jnp.swapaxes(field_in[..., :, :depth_rows, :], -3, -2)
    right_side = jnp.swapaxes(jnp.flip(field_in[..., :, -depth_rows:, :], -2), -3, -2)
    return jnp.stack([top_side, bottom_side, left_side, right_side], -4)


def place_edges(strips, edge_length):
    depth_rows = strips.shape[-3]
    extra = edge_length - depth_rows
    top_side = pad_axis(strips[..., 0, :, :, :], 3, 0, extra)
    bottom_side = pad_axis(jnp.flip(strips[..., 1, :, :, :], -3), 3, extra, 0)
    left_side = pad_axis(jnp.swapaxes(strips[..., 2, :, :, :], -3, -2), 2, 0, extra)
    right_side = pad_axis(jnp.flip(jnp.swapaxes(strips[..., 3, :, :, :], -3, -2), -2), 2, extra, 0)
    return top_side + bottom_side + left_side + right_side


def assemble(field_in, side_cells):
    top_block = jnp.flip(side_cells[..., 0, :, :, :], -3)
    bottom_block = side_cells[..., 1, :, :, :]
    left_block = jnp.flip(jnp.swapaxes(side_cells[..., 2, :, :, :], -3, -2), -2)
    right_block = jnp.swapaxes(side_cells[..., 3, :, :, :], -3, -2)
    middle = jnp.concatenate([left_block, field_in, right_block], -2)
    top_full = pad_axis(top_block, 2, HALO, HALO)
    bottom_full = pad_axis(bottom_block, 2, HALO, HALO)
    return jnp.concatenate([top_full, middle, bottom_full], -3)


def rim_cells(grad_padded_tile):
    edge_length = grad_padded_tile.shape[-2] - 2 * HALO
    inner = grad_padded_tile[..., HALO : HALO + edge_length, HALO : HALO + edge_length, :]
    top_side = jnp.flip(grad_padded_tile[..., :HALO, HALO : HALO + edge_length, :], -3)
    bottom_side = grad_padded_tile[..., HALO + edge_length :, HALO : HALO + edge_length, :]
    left_side = jnp.swapaxes(
        jnp.flip(grad_padded_tile[..., HALO : HALO + edge_length, :HALO, :], -2), -3, -2
    )
    right_side = jnp.swapaxes(
        grad_padded_tile[..., HALO : HALO + edge_length, HALO + edge_length :, :], -3, -2
    )
    return (inner, jnp.stack([top_side, bottom_side, left_side, right_side], -4))


def depthwise(padded_tile, kernel):
    edge_length = padded_tile.shape[-2] - 2 * HALO
    summed = jnp.zeros(
        padded_tile.shape[:-3] + (edge_length, edge_length, padded_tile.shape[-1]), jnp.float32
    )
    for first_operand in range(KERNEL_TAPS):
        for second_operand in range(KERNEL_TAPS):
            tap_window = padded_tile[
                ...,
                DILATION_STEP * first_operand : DILATION_STEP * first_operand + edge_length,
                DILATION_STEP * second_operand : DILATION_STEP * second_operand + edge_length,
                :,
            ].astype(jnp.float32)
            summed = summed + tap_window * kernel[first_operand * KERNEL_TAPS + second_operand]
    return summed


def depthwise_back(grad_convolved, kernel):
    edge_length = grad_convolved.shape[-2]
    full_len = edge_length + 2 * HALO
    grad_padded_tile = jnp.zeros(
        grad_convolved.shape[:-3] + (full_len, full_len, grad_convolved.shape[-1]), jnp.float32
    )
    for first_operand in range(KERNEL_TAPS):
        for second_operand in range(KERNEL_TAPS):
            grad_padded_tile = grad_padded_tile.at[
                ...,
                DILATION_STEP * first_operand : DILATION_STEP * first_operand + edge_length,
                DILATION_STEP * second_operand : DILATION_STEP * second_operand + edge_length,
                :,
            ].add(grad_convolved * kernel[first_operand * KERNEL_TAPS + second_operand])
    return grad_padded_tile


def tap_sums(padded_tile, grad_convolved):
    edge_length = grad_convolved.shape[-2]
    channels = grad_convolved.shape[-1]
    tap_rows = []
    for first_operand in range(KERNEL_TAPS):
        for second_operand in range(KERNEL_TAPS):
            tap_window = padded_tile[
                ...,
                DILATION_STEP * first_operand : DILATION_STEP * first_operand + edge_length,
                DILATION_STEP * second_operand : DILATION_STEP * second_operand + edge_length,
                :,
            ].astype(jnp.float32)
            tap_rows.append(jnp.sum((tap_window * grad_convolved).reshape(-1, channels), 0))
    return jnp.stack(tap_rows)


def normalize(conv):
    mean_value = jnp.mean(conv, -1, keepdims=True)
    centred = conv - mean_value
    inv_std = lax.rsqrt(jnp.mean(centred * centred, -1, keepdims=True) + 1e-06)
    return (centred * inv_std, inv_std)


def neighbour_sides(field_in, source, flipped_mask):
    members = field_in.shape[0]
    tile_local = field_in.shape[1]
    edge_length = field_in.shape[2]
    strips = edge_strips(field_in, HALO).reshape(members, tile_local * 4, HALO, edge_length, C)
    from_before = from_behind(strips, "tile", 1)
    from_ahead = from_behind(strips, "tile", -1)
    candidates = jnp.concatenate([from_before, strips, from_ahead], 1)
    side_cells = jnp.take(candidates, source, axis=1).reshape(
        members, tile_local, 4, HALO, edge_length, C
    )
    return jnp.where(flipped_mask, jnp.flip(side_cells, -2), side_cells)


def body(features, cotangent, kernel, weight_in, weight_out, tile_neighbour, edge_code):
    members = features.shape[0]
    tile_local = features.shape[1]
    edge_length = features.shape[2]
    position = lax.axis_index("tile")
    owners = lax.axis_size("tile")
    holder = tile_neighbour // tile_local
    offset = (holder - position + 1) % owners
    source = ((offset * tile_local + tile_neighbour % tile_local) * 4 + edge_code % 4).reshape(-1)
    flipped_mask = (edge_code >= 4)[:, :, None, None, None]
    pixel_total = owners * lax.axis_size("ens") * members * tile_local * edge_length * edge_length
    norm_factor = 1.0 / jnp.sqrt(jnp.float32(pixel_total))
    side_cells = neighbour_sides(features, source, flipped_mask)
    padded_tile = assemble(features, side_cells)
    conv = depthwise(padded_tile, kernel)
    normed_f, inv_std = normalize(conv)
    normed = normed_f.astype(jnp.bfloat16).reshape(-1, C)
    preact = jnp.dot(normed, weight_in, preferred_element_type=jnp.float32)
    hidden = jax.nn.gelu(preact).astype(jnp.bfloat16)
    grad_rows = cotangent.reshape(-1, C)
    part_out = lax.dot_general(
        hidden, grad_rows, (((0,), (0,)), ((), ())), preferred_element_type=jnp.float32
    )
    d_hidden = lax.dot_general(
        grad_rows, weight_out, (((1,), (1,)), ((), ())), preferred_element_type=jnp.float32
    )
    _, pull_back = jax.vjp(jax.nn.gelu, preact)
    d_preact = pull_back(d_hidden)[0].astype(jnp.bfloat16)
    part_in = lax.dot_general(
        normed, d_preact, (((0,), (0,)), ((), ())), preferred_element_type=jnp.float32
    )
    d_normed = lax.dot_general(
        d_preact, weight_in, (((1,), (1,)), ((), ())), preferred_element_type=jnp.float32
    ).reshape(conv.shape)
    grad_convolved = inv_std * (
        d_normed
        - jnp.mean(d_normed, -1, keepdims=True)
        - normed_f * jnp.mean(d_normed * normed_f, -1, keepdims=True)
    )
    grad_padded_tile = depthwise_back(grad_convolved, kernel)
    inner, side_grads = rim_cells(grad_padded_tile)
    side_grads = jnp.where(flipped_mask, jnp.flip(side_grads, -2), side_grads)
    flat_grads = side_grads.reshape(members, tile_local * 4, HALO * edge_length * C)
    slots = tile_local * 4
    onehot = (source[None, :] == jnp.arange(3 * slots, dtype=jnp.int32)[:, None]).astype(
        jnp.float32
    )
    pooled = jnp.einsum("qs,msf->mqf", onehot, flat_grads, precision=lax.Precision.HIGHEST)
    to_before = pooled[:, :slots]
    own_part = pooled[:, slots : 2 * slots]
    to_ahead = pooled[:, 2 * slots :]
    from_later = from_behind(to_before.astype(jnp.bfloat16), "tile", -1).astype(to_before.dtype)
    from_earlier = from_behind(to_ahead.astype(jnp.bfloat16), "tile", 1).astype(to_ahead.dtype)
    edge_back = (own_part + from_later + from_earlier).reshape(
        members, tile_local, 4, HALO, edge_length, C
    )
    part_kernel = tap_sums(padded_tile, grad_convolved)
    pending = (part_kernel, part_in, part_out)
    summed = lax.psum((pending[0], pending[1], pending[2]), ("tile", "ens"))
    summed_kernel = summed[0]
    summed_in = summed[1]
    summed_out = summed[2]
    grad_features = (
        cotangent.astype(jnp.float32) + inner + place_edges(edge_back, edge_length)
    ).astype(jnp.bfloat16)
    return (
        grad_features,
        summed_kernel * norm_factor,
        summed_in * norm_factor,
        summed_out * norm_factor,
    )


def solution(mesh):
    in_specs = (
        P("ens", "tile", None, None, None),
        P("ens", "tile", None, None, None),
        P(),
        P(),
        P(),
        P("tile", None),
        P("tile", None),
    )
    out_specs = (P("ens", "tile", None, None, None), P(), P(), P())
    return jax.shard_map(body, mesh=mesh, in_specs=in_specs, out_specs=out_specs, check_vma=False)
```

profile of v0, /device:TPU:0, one launch (start us, length us, event | category | flops | bytes accessed | tf_op | source)
XLA Modules:
  0.0 287.6 jit_solution(13282349768673377111)
XLA Ops:
  7.3 1.0 fusion.150
  8.2 0.9 slice_bitcast_fusion.7
  9.6 3.0 %collective-permute-start = (bf16[1,4,6,16,256]{4,2,3,1,0:T(8,128)(2,1)S(1)}, bf16[1,4,6,16,256]{4,2,3,1,0:T(8,128)(2,1)S(1)}, u32[]{:S(2)}, u32[]{:S(2)}) collective-permute-start(bf16[1,4,6,16,256]{4,2,3,1,0:T(8,128)(2,1)S(1)} %maximum_bitcast_fusion.1), channel_id=1, source_target_pairs={{0,4},{4,8},{8,12},{12,16},{16,20},{20,24},{24,28},{28,0},{1,5},{5... | collective-permute-start | bytes 589832 | tf_op jit(solution)/shard_map/ppermute | solution.py:14
  12.6 3.1 %collective-permute-start.1 = (bf16[1,4,6,16,256]{4,2,3,1,0:T(8,128)(2,1)S(1)}, bf16[1,4,6,16,256]{4,2,3,1,0:T(8,128)(2,1)S(1)}, u32[]{:S(2)}, u32[]{:S(2)}) collective-permute-start(bf16[1,4,6,16,256]{4,2,3,1,0:T(8,128)(2,1)S(1)} %maximum_bitcast_fusion.1), channel_id=1, source_target_pairs={{0,28},{4,0},{8,4},{12,8},{16,12},{20,16},{24,20},{28,24},{1,29},{... | collective-permute-start | bytes 589832 | tf_op jit(solution)/shard_map/ppermute | solution.py:14
  15.7 1.0 fusion.151
  16.7 1.0 fusion.152
  17.9 0.9 fusion.153
  20.2 0.7 fusion.157
  20.9 0.7 and_reduce_fusion.4
  21.7 0.8 and_reduce_fusion.2
  23.7 0.7 and_reduce_fusion
  25.6 1.3 fusion.162
  28.9 2.2 fusion.144
  31.6 1.8 fusion.6
  34.1 1.6 fusion.113
  35.7 1.2 fusion.62
  37.0 1.9 add_select_fusion.5
  38.9 1.6 scatter-add.165
  40.6 2.6 add_select_fusion.4
  43.2 1.6 scatter-add.166
  44.8 2.7 add_select_fusion.3
  47.5 1.6 scatter-add.169
  49.1 2.6 add_select_fusion.2
  51.7 1.6 scatter-add.170
  53.3 2.6 add_select_fusion.1
  55.9 1.6 scatter-add.171
  57.5 2.6 add_select_fusion
  60.1 1.7 scatter-add.174
  61.8 0.8 fusion.127
  62.5 0.7 slice_add_fusion.42
  63.7 0.7 slice_add_fusion.41
  64.8 0.7 slice_add_fusion.40
  65.9 0.7 fusion.126
  66.7 0.7 slice_add_fusion.38
  67.8 0.7 slice_add_fusion.37
  68.8 0.7 fusion.125
  69.5 0.7 slice_add_fusion.35
  70.6 0.7 slice_add_fusion.34
  71.7 0.7 slice_add_fusion.33
  72.8 0.7 fusion.124
  73.5 0.7 slice_add_fusion.31
  74.6 0.7 slice_add_fusion.30
  75.7 0.8 fusion.123
  76.5 0.7 slice_add_fusion.28
  77.6 0.7 slice_add_fusion.27
  78.7 0.7 slice_add_fusion.26
  79.8 0.7 fusion.122
  80.5 0.7 slice_add_fusion.24
  81.6 0.7 slice_add_fusion.23
  82.7 0.8 fusion.121
  89.9 0.7 fusion.44
  92.3 1.3 fusion.163
  94.1 39.4 %psum.21 = f32[49,256]{1,0:T(8,128)} all-reduce(f32[49,256]{1,0:T(8,128)S(1)} %stack.239), channel_id=1, replica_groups=mesh['tile'=8,'ens'=4] {'tile','ens'}, use_global_device_ids=true, to_apply=%region_59.60 | all-reduce | flops 12544 | bytes 100352 | tf_op jit(solution)/shard_map/psum | solution.py:195
  134.6 0.8 fusion.161
  135.3 0.9 fusion.149
  136.2 3.9 %collective-permute-start.2 = (bf16[1,4,24576]{2,1,0:T(4,128)(2,1)}, bf16[1,4,24576]{2,1,0:T(4,128)(2,1)S(1)}, u32[]{:S(2)}, u32[]{:S(2)}) collective-permute-start(bf16[1,4,24576]{2,1,0:T(4,128)(2,1)} %get-tuple-element.668), channel_id=1, source_target_pairs={{0,28},{4,0},{8,4},{12,8},{16,12},{20,16},{24,20},{28,24},{1,29},{... | collective-permute-start | bytes 589832 | tf_op jit(solution)/shard_map/ppermute | solution.py:14
  140.1 1.6 fusion.9
  141.7 0.8 copy-done.9
  143.7 5.0 %collective-permute-done.3 = bf16[1,4,24576]{2,1,0:T(4,128)(2,1)} collective-permute-done((bf16[1,4,24576]{2,1,0:T(4,128)(2,1)}, bf16[1,4,24576]{2,1,0:T(4,128)(2,1)}, u32[]{:S(2)}, u32[]{:S(2)}) %collective-permute-start.3) | collective-permute-done | bytes 196640 | tf_op jit(solution)/shard_map/ppermute | solution.py:14
  148.8 1.1 fusion.14
  150.3 0.7 fusion.115
  151.0 126.2 %all-reduce.10.cloned.1.call-done = (f32[256,1024]{1,0:T(8,128)}, f32[1024,256]{1,0:T(8,128)}) async-done(((f32[256,1024]{1,0:T(8,128)}, f32[1024,256]{1,0:T(8,128)}), (f32[256,1024]{1,0:T(8,128)}, f32[1024,256]{1,0:T(8,128)})) %all-reduce.10.cloned.1.call-update) | async-done | bytes 2097168 | tf_op jit(solution)/shard_map/psum | solution.py:195
  277.2 2.4 broadcast_multiply_fusion
  279.6 1.1 broadcast_multiply_fusion.1
  (282 shorter events, 23.2 us)
Async XLA Ops:
  7.2 24.4 %copy-start = (bf16[256,1024]{1,0:T(8,128)(2,1)S(1)}, bf16[256,1024]{1,0:T(8,128)(2,1)}, u32[]{:S(2)}) copy-start(bf16[256,1024]{1,0:T(8,128)(2,1)} %param.108) | copy-start | bytes 1572868
  7.2 13.7 %copy-start.39 = (s32[5]{0:T(128)S(1)}, s32[5]{0:T(128)}, u32[]{:S(2)}) copy-start(s32[5]{0:T(128)} %constant.1557.clone.1) | copy-start | bytes 64
  7.2 17.8 %copy-start.83 = (s32[1,4]{1,0:T(1,128)S(1)}, s32[1,4]{1,0:T(1,128)}, u32[]{:S(2)}) copy-start(s32[1,4]{1,0:T(1,128)} %param.110) | copy-start | bytes 52
  7.2 17.8 %copy-start.84 = (s32[1,4]{1,0:T(1,128)S(1)}, s32[1,4]{1,0:T(1,128)}, u32[]{:S(2)}) copy-start(s32[1,4]{1,0:T(1,128)} %param.111) | copy-start | bytes 52
  7.2 18.4 %copy-start.5 = (bf16[1,1,16,16,256]{4,3,2,1,0:T(8,128)(2,1)S(1)}, bf16[1,1,16,16,256]{4,3,2,1,0:T(8,128)(2,1)}, u32[]{:S(2)}) copy-start(bf16[1,1,16,16,256]{4,3,2,1,0:T(8,128)(2,1)} %param.106) | copy-start | bytes 393220
  7.2 18.4 %copy-start.4 = (bf16[1024,256]{1,0:T(8,128)(2,1)S(1)}, bf16[1024,256]{1,0:T(8,128)(2,1)}, u32[]{:S(2)}) copy-start(bf16[1024,256]{1,0:T(8,128)(2,1)} %param.109) | copy-start | bytes 1572868
  7.2 270.0 %all-reduce.10.cloned.1.call-start = ((), (), s32[]{:S(2)}) async-start(), calls=%async_computation | async-start | bytes 4194304 | tf_op jit(solution)/shard_map/psum | solution.py:195
  9.6 17.3 %collective-permute-start = (bf16[1,4,6,16,256]{4,2,3,1,0:T(8,128)(2,1)S(1)}, bf16[1,4,6,16,256]{4,2,3,1,0:T(8,128)(2,1)S(1)}, u32[]{:S(2)}, u32[]{:S(2)}) collective-permute-start(bf16[1,4,6,16,256]{4,2,3,1,0:T(8,128)(2,1)S(1)} %maximum_bitcast_fusion.1), channel_id=1, source_target_pairs={{0,4},{4,8},{8,12},{12,16},{16,20},{20,24},{24,28},{28,0},{1,5},{5... | collective-permute-start | bytes 589832 | tf_op jit(solution)/shard_map/ppermute | solution.py:14
  12.6 14.3 %collective-permute-start.1 = (bf16[1,4,6,16,256]{4,2,3,1,0:T(8,128)(2,1)S(1)}, bf16[1,4,6,16,256]{4,2,3,1,0:T(8,128)(2,1)S(1)}, u32[]{:S(2)}, u32[]{:S(2)}) collective-permute-start(bf16[1,4,6,16,256]{4,2,3,1,0:T(8,128)(2,1)S(1)} %maximum_bitcast_fusion.1), channel_id=1, source_target_pairs={{0,28},{4,0},{8,4},{12,8},{16,12},{20,16},{24,20},{28,24},{1,29},{... | collective-permute-start | bytes 589832 | tf_op jit(solution)/shard_map/ppermute | solution.py:14
  17.7 10.9 %copy-start.10 = (f32[1,256]{1,0:T(1,128)}, f32[1,256]{1,0:T(1,128)S(1)}, u32[]{:S(2)}) copy-start(f32[1,256]{1,0:T(1,128)S(1)} %get-tuple-element.706) | copy-start | bytes 3076
  17.8 10.9 %copy-start.11 = (f32[1,256]{1,0:T(1,128)}, f32[1,256]{1,0:T(1,128)S(1)}, u32[]{:S(2)}) copy-start(f32[1,256]{1,0:T(1,128)S(1)} %get-tuple-element.707) | copy-start | bytes 3076
  17.8 10.9 %copy-start.12 = (f32[1,256]{1,0:T(1,128)}, f32[1,256]{1,0:T(1,128)S(1)}, u32[]{:S(2)}) copy-start(f32[1,256]{1,0:T(1,128)S(1)} %get-tuple-element.708) | copy-start | bytes 3076
  17.8 10.9 %copy-start.13 = (f32[1,256]{1,0:T(1,128)}, f32[1,256]{1,0:T(1,128)S(1)}, u32[]{:S(2)}) copy-start(f32[1,256]{1,0:T(1,128)S(1)} %get-tuple-element.709) | copy-start | bytes 3076
  17.8 10.9 %copy-start.14 = (f32[1,256]{1,0:T(1,128)}, f32[1,256]{1,0:T(1,128)S(1)}, u32[]{:S(2)}) copy-start(f32[1,256]{1,0:T(1,128)S(1)} %get-tuple-element.710) | copy-start | bytes 3076
  17.8 10.9 %copy-start.15 = (f32[1,256]{1,0:T(1,128)}, f32[1,256]{1,0:T(1,128)S(1)}, u32[]{:S(2)}) copy-start(f32[1,256]{1,0:T(1,128)S(1)} %get-tuple-element.711) | copy-start | bytes 3076
  17.8 10.9 %copy-start.16 = (f32[1,256]{1,0:T(1,128)}, f32[1,256]{1,0:T(1,128)S(1)}, u32[]{:S(2)}) copy-start(f32[1,256]{1,0:T(1,128)S(1)} %get-tuple-element.712) | copy-start | bytes 3076
  17.8 10.9 %copy-start.17 = (f32[1,256]{1,0:T(1,128)}, f32[1,256]{1,0:T(1,128)S(1)}, u32[]{:S(2)}) copy-start(f32[1,256]{1,0:T(1,128)S(1)} %get-tuple-element.713) | copy-start | bytes 3076
  17.8 10.9 %copy-start.18 = (f32[1,256]{1,0:T(1,128)}, f32[1,256]{1,0:T(1,128)S(1)}, u32[]{:S(2)}) copy-start(f32[1,256]{1,0:T(1,128)S(1)} %get-tuple-element.714) | copy-start | bytes 3076
  17.8 10.9 %copy-start.19 = (f32[1,256]{1,0:T(1,128)}, f32[1,256]{1,0:T(1,128)S(1)}, u32[]{:S(2)}) copy-start(f32[1,256]{1,0:T(1,128)S(1)} %get-tuple-element.715) | copy-start | bytes 3076
  17.8 10.9 %copy-start.20 = (f32[1,256]{1,0:T(1,128)}, f32[1,256]{1,0:T(1,128)S(1)}, u32[]{:S(2)}) copy-start(f32[1,256]{1,0:T(1,128)S(1)} %get-tuple-element.716) | copy-start | bytes 3076
  17.9 10.9 %copy-start.21 = (f32[1,256]{1,0:T(1,128)}, f32[1,256]{1,0:T(1,128)S(1)}, u32[]{:S(2)}) copy-start(f32[1,256]{1,0:T(1,128)S(1)} %get-tuple-element.717) | copy-start | bytes 3076
  17.9 10.9 %copy-start.22 = (f32[1,256]{1,0:T(1,128)}, f32[1,256]{1,0:T(1,128)S(1)}, u32[]{:S(2)}) copy-start(f32[1,256]{1,0:T(1,128)S(1)} %get-tuple-element.718) | copy-start | bytes 3076
  17.9 10.9 %copy-start.23 = (f32[1,256]{1,0:T(1,128)}, f32[1,256]{1,0:T(1,128)S(1)}, u32[]{:S(2)}) copy-start(f32[1,256]{1,0:T(1,128)S(1)} %get-tuple-element.719) | copy-start | bytes 3076
  17.9 10.9 %copy-start.24 = (f32[1,256]{1,0:T(1,128)}, f32[1,256]{1,0:T(1,128)S(1)}, u32[]{:S(2)}) copy-start(f32[1,256]{1,0:T(1,128)S(1)} %get-tuple-element.720) | copy-start | bytes 3076
  17.9 10.9 %copy-start.25 = (f32[1,256]{1,0:T(1,128)}, f32[1,256]{1,0:T(1,128)S(1)}, u32[]{:S(2)}) copy-start(f32[1,256]{1,0:T(1,128)S(1)} %get-tuple-element.721) | copy-start | bytes 3076
  17.9 10.9 %copy-start.26 = (f32[1,256]{1,0:T(1,128)}, f32[1,256]{1,0:T(1,128)S(1)}, u32[]{:S(2)}) copy-start(f32[1,256]{1,0:T(1,128)S(1)} %get-tuple-element.722) | copy-start | bytes 3076
  17.9 10.9 %copy-start.27 = (f32[1,256]{1,0:T(1,128)}, f32[1,256]{1,0:T(1,128)S(1)}, u32[]{:S(2)}) copy-start(f32[1,256]{1,0:T(1,128)S(1)} %get-tuple-element.723) | copy-start | bytes 3076
  17.9 10.9 %copy-start.35 = (f32[1,256]{1,0:T(1,128)}, f32[1,256]{1,0:T(1,128)S(1)}, u32[]{:S(2)}) copy-start(f32[1,256]{1,0:T(1,128)S(1)} %get-tuple-element.705) | copy-start | bytes 3076
  18.9 9.9 %copy-start.28 = (f32[1,256]{1,0:T(1,128)}, f32[1,256]{1,0:T(1,128)S(1)}, u32[]{:S(2)}) copy-start(f32[1,256]{1,0:T(1,128)S(1)} %get-tuple-element.725) | copy-start | bytes 3076
  18.9 9.9 %copy-start.29 = (f32[1,256]{1,0:T(1,128)}, f32[1,256]{1,0:T(1,128)S(1)}, u32[]{:S(2)}) copy-start(f32[1,256]{1,0:T(1,128)S(1)} %get-tuple-element.726) | copy-start | bytes 3076
  18.9 9.9 %copy-start.30 = (f32[1,256]{1,0:T(1,128)}, f32[1,256]{1,0:T(1,128)S(1)}, u32[]{:S(2)}) copy-start(f32[1,256]{1,0:T(1,128)S(1)} %get-tuple-element.727) | copy-start | bytes 3076
  18.9 9.9 %copy-start.31 = (f32[1,256]{1,0:T(1,128)}, f32[1,256]{1,0:T(1,128)S(1)}, u32[]{:S(2)}) copy-start(f32[1,256]{1,0:T(1,128)S(1)} %get-tuple-element.728) | copy-start | bytes 3076
  18.9 9.9 %copy-start.32 = (f32[1,256]{1,0:T(1,128)}, f32[1,256]{1,0:T(1,128)S(1)}, u32[]{:S(2)}) copy-start(f32[1,256]{1,0:T(1,128)S(1)} %get-tuple-element.729) | copy-start | bytes 3076
  18.9 9.9 %copy-start.33 = (f32[1,256]{1,0:T(1,128)}, f32[1,256]{1,0:T(1,128)S(1)}, u32[]{:S(2)}) copy-start(f32[1,256]{1,0:T(1,128)S(1)} %get-tuple-element.730) | copy-start | bytes 3076
  18.9 9.9 %copy-start.34 = (f32[1,256]{1,0:T(1,128)}, f32[1,256]{1,0:T(1,128)S(1)}, u32[]{:S(2)}) copy-start(f32[1,256]{1,0:T(1,128)S(1)} %get-tuple-element.731) | copy-start | bytes 3076
  18.9 9.9 %copy-start.37 = (f32[1,256]{1,0:T(1,128)}, f32[1,256]{1,0:T(1,128)S(1)}, u32[]{:S(2)}) copy-start(f32[1,256]{1,0:T(1,128)S(1)} %get-tuple-element.732) | copy-start | bytes 3076
  19.0 9.9 %copy-start.38 = (f32[1,256]{1,0:T(1,128)}, f32[1,256]{1,0:T(1,128)S(1)}, u32[]{:S(2)}) copy-start(f32[1,256]{1,0:T(1,128)S(1)} %get-tuple-element.724) | copy-start | bytes 3076
  28.9 2.7 copy-start.3
  91.5 2.1 copy-start.40
  91.5 2.1 copy-start.41
  91.5 2.1 copy-start.42
  91.5 2.1 copy-start.43
  91.5 2.1 copy-start.44
  91.5 2.1 copy-start.45
  91.5 2.1 copy-start.46
  91.5 2.1 copy-start.47
  91.5 2.1 copy-start.48
  91.6 2.1 copy-start.49
  91.6 2.1 copy-start.50
  91.6 2.1 copy-start.51
  91.6 2.1 copy-start.52
  91.6 2.1 copy-start.53
  91.6 2.1 copy-start.54
  91.6 2.1 copy-start.55
  91.6 2.1 copy-start.56
  91.6 2.1 copy-start.57
  91.6 2.1 copy-start.58
  91.7 2.1 copy-start.59
  93.6 40.4 %copy-start.80 = (pred[4]{0:T(512)(128)(4,1)S(1)}, pred[4]{0:T(512)(128)(4,1)}, u32[]{:S(2)}) copy-start(pred[4]{0:T(512)(128)(4,1)} %copy-done.79) | copy-start | bytes 16
  134.6 5.5 %copy-start.6 = (bf16[1,1,16,16,256]{4,3,2,1,0:T(8,128)(2,1)S(1)}, bf16[1,1,16,16,256]{4,3,2,1,0:T(8,128)(2,1)}, u32[]{:S(2)}) copy-start(bf16[1,1,16,16,256]{4,3,2,1,0:T(8,128)(2,1)} %param.106) | copy-start | bytes 393220
  134.6 5.5 %copy-start.85 = (f32[256,1024]{1,0:T(8,128)S(1)}, f32[256,1024]{1,0:T(8,128)}, u32[]{:S(2)}) copy-start(f32[256,1024]{1,0:T(8,128)} %get-tuple-element.748) | copy-start | bytes 3145732
  136.2 7.5 %collective-permute-start.2 = (bf16[1,4,24576]{2,1,0:T(4,128)(2,1)}, bf16[1,4,24576]{2,1,0:T(4,128)(2,1)S(1)}, u32[]{:S(2)}, u32[]{:S(2)}) collective-permute-start(bf16[1,4,24576]{2,1,0:T(4,128)(2,1)} %get-tuple-element.668), channel_id=1, source_target_pairs={{0,28},{4,0},{8,4},{12,8},{16,12},{20,16},{24,20},{28,24},{1,29},{... | collective-permute-start | bytes 589832 | tf_op jit(solution)/shard_map/ppermute | solution.py:14
  140.1 8.7 %collective-permute-start.3 = (bf16[1,4,24576]{2,1,0:T(4,128)(2,1)}, bf16[1,4,24576]{2,1,0:T(4,128)(2,1)}, u32[]{:S(2)}, u32[]{:S(2)}) collective-permute-start(bf16[1,4,24576]{2,1,0:T(4,128)(2,1)} %get-tuple-element.669), channel_id=1, source_target_pairs={{0,4},{4,8},{8,12},{12,16},{16,20},{20,24},{24,28},{28,0},{1,5},{5... | collective-permute-start | bytes 589832 | tf_op jit(solution)/shard_map/ppermute | solution.py:14
  277.2 2.4 copy-start.2
  (27 other events, 48.8 us)
Sparse Core Ops, SparseCore 0:
  141.8 135.3 all-reduce.9
where the time goes:
time: 289 us; the launch traced here: 288 us
  waiting for transfers between devices  132 us (46%)
  other arithmetic  47.7 us (17%)
  blocking collectives  39.4 us (14%)
  local copies, waits for them, and re-layouts  35.3 us (12%)
  between operations  16.1 us (6%)
  starting transfers between devices  10 us (3%)
  matrix products  7.09 us (2%)
    psum x1, waiting for transfers between devices, body(): summed = lax.psum((pending[0], pending[1], pending[2]), ('tile', 'ens'))  126 us
    psum x1, blocking collectives, body(): summed = lax.psum((pending[0], pending[1], pending[2]), ('tile', 'ens'))  39.4 us
    scatter-add x37, local copies, waits for them, and re-layouts, depthwise_back(): grad_padded_tile = grad_padded_tile.at[..., DILATION_STEP * first_operand...  21.4 us
    another operation x12, other arithmetic  17.2 us
    add x28, other arithmetic, depthwise_back(): grad_padded_tile = grad_padded_tile.at[..., DILATION_STEP * first_operand...  11.2 us
    ppermute x4, starting transfers between devices, from_behind(): lax.ppermute(x, axis, [(i, (i + by) % length) for i in range(length)])  10 us
  transfers between devices with their start and end apart: 5, of which 3 were waited for; matrix products, arithmetic and copies ran while one was open for 5% of the time, Pallas kernels for 0%

commit v1 on v0

v1 whole, which is shorter than its diff:
```python
import functools
import math

import jax
import jax.numpy as jnp
from jax import lax
from jax.experimental import pallas as pl
from jax.experimental.pallas import tpu as pltpu
from jax.sharding import PartitionSpec as P

C = 256
HID = 1024
TAPS = 7
STEP = 2
HALO = 6
N = 16
ROWS = N + 2 * HALO
LANES = 128
FRAME = 32
LEFT = 8
GROUP = 4
EXTRA = 16
F32 = jnp.float32
BF16 = jnp.bfloat16
GELU_A = math.sqrt(2.0 / math.pi)
GELU_B = 0.044715
VMEM = pl.BlockSpec(memory_space=pltpu.VMEM)
SMEM = pl.BlockSpec(memory_space=pltpu.SMEM)


def dot(a, b, ca, cb):
    return lax.dot_general(a, b, (((ca,), (cb,)), ((), ())), preferred_element_type=F32)


def tap_offset(b):
    return LEFT - HALO + STEP * b


def side_onehots(meta):
    parts = []
    for s in range(4):
        n = HALO * N if s < 2 else 8 * N
        rho = lax.broadcasted_iota(jnp.int32, (n, 1), 0)
        if s < 2:
            m = rho & (N - 1)
            k = rho >> 4
            if s == 0:
                k = HALO - 1 - k
            ok = None
        else:
            m = rho >> 3
            q = rho & 7
            k = LEFT - 1 - q if s == 2 else q
            ok = k < HALO
        target = meta[3 * s] + meta[3 * s + 1] * k + meta[3 * s + 2] * m
        if ok is not None:
            target = jnp.where(ok, target, -1)
        lane = lax.broadcasted_iota(jnp.int32, (n, 3 * N * N), 1)
        parts.append(jnp.where(target == lane, 1.0, 0.0).astype(BF16))
    return parts


def fill_frame(meta, own_ref, one_ref, two_ref, frame):
    own = own_ref[...]
    zero_cols = jnp.zeros((HALO, LEFT, LANES), F32)
    onehots = side_onehots(meta)
    rims = [
        dot(s[:, : N * N], own, 1, 0)
        + dot(s[:, N * N : 2 * N * N], one_ref[...], 1, 0)
        + dot(s[:, 2 * N * N :], two_ref[...], 1, 0)
        for s in onehots
    ]
    inner = own.astype(F32).reshape(N, N, C)
    for l in range(C // LANES):
        lanes = slice(l * LANES, (l + 1) * LANES)
        for top in (0, HALO + N):
            for left in (0, LEFT + N):
                frame[l, top : top + HALO, left : left + LEFT, :] = zero_cols
        frame[l, :HALO, LEFT : LEFT + N, :] = rims[0][:, lanes].reshape(HALO, N, LANES)
        frame[l, HALO + N :, LEFT : LEFT + N, :] = rims[1][:, lanes].reshape(HALO, N, LANES)
        frame[l, HALO : HALO + N, :LEFT, :] = rims[2][:, lanes].reshape(N, 8, LANES)
        frame[l, HALO : HALO + N, LEFT + N :, :] = rims[3][:, lanes].reshape(N, 8, LANES)
        frame[l, HALO : HALO + N, LEFT : LEFT + N, :] = inner[:, :, lanes]


def forward_kernel(
    meta, core, own_ref, one_ref, two_ref, cot_ref, taps_ref, win_ref, wout_ref,
    send_ref, keep_ref, dconv_ref, frame, conv,
):
    fill_frame(meta, own_ref, one_ref, two_ref, frame)
    for l in range(C // LANES):
        lanes = slice(l * LANES, (l + 1) * LANES)
        acc = [None] * N
        for b in range(TAPS):
            off = tap_offset(b)
            coef = [taps_ref[a * TAPS + b : a * TAPS + b + 1, lanes] for a in range(TAPS)]
            for r in range(ROWS):
                x = frame[l, r, off : off + N, :]
                for a in range(TAPS):
                    i = r - STEP * a
                    if 0 <= i < N:
                        term = x * coef[a]
                        acc[i] = term if acc[i] is None else acc[i] + term
        for i in range(N):
            conv[i * N : (i + 1) * N, lanes] = acc[i]
    value = conv[...]
    centred = value - jnp.mean(value, -1, keepdims=True)
    inv_std = lax.rsqrt(jnp.mean(centred * centred, -1, keepdims=True) + 1e-06)
    normed_f = centred * inv_std
    normed = normed_f.astype(BF16)
    cot = cot_ref[...]
    first = core[0] == 0
    d_normed = None
    for h in range(GROUP):
        cols = slice(h * C, (h + 1) * C)
        w_in = win_ref[:, cols]
        pre = dot(normed, w_in, 1, 0)
        d_hidden = dot(cot, wout_ref[cols, :], 1, 1)
        square = pre * pre
        t = jnp.tanh(pre * (GELU_A + (GELU_A * GELU_B) * square))
        half = 0.5 + 0.5 * t
        hidden = (pre * half).astype(BF16)
        slope = half + (0.5 * pre) * (1.0 - t * t) * (GELU_A + (3.0 * GELU_A * GELU_B) * square)
        d_pre = (d_hidden * slope).astype(BF16)
        part_out = dot(hidden, cot, 0, 0).astype(BF16)
        part_in = dot(normed, d_pre, 0, 0).astype(BF16)
        send_ref[h] = jnp.where(first, part_out, part_in)
        keep_ref[h] = jnp.where(first, part_in, part_out)
        back = dot(d_pre, w_in, 1, 1)
        d_normed = back if d_normed is None else d_normed + back
    dconv_ref[...] = inv_std * (
        d_normed
        - jnp.mean(d_normed, -1, keepdims=True)
        - normed_f * jnp.mean(d_normed * normed_f, -1, keepdims=True)
    )


def taps_kernel(meta, own_ref, one_ref, two_ref, dconv_ref, out_ref, frame):
    fill_frame(meta, own_ref, one_ref, two_ref, frame)
    out_ref[...] = jnp.zeros(out_ref.shape, F32)
    for l in range(C // LANES):
        lanes = slice(l * LANES, (l + 1) * LANES)
        grad = [dconv_ref[i * N : (i + 1) * N, lanes] for i in range(N)]
        for b in range(TAPS):
            off = tap_offset(b)
            acc = [None] * TAPS
            for r in range(ROWS):
                x = frame[l, r, off : off + N, :]
                for a in range(TAPS):
                    i = r - STEP * a
                    if 0 <= i < N:
                        term = x * grad[i]
                        acc[a] = term if acc[a] is None else acc[a] + term
            for a in range(TAPS):
                t = a * TAPS + b
                out_ref[t // EXTRA, t % EXTRA : t % EXTRA + 1, lanes] = jnp.sum(
                    acc[a], 0, keepdims=True
                )


def backward_kernel(meta, dconv_ref, taps_ref, cot_ref, own_ref, one_ref, two_ref, shifted, rim):
    residues = (2, 4, 6, 0)
    pad = jnp.zeros((ROWS, 8, LANES), F32)
    for l in range(C // LANES):
        lanes = slice(l * LANES, (l + 1) * LANES)
        grad = [
            [dconv_ref[i * N + 8 * t : i * N + 8 * t + 8, lanes] for t in range(2)]
            for i in range(N)
        ]
        for n, s in enumerate(residues):
            shifted[l, n, :, 0:8, :] = pad
            shifted[l, n, :, 32:40, :] = pad
            pieces = [(b, tap_offset(b) // 8) for b in range(TAPS) if tap_offset(b) % 8 == s]
            coef = {
                (a, b): taps_ref[a * TAPS + b : a * TAPS + b + 1, lanes]
                for a in range(TAPS)
                for b, _ in pieces
            }
            for r in range(ROWS):
                acc = [None] * 3
                for a in range(TAPS):
                    i = r - STEP * a
                    if 0 <= i < N:
                        for b, up in pieces:
                            for t in range(2):
                                term = grad[i][t] * coef[a, b]
                                acc[t + up] = term if acc[t + up] is None else acc[t + up] + term
                for t in range(3):
                    shifted[l, n, r, 8 + 8 * t : 16 + 8 * t, :] = (
                        jnp.zeros((8, LANES), F32) if acc[t] is None else acc[t]
                    )

        def gather(rows, first_col, count):
            total = None
            for n, s in enumerate(residues):
                at = 8 + first_col - s
                piece = shifted[l, n, rows, at : at + count, :]
                total = piece if total is None else total + piece
            return total

        top = gather(slice(0, HALO), LEFT, N)
        bottom = gather(slice(HALO + N, ROWS), LEFT, N)
        middle = slice(HALO, HALO + N)
        left = gather(middle, 0, 8)
        right = gather(middle, LEFT + N, 8)
        inner = gather(middle, LEFT, N)
        at = 0
        for block in (top, bottom, left, right):
            n = block.shape[0] * block.shape[1]
            rim[at : at + n, lanes] = block.reshape(n, LANES).astype(BF16)
            at += n
        own_ref[:, lanes] = inner.reshape(N * N, LANES) + cot_ref[:, lanes].astype(F32)
    onehot = jnp.concatenate(side_onehots(meta), 0)
    cells = rim[...]
    own_ref[...] += dot(onehot[:, : N * N], cells, 0, 0)
    one_ref[...] = dot(onehot[:, N * N : 2 * N * N], cells, 0, 0).astype(BF16)
    two_ref[...] = dot(onehot[:, 2 * N * N :], cells, 0, 0).astype(BF16)


def spread_kernel(place, keep_ref, got_ref, taps_ref, own_ref, one_ref, two_ref, three_ref):
    for d, out in enumerate((own_ref, one_ref, two_ref, three_ref)):
        j = place[0] ^ d
        out[:C, :] = (keep_ref[j].astype(F32) + got_ref[j].astype(F32)).astype(out.dtype)
        out[C:, :] = taps_ref[j].astype(out.dtype)


def finish_kernel(scale, place, core, *refs):
    mine, theirs = refs[:GROUP], refs[GROUP : 2 * GROUP]
    kernel_ref, in_ref, out_ref, rows = refs[2 * GROUP :]
    first = core[0] == 0
    for d in range(GROUP):
        j = place[0] ^ d
        at = pl.multiple_of(j * C, C)
        a = mine[d][:C, :]
        b = theirs[d][:C, :]
        in_ref[:, pl.ds(at, C)] = jnp.where(first, a, b).astype(F32) * scale
        out_ref[pl.ds(at, C), :] = jnp.where(first, b, a).astype(F32) * scale
        rows[j] = (mine[d][C:, :].astype(F32) + theirs[d][C:, :].astype(F32)) * scale
    for j in range(GROUP):
        n = min(EXTRA, TAPS * TAPS - j * EXTRA)
        kernel_ref[j * EXTRA : j * EXTRA + n, :] = rows[j, :n, :]


def call(kernel, outs, scratch=(), specs=(), flops=0, nbytes=0, vmem=48):
    return pl.pallas_call(
        kernel,
        out_shape=outs,
        in_specs=specs,
        out_specs=jax.tree.map(lambda _: VMEM, outs),
        scratch_shapes=scratch,
        compiler_params=pltpu.CompilerParams(vmem_limit_bytes=vmem * 1024 * 1024),
        cost_estimate=pl.CostEstimate(flops=flops, bytes_accessed=nbytes, transcendentals=0),
    )


def body(features, cotangent, kernel, weight_in, weight_out, tile_neighbour, edge_code):
    owners = lax.axis_size("tile")
    members = lax.axis_size("ens")
    position = lax.axis_index("tile")
    member = lax.axis_index("ens")
    devices = owners * members
    scale = 1.0 / math.sqrt(devices * N * N)
    both = ("tile", "ens")
    struct = jax.ShapeDtypeStruct

    def swap(x, bits):
        return lax.ppermute(x, both, [(i, i ^ bits) for i in range(devices)])

    def one_over(x):
        return lax.ppermute(x, "tile", [(i, i ^ 1) for i in range(owners)])

    def two_over(x):
        moves = [(i, (i + 1 if i % 2 else i - 1) % owners) for i in range(owners)]
        return lax.ppermute(x, "tile", moves)

    offset = (tile_neighbour[0] - position + 1) % owners
    odd = position % 2
    source = jnp.where(offset == 1, 0, jnp.where((offset == 0) == (odd == 1), 1, 2))
    edge = edge_code[0] % 4
    flipped = edge_code[0] // 4 % 2
    along = jnp.where(edge < 2, 1, N)
    across = jnp.where(edge < 2, N, 1)
    base = source * (N * N) + flipped * (N - 1) * along + (edge % 2) * (N - 1) * across
    step_k = across * (1 - 2 * (edge % 2))
    step_m = along * (1 - 2 * flipped)
    meta = jnp.stack([base, step_k, step_m], -1).reshape(-1).astype(jnp.int32)
    core = (member % 2).reshape(1).astype(jnp.int32)
    place = ((member // 2) % 2 + 2 * (position % 2)).reshape(1).astype(jnp.int32)

    own = features.reshape(N * N, C)
    cot = cotangent.reshape(N * N, C)
    two = two_over(own)
    one = one_over(own)

    frame = pltpu.VMEM((2, ROWS, FRAME, LANES), F32)
    send, keep, dconv = call(
        forward_kernel,
        (struct((GROUP, C, C), BF16), struct((GROUP, C, C), BF16), struct((N * N, C), F32)),
        [frame, pltpu.VMEM((N * N, C), F32)],
        [SMEM] * 2 + [VMEM] * 7,
        flops=700_000_000,
        nbytes=4_000_000,
    )(meta, core, own, one, two, cot, kernel, weight_in, weight_out)
    got = swap(send, 1)
    part_taps = call(
        taps_kernel,
        struct((GROUP, EXTRA, C), F32),
        [frame],
        [SMEM] + [VMEM] * 4,
        nbytes=6_000_000,
    )(meta, own, one, two, dconv)

    block = struct((C + EXTRA, C), BF16)
    pieces = call(
        spread_kernel, (block,) * GROUP, (), [SMEM] + [VMEM] * 3, nbytes=3_000_000
    )(place, keep, got, part_taps)
    square = [2, members, 2 + members]
    total = pieces[0].astype(F32)
    for piece, bits in zip(pieces[1:], square):
        total = total + swap(piece, bits).astype(F32)
    total = total.astype(BF16)

    grad_own, grad_one, grad_two = call(
        backward_kernel,
        (struct((N * N, C), F32), struct((N * N, C), BF16), struct((N * N, C), BF16)),
        [pltpu.VMEM((2, 4, ROWS, 40, LANES), F32), pltpu.VMEM((28 * N, C), BF16)],
        [SMEM] + [VMEM] * 3,
        nbytes=10_000_000,
    )(meta, dconv, kernel, cot)

    rest = [1 << n for n in range(2, members.bit_length() - 1)]
    rest += [members << n for n in range(1, owners.bit_length() - 1)]
    while rest:
        bits, rest = rest[:2], rest[2:]
        if len(bits) == 2:
            a, b = bits
            far, near, mid = swap(total, a + b), swap(total, a), swap(total, b)
            total = (total.astype(F32) + near.astype(F32)) + (mid.astype(F32) + far.astype(F32))
        else:
            total = total.astype(F32) + swap(total, bits[0]).astype(F32)
        total = total.astype(BF16)

    back_two = two_over(grad_two)
    back_one = one_over(grad_one)
    grad_features = (grad_own + back_one.astype(F32) + back_two.astype(F32)).astype(BF16)

    mine = [total] + [swap(total, bits) for bits in square]
    theirs = [swap(x, 1) for x in mine]
    grad_kernel, grad_in, grad_out = call(
        functools.partial(finish_kernel, scale),
        (struct((TAPS * TAPS, C), F32), struct((C, HID), F32), struct((HID, C), F32)),
        [pltpu.VMEM((GROUP, EXTRA, C), F32)],
        [SMEM] * 2 + [VMEM] * 8,
        nbytes=4_000_000,
    )(place, core, *mine, *theirs)
    return grad_features.reshape(features.shape), grad_kernel, grad_in, grad_out


def solution(mesh):
    halved = P("ens", "tile", None, None, None)
    in_specs = (halved, halved, P(), P(), P(), P("tile", None), P("tile", None))
    out_specs = (halved, P(), P(), P())
    return jax.shard_map(body, mesh=mesh, in_specs=in_specs, out_specs=out_specs, check_vma=False)
```

time: 289 us -> 65.5 us (0.23)
  waiting for transfers between devices: 132 us -> 26.8 us
  other arithmetic: 47.7 us -> 1.59 us
  blocking collectives: 39.4 us -> 0 us
  local copies, waits for them, and re-layouts: 35.3 us -> 4.08 us
  between operations: 16.1 us -> 0.76 us
  starting transfers between devices: 10 us -> 22.7 us
  Pallas kernels: 0 us -> 9.39 us
  matrix products: 7.09 us -> 0 us
    psum x1 -> x0, waiting for transfers between devices: 126 us -> none  [body(): summed = lax.psum((pending[0], pending[1], pending[2]), ('tile', 'ens'))]
    psum x1 -> x0, blocking collectives: 39.4 us -> none  [body(): summed = lax.psum((pending[0], pending[1], pending[2]), ('tile', 'ens'))]
    scatter-add x37 -> x0, local copies, waits for them, and re-layouts: 21.4 us -> none  [depthwise_back(): grad_padded_tile = grad_padded_tile.at[..., DILATION_STEP * first_operand...]
    ppermute x4 -> x18, waiting for transfers between devices: 5.67 us -> 26.8 us  [the longest x14 15.8 us: swap(): return lax.ppermute(x, both, [(i, i ^ bits) for i in range(devices)])]
    another operation x13 -> x1, other arithmetic: 17.3 us -> 0.01 us  [body(): meta = jnp.stack([base, step_k, step_m], -1).reshape(-1).astype(jnp.int32)]
    ppermute x4 -> x18, starting transfers between devices: 10 us -> 22.7 us  [the longest x14 12.7 us: swap(): return lax.ppermute(x, both, [(i, i ^ bits) for i in range(devices)])]
    add x29 -> x1, other arithmetic: 12.3 us -> 0.69 us  [body(): source * (N * N) + flipped * (N - 1) * along + edge % 2 * (N - 1) * across]
    pallas_call x0 -> x5, Pallas kernels: none -> 9.39 us  [the longest x1 3.92 us: body(): call(forward_kernel, (struct((GROUP, C, C), BF16), struct((GROUP, C, C),...]
  transfers between devices with their start and end apart: 5 -> 18, of which waited for: 3 -> 10; matrix products, arithmetic and copies ran while one was open for 5% -> 2% of each run, Pallas kernels for 0% -> 6%
where the time goes in v1:
time: 65.5 us; the launch traced here: 65.3 us
  waiting for transfers between devices  26.8 us (41%)
  starting transfers between devices  22.7 us (35%)
  Pallas kernels  9.39 us (14%)
  local copies, waits for them, and re-layouts  4.08 us (6%)
  other arithmetic  1.59 us (2%)
  between operations  0.76 us (1%)
    ppermute x14, waiting for transfers between devices, swap(): return lax.ppermute(x, both, [(i, i ^ bits) for i in range(devices)])  15.8 us
    ppermute x14, starting transfers between devices, swap(): return lax.ppermute(x, both, [(i, i ^ bits) for i in range(devices)])  12.7 us
    ppermute x2, starting transfers between devices, two_over(): return lax.ppermute(x, 'tile', moves)  8.48 us
    ppermute x2, waiting for transfers between devices, one_over(): return lax.ppermute(x, 'tile', [(i, i ^ 1) for i in range(owners)])  8.06 us
    pallas_call x1, Pallas kernels, body(): call(forward_kernel, (struct((GROUP, C, C), BF16), struct((GROUP, C, C),...  3.92 us
    unnamed x14, local copies, waits for them, and re-layouts  3.9 us
    ppermute x2, waiting for transfers between devices, two_over(): return lax.ppermute(x, 'tile', moves)  2.89 us
    pallas_call x1, Pallas kernels, body(): call(backward_kernel, (struct((N * N, C), F32), struct((N * N, C), BF16),...  2.09 us
  transfers between devices with their start and end apart: 18, of which 10 were waited for; matrix products, arithmetic and copies ran while one was open for 2% of the time, Pallas kernels for 6%

profile of v1, /device:TPU:0, one launch (start us, length us, event | category | flops | bytes accessed | tf_op | source)
XLA Modules:
  0.0 65.3 jit_solution(2258304148829486866)
XLA Ops:
  0.6 0.0 copy-start.4
  0.6 6.0 %collective-permute-start.1 = (bf16[256,256]{1,0:T(8,128)(2,1)}, bf16[256,256]{1,0:T(8,128)(2,1)S(1)}, u32[]{:S(2)}, u32[]{:S(2)}) collective-permute-start(bf16[256,256]{1,0:T(8,128)(2,1)} %bitcast.28), channel_id=1, source_target_pairs={{0,28},{4,8},{8,4},{12,16},{16,12},{20,24},{24,20},{28,0},{1,29},{... | collective-permute-start | bytes 393224 | tf_op jit(solution)/shard_map/ppermute | solution.py:274
  6.7 0.0 collective-permute-start
  6.7 0.7 %multiply_add_fusion = (s32[4,1]{0,1:T(1,128)S(1)}, s32[4,1]{0,1:T(1,128)S(1)}, s32[4,1]{0,1:T(1,128)S(1)}) fusion(pred[]{:T(512)S(6)} %eq.49, s32[1,4]{1,0:T(1,128)} %param.12, s32[]{:T(128)S(6)} %axis_index.23, s32[1,4]{1,0:T(1,128)} %param.13), kind=kLoop, calls=%fused_computation.28 | loop fusion | flops 276 | bytes 85 | tf_op jit(solution)/shard_map/add | solution.py:283
  7.4 0.1 copy.11
  7.5 0.1 reshape.326.meta
  7.6 2.9 %collective-permute-done.1.two_ref = bf16[256,256]{1,0:T(8,128)(2,1)S(1)} collective-permute-done((bf16[256,256]{1,0:T(8,128)(2,1)}, bf16[256,256]{1,0:T(8,128)(2,1)S(1)}, u32[]{:S(2)}, u32[]{:S(2)}) %collective-permute-start.1) | collective-permute-done | bytes 131104 | tf_op jit(solution)/shard_map/ppermute | solution.py:274
  10.5 2.7 %collective-permute-done.one_ref = bf16[256,256]{1,0:T(8,128)(2,1)S(1)} collective-permute-done((bf16[256,256]{1,0:T(8,128)(2,1)}, bf16[256,256]{1,0:T(8,128)(2,1)S(1)}, u32[]{:S(2)}, u32[]{:S(2)}) %collective-permute-start) | collective-permute-done | bytes 131104 | tf_op jit(solution)/shard_map/ppermute | solution.py:270
  13.2 0.0 copy-done.4
  13.2 0.0 copy-start
  13.2 0.9 %copy-done = bf16[1,1,16,16,256]{4,3,2,1,0:T(8,128)(2,1)S(1)} copy-done((bf16[1,1,16,16,256]{4,3,2,1,0:T(8,128)(2,1)S(1)}, bf16[1,1,16,16,256]{4,3,2,1,0:T(8,128)(2,1)}, u32[]{:S(2)}) %copy-start) | copy-done | bytes 131096
  14.1 0.0 copy-start.2
  14.1 0.9 %copy-done.2 = bf16[1,1,16,16,256]{4,3,2,1,0:T(8,128)(2,1)S(1)} copy-done((bf16[1,1,16,16,256]{4,3,2,1,0:T(8,128)(2,1)S(1)}, bf16[1,1,16,16,256]{4,3,2,1,0:T(8,128)(2,1)}, u32[]{:S(2)}) %copy-start.2) | copy-done | bytes 131096
  15.0 0.0 copy-start.5
  15.0 1.0 %copy-done.5 = bf16[256,1024]{1,0:T(8,128)(2,1)S(1)} copy-done((bf16[256,1024]{1,0:T(8,128)(2,1)S(1)}, bf16[256,1024]{1,0:T(8,128)(2,1)}, u32[]{:S(2)}) %copy-start.5) | copy-done | bytes 524312
  16.1 0.0 copy-start.6
  16.1 1.0 %copy-done.6 = bf16[1024,256]{1,0:T(8,128)(2,1)S(1)} copy-done((bf16[1024,256]{1,0:T(8,128)(2,1)S(1)}, bf16[1024,256]{1,0:T(8,128)(2,1)}, u32[]{:S(2)}) %copy-start.6) | copy-done | bytes 524312
  17.1 0.0 copy-start.1
  17.1 3.9 %shard_map.102 = (bf16[4,256,256]{2,1,0:T(8,128)(2,1)S(1)}, bf16[4,256,256]{2,1,0:T(8,128)(2,1)S(1)}, f32[256,256]{1,0:T(8,128)S(1)}) custom-call(s32[12]{0:T(128)S(1)} %reshape.326.meta, s32[1]{0:T(128)} %bitcast.2.core, bf16[256,256]{1,0:T(8,128)(2,1)S(1)} %bitcast.30, bf16[256,256]{1,0:T(8,128)(2,1)S(1)} %collective-permute-done.one_ref, ...), custom_call_target="tpu_custom_call" | custom-call | flops 700000000 | bytes 4000000 | tf_op jit(solution)/shard_map/pallas_call | solution.py:296
  21.0 0.1 collective-permute-start.4
  21.1 0.0 copy-done.1
  21.1 1.8 %shard_map.104.taps_ref = f32[4,16,256]{2,1,0:T(8,128)S(1)} custom-call(s32[12]{0:T(128)S(1)} %reshape.326.meta, bf16[256,256]{1,0:T(8,128)(2,1)S(1)} %bitcast.31, bf16[256,256]{1,0:T(8,128)(2,1)S(1)} %collective-permute-done.one_ref, bf16[256,256]{1,0:T(8,128)(2,1)S(1)} %collective-permute-done.1.two_ref, f32[256,256]{1,0:T(8,128)S(1)} %get-tuple-element.17.dconv_ref), custom_call_target="tpu_custom_call" | custom-call | bytes 6000000 | tf_op jit(solution)/shard_map/pallas_call | solution.py:305
  23.0 0.0 collective-permute-done.4.got_ref
  23.0 0.1 shard_map.105
  23.1 1.6 %collective-permute-start.5 = (bf16[272,256]{1,0:T(8,128)(2,1)S(1)}, bf16[272,256]{1,0:T(8,128)(2,1)S(1)}, u32[]{:S(2)}, u32[]{:S(2)}) collective-permute-start(bf16[272,256]{1,0:T(8,128)(2,1)S(1)} %get-tuple-element.24), channel_id=1, source_target_pairs={{0,2},{1,3},{2,0},{3,1},{4,6},{5,7},{6,4},{7,5},{8,10},{9,11},{10,... | collective-permute-start | bytes 417800 | tf_op jit(solution)/shard_map/ppermute | solution.py:267
  24.7 0.0 collective-permute-start.6
  24.7 2.0 %collective-permute-start.7 = (bf16[272,256]{1,0:T(8,128)(2,1)S(1)}, bf16[272,256]{1,0:T(8,128)(2,1)S(1)}, u32[]{:S(2)}, u32[]{:S(2)}) collective-permute-start(bf16[272,256]{1,0:T(8,128)(2,1)S(1)} %get-tuple-element.26), channel_id=1, source_target_pairs={{0,6},{1,7},{2,4},{3,5},{4,2},{5,3},{6,0},{7,1},{8,14},{9,15},{10,... | collective-permute-start | bytes 417800 | tf_op jit(solution)/shard_map/ppermute | solution.py:267
  26.7 2.5 %collective-permute-done.5 = bf16[272,256]{1,0:T(8,128)(2,1)S(1)} collective-permute-done((bf16[272,256]{1,0:T(8,128)(2,1)S(1)}, bf16[272,256]{1,0:T(8,128)(2,1)S(1)}, u32[]{:S(2)}, u32[]{:S(2)}) %collective-permute-start.5) | collective-permute-done | bytes 139296 | tf_op jit(solution)/shard_map/ppermute | solution.py:267
  29.2 2.0 %collective-permute-done.6 = bf16[272,256]{1,0:T(8,128)(2,1)S(1)} collective-permute-done((bf16[272,256]{1,0:T(8,128)(2,1)S(1)}, bf16[272,256]{1,0:T(8,128)(2,1)S(1)}, u32[]{:S(2)}, u32[]{:S(2)}) %collective-permute-start.6) | collective-permute-done | bytes 139296 | tf_op jit(solution)/shard_map/ppermute | solution.py:267
  31.2 2.1 %collective-permute-done.7 = bf16[272,256]{1,0:T(8,128)(2,1)S(1)} collective-permute-done((bf16[272,256]{1,0:T(8,128)(2,1)S(1)}, bf16[272,256]{1,0:T(8,128)(2,1)S(1)}, u32[]{:S(2)}, u32[]{:S(2)}) %collective-permute-start.7) | collective-permute-done | bytes 139296 | tf_op jit(solution)/shard_map/ppermute | solution.py:267
  33.4 0.1 add_convert_fusion.1
  33.5 0.0 copy-start.3
  33.5 1.8 %collective-permute-start.10 = (bf16[272,256]{1,0:T(8,128)(2,1)S(1)}, bf16[272,256]{1,0:T(8,128)(2,1)S(1)}, u32[]{:S(2)}, u32[]{:S(2)}) collective-permute-start(bf16[272,256]{1,0:T(8,128)(2,1)S(1)} %add_convert_fusion.1), channel_id=1, source_target_pairs={{0,24},{1,25},{2,26},{3,27},{4,28},{5,29},{6,30},{7,31},{8,16},{9,... | collective-permute-start | bytes 417800 | tf_op jit(solution)/shard_map/ppermute | solution.py:267
  35.2 0.0 collective-permute-start.9
  35.2 2.7 %collective-permute-start.8 = (bf16[272,256]{1,0:T(8,128)(2,1)S(1)}, bf16[272,256]{1,0:T(8,128)(2,1)S(1)}, u32[]{:S(2)}, u32[]{:S(2)}) collective-permute-start(bf16[272,256]{1,0:T(8,128)(2,1)S(1)} %add_convert_fusion.1), channel_id=1, source_target_pairs={{0,8},{1,9},{2,10},{3,11},{4,12},{5,13},{6,14},{7,15},{8,0},{9,1},... | collective-permute-start | bytes 417800 | tf_op jit(solution)/shard_map/ppermute | solution.py:267
  37.9 4.0 %collective-permute-done.10 = bf16[272,256]{1,0:T(8,128)(2,1)S(1)} collective-permute-done((bf16[272,256]{1,0:T(8,128)(2,1)S(1)}, bf16[272,256]{1,0:T(8,128)(2,1)S(1)}, u32[]{:S(2)}, u32[]{:S(2)}) %collective-permute-start.10) | collective-permute-done | bytes 139296 | tf_op jit(solution)/shard_map/ppermute | solution.py:267
  41.9 4.7 %collective-permute-done.9 = bf16[272,256]{1,0:T(8,128)(2,1)S(1)} collective-permute-done((bf16[272,256]{1,0:T(8,128)(2,1)S(1)}, bf16[272,256]{1,0:T(8,128)(2,1)S(1)}, u32[]{:S(2)}, u32[]{:S(2)}) %collective-permute-start.9) | collective-permute-done | bytes 139296 | tf_op jit(solution)/shard_map/ppermute | solution.py:267
  46.7 0.0 collective-permute-done.8
  46.7 0.1 add_convert_fusion.refs_0_
  46.8 2.5 %collective-permute-start.13 = (bf16[272,256]{1,0:T(8,128)(2,1)S(1)}, bf16[272,256]{1,0:T(8,128)(2,1)S(1)}, u32[]{:S(2)}, u32[]{:S(2)}) collective-permute-start(bf16[272,256]{1,0:T(8,128)(2,1)S(1)} %add_convert_fusion.refs_0_), channel_id=1, source_target_pairs={{0,6},{1,7},{2,4},{3,5},{4,2},{5,3},{6,0},{7,1},{8,14},{9,15},{10,... | collective-permute-start | bytes 417800 | tf_op jit(solution)/shard_map/ppermute | solution.py:267
  49.3 0.5 collective-permute-start.12
  49.8 0.5 collective-permute-start.11
  50.3 0.0 copy-done.3
  50.3 2.1 %shard_map.103 = (f32[256,256]{1,0:T(8,128)S(1)}, bf16[256,256]{1,0:T(8,128)(2,1)S(1)}, bf16[256,256]{1,0:T(8,128)(2,1)S(1)}) custom-call(s32[12]{0:T(128)S(1)} %reshape.326.meta, f32[256,256]{1,0:T(8,128)S(1)} %get-tuple-element.17.dconv_ref, f32[49,256]{1,0:T(8,128)S(1)} %copy-done.4, bf16[256,256]{1,0:T(8,128)(2,1)S(1)} %bitcast.33), custom_call_target="tpu_custom_call" | custom-call | bytes 10000000 | tf_op jit(solution)/shard_map/pallas_call | solution.py:323
  52.4 1.6 %collective-permute-start.2 = (bf16[256,256]{1,0:T(8,128)(2,1)S(1)}, bf16[256,256]{1,0:T(8,128)(2,1)S(1)}, u32[]{:S(2)}, u32[]{:S(2)}) collective-permute-start(bf16[256,256]{1,0:T(8,128)(2,1)S(1)} %get-tuple-element.19), channel_id=1, source_target_pairs={{0,4},{4,0},{8,12},{12,8},{16,20},{20,16},{24,28},{28,24},{1,5},{5... | collective-permute-start | bytes 393224 | tf_op jit(solution)/shard_map/ppermute | solution.py:270
  54.0 2.4 %collective-permute-start.3 = (bf16[256,256]{1,0:T(8,128)(2,1)S(1)}, bf16[256,256]{1,0:T(8,128)(2,1)S(1)}, u32[]{:S(2)}, u32[]{:S(2)}) collective-permute-start(bf16[256,256]{1,0:T(8,128)(2,1)S(1)} %get-tuple-element.20), channel_id=1, source_target_pairs={{0,28},{4,8},{8,4},{12,16},{16,12},{20,24},{24,20},{28,0},{1,29},{... | collective-permute-start | bytes 393224 | tf_op jit(solution)/shard_map/ppermute | solution.py:274
  56.4 5.4 %collective-permute-done.2 = bf16[256,256]{1,0:T(8,128)(2,1)S(1)} collective-permute-done((bf16[256,256]{1,0:T(8,128)(2,1)S(1)}, bf16[256,256]{1,0:T(8,128)(2,1)S(1)}, u32[]{:S(2)}, u32[]{:S(2)}) %collective-permute-start.2) | collective-permute-done | bytes 131104 | tf_op jit(solution)/shard_map/ppermute | solution.py:270
  61.8 0.0 collective-permute-start.14
  61.8 0.0 collective-permute-done.13.refs_3_
  61.8 0.5 collective-permute-start.17
  62.3 0.0 collective-permute-done.12.refs_2_
  62.3 0.1 collective-permute-start.16
  62.4 0.0 collective-permute-done.11.refs_1_
  62.4 0.4 collective-permute-start.15
  62.8 0.0 collective-permute-done.3
  62.8 0.7 %add_convert_fusion.2 = bf16[256,256]{1,0:T(8,128)(2,1)} fusion(bf16[256,256]{1,0:T(8,128)(2,1)S(1)} %collective-permute-done.3, f32[256,256]{1,0:T(8,128)S(1)} %get-tuple-element.18, bf16[256,256]{1,0:T(8,128)(2,1)S(1)} %collective-permute-done.2), kind=kLoop, calls=%fused_computation.2 | loop fusion | flops 327680 | bytes 655360 | tf_op jit(solution)/shard_map/convert_element_type | solution.py:345
  63.5 0.0 collective-permute-done.14.refs_4_
  63.5 0.0 collective-permute-done.17.refs_7_
  63.5 0.1 collective-permute-done.16.refs_6_
  63.6 0.2 collective-permute-done.15.refs_5_
  63.8 1.4 %shard_map.106 = (f32[49,256]{1,0:T(8,128)}, f32[256,1024]{1,0:T(8,128)}, f32[1024,256]{1,0:T(8,128)}) custom-call(s32[1]{0:T(128)} %bitcast.6.place, s32[1]{0:T(128)} %bitcast.2.core, bf16[272,256]{1,0:T(8,128)(2,1)S(1)} %add_convert_fusion.refs_0_, bf16[272,256]{1,0:T(8,128)(2,1)S(1)} %collective-permute-done.11.refs_1_, ...), custom_call_target="tpu_custom_call" | custom-call | bytes 4000000 | tf_op jit(solution)/shard_map/pallas_call | solution.py:349
  (2 shorter events, 0.0 us)
Async XLA Ops:
  0.6 12.6 %copy-start.4 = (f32[49,256]{1,0:T(8,128)S(1)}, f32[49,256]{1,0:T(8,128)}, u32[]{:S(2)}) copy-start(f32[49,256]{1,0:T(8,128)} %taps_ref.3) | copy-start | bytes 150532
  0.6 9.9 %collective-permute-start.1 = (bf16[256,256]{1,0:T(8,128)(2,1)}, bf16[256,256]{1,0:T(8,128)(2,1)S(1)}, u32[]{:S(2)}, u32[]{:S(2)}) collective-permute-start(bf16[256,256]{1,0:T(8,128)(2,1)} %bitcast.28), channel_id=1, source_target_pairs={{0,28},{4,8},{8,4},{12,16},{16,12},{20,24},{24,20},{28,0},{1,29},{... | collective-permute-start | bytes 393224 | tf_op jit(solution)/shard_map/ppermute | solution.py:274
  6.7 6.5 %collective-permute-start = (bf16[256,256]{1,0:T(8,128)(2,1)}, bf16[256,256]{1,0:T(8,128)(2,1)S(1)}, u32[]{:S(2)}, u32[]{:S(2)}) collective-permute-start(bf16[256,256]{1,0:T(8,128)(2,1)} %bitcast.29), channel_id=1, source_target_pairs={{0,4},{4,0},{8,12},{12,8},{16,20},{20,16},{24,28},{28,24},{1,5},{5... | collective-permute-start | bytes 393224 | tf_op jit(solution)/shard_map/ppermute | solution.py:270
  13.2 0.9 %copy-start = (bf16[1,1,16,16,256]{4,3,2,1,0:T(8,128)(2,1)S(1)}, bf16[1,1,16,16,256]{4,3,2,1,0:T(8,128)(2,1)}, u32[]{:S(2)}) copy-start(bf16[1,1,16,16,256]{4,3,2,1,0:T(8,128)(2,1)} %param.7) | copy-start | bytes 393220
  14.1 0.9 %copy-start.2 = (bf16[1,1,16,16,256]{4,3,2,1,0:T(8,128)(2,1)S(1)}, bf16[1,1,16,16,256]{4,3,2,1,0:T(8,128)(2,1)}, u32[]{:S(2)}) copy-start(bf16[1,1,16,16,256]{4,3,2,1,0:T(8,128)(2,1)} %param.8) | copy-start | bytes 393220
  15.0 1.0 %copy-start.5 = (bf16[256,1024]{1,0:T(8,128)(2,1)S(1)}, bf16[256,1024]{1,0:T(8,128)(2,1)}, u32[]{:S(2)}) copy-start(bf16[256,1024]{1,0:T(8,128)(2,1)} %win_ref.1) | copy-start | bytes 1572868
  16.1 1.0 %copy-start.6 = (bf16[1024,256]{1,0:T(8,128)(2,1)S(1)}, bf16[1024,256]{1,0:T(8,128)(2,1)}, u32[]{:S(2)}) copy-start(bf16[1024,256]{1,0:T(8,128)(2,1)} %wout_ref.1) | copy-start | bytes 1572868
  17.1 4.0 %copy-start.1 = (bf16[1,1,16,16,256]{4,3,2,1,0:T(8,128)(2,1)S(1)}, bf16[1,1,16,16,256]{4,3,2,1,0:T(8,128)(2,1)}, u32[]{:S(2)}) copy-start(bf16[1,1,16,16,256]{4,3,2,1,0:T(8,128)(2,1)} %param.7) | copy-start | bytes 393220
  21.0 2.0 %collective-permute-start.4 = (bf16[4,256,256]{2,1,0:T(8,128)(2,1)S(1)}, bf16[4,256,256]{2,1,0:T(8,128)(2,1)S(1)}, u32[]{:S(2)}, u32[]{:S(2)}) collective-permute-start(bf16[4,256,256]{2,1,0:T(8,128)(2,1)S(1)} %get-tuple-element.22), channel_id=1, source_target_pairs={{0,1},{1,0},{2,3},{3,2},{4,5},{5,4},{6,7},{7,6},{8,9},{9,8},{10,11... | collective-permute-start | bytes 1572872 | tf_op jit(solution)/shard_map/ppermute | solution.py:267
  23.1 6.1 %collective-permute-start.5 = (bf16[272,256]{1,0:T(8,128)(2,1)S(1)}, bf16[272,256]{1,0:T(8,128)(2,1)S(1)}, u32[]{:S(2)}, u32[]{:S(2)}) collective-permute-start(bf16[272,256]{1,0:T(8,128)(2,1)S(1)} %get-tuple-element.24), channel_id=1, source_target_pairs={{0,2},{1,3},{2,0},{3,1},{4,6},{5,7},{6,4},{7,5},{8,10},{9,11},{10,... | collective-permute-start | bytes 417800 | tf_op jit(solution)/shard_map/ppermute | solution.py:267
  24.7 6.5 %collective-permute-start.6 = (bf16[272,256]{1,0:T(8,128)(2,1)S(1)}, bf16[272,256]{1,0:T(8,128)(2,1)S(1)}, u32[]{:S(2)}, u32[]{:S(2)}) collective-permute-start(bf16[272,256]{1,0:T(8,128)(2,1)S(1)} %get-tuple-element.25), channel_id=1, source_target_pairs={{0,4},{1,5},{2,6},{3,7},{4,0},{5,1},{6,2},{7,3},{8,12},{9,13},{10,... | collective-permute-start | bytes 417800 | tf_op jit(solution)/shard_map/ppermute | solution.py:267
  24.7 8.7 %collective-permute-start.7 = (bf16[272,256]{1,0:T(8,128)(2,1)S(1)}, bf16[272,256]{1,0:T(8,128)(2,1)S(1)}, u32[]{:S(2)}, u32[]{:S(2)}) collective-permute-start(bf16[272,256]{1,0:T(8,128)(2,1)S(1)} %get-tuple-element.26), channel_id=1, source_target_pairs={{0,6},{1,7},{2,4},{3,5},{4,2},{5,3},{6,0},{7,1},{8,14},{9,15},{10,... | collective-permute-start | bytes 417800 | tf_op jit(solution)/shard_map/ppermute | solution.py:267
  33.5 16.9 %copy-start.3 = (bf16[1,1,16,16,256]{4,3,2,1,0:T(8,128)(2,1)S(1)}, bf16[1,1,16,16,256]{4,3,2,1,0:T(8,128)(2,1)}, u32[]{:S(2)}) copy-start(bf16[1,1,16,16,256]{4,3,2,1,0:T(8,128)(2,1)} %param.8) | copy-start | bytes 393220
  33.5 8.5 %collective-permute-start.10 = (bf16[272,256]{1,0:T(8,128)(2,1)S(1)}, bf16[272,256]{1,0:T(8,128)(2,1)S(1)}, u32[]{:S(2)}, u32[]{:S(2)}) collective-permute-start(bf16[272,256]{1,0:T(8,128)(2,1)S(1)} %add_convert_fusion.1), channel_id=1, source_target_pairs={{0,24},{1,25},{2,26},{3,27},{4,28},{5,29},{6,30},{7,31},{8,16},{9,... | collective-permute-start | bytes 417800 | tf_op jit(solution)/shard_map/ppermute | solution.py:267
  35.2 11.4 %collective-permute-start.9 = (bf16[272,256]{1,0:T(8,128)(2,1)S(1)}, bf16[272,256]{1,0:T(8,128)(2,1)S(1)}, u32[]{:S(2)}, u32[]{:S(2)}) collective-permute-start(bf16[272,256]{1,0:T(8,128)(2,1)S(1)} %add_convert_fusion.1), channel_id=1, source_target_pairs={{0,16},{1,17},{2,18},{3,19},{4,20},{5,21},{6,22},{7,23},{8,24},{9,... | collective-permute-start | bytes 417800 | tf_op jit(solution)/shard_map/ppermute | solution.py:267
  35.2 11.4 %collective-permute-start.8 = (bf16[272,256]{1,0:T(8,128)(2,1)S(1)}, bf16[272,256]{1,0:T(8,128)(2,1)S(1)}, u32[]{:S(2)}, u32[]{:S(2)}) collective-permute-start(bf16[272,256]{1,0:T(8,128)(2,1)S(1)} %add_convert_fusion.1), channel_id=1, source_target_pairs={{0,8},{1,9},{2,10},{3,11},{4,12},{5,13},{6,14},{7,15},{8,0},{9,1},... | collective-permute-start | bytes 417800 | tf_op jit(solution)/shard_map/ppermute | solution.py:267
  46.8 15.0 %collective-permute-start.13 = (bf16[272,256]{1,0:T(8,128)(2,1)S(1)}, bf16[272,256]{1,0:T(8,128)(2,1)S(1)}, u32[]{:S(2)}, u32[]{:S(2)}) collective-permute-start(bf16[272,256]{1,0:T(8,128)(2,1)S(1)} %add_convert_fusion.refs_0_), channel_id=1, source_target_pairs={{0,6},{1,7},{2,4},{3,5},{4,2},{5,3},{6,0},{7,1},{8,14},{9,15},{10,... | collective-permute-start | bytes 417800 | tf_op jit(solution)/shard_map/ppermute | solution.py:267
  49.3 13.0 %collective-permute-start.12 = (bf16[272,256]{1,0:T(8,128)(2,1)S(1)}, bf16[272,256]{1,0:T(8,128)(2,1)S(1)}, u32[]{:S(2)}, u32[]{:S(2)}) collective-permute-start(bf16[272,256]{1,0:T(8,128)(2,1)S(1)} %add_convert_fusion.refs_0_), channel_id=1, source_target_pairs={{0,4},{1,5},{2,6},{3,7},{4,0},{5,1},{6,2},{7,3},{8,12},{9,13},{10,... | collective-permute-start | bytes 417800 | tf_op jit(solution)/shard_map/ppermute | solution.py:267
  49.8 12.6 %collective-permute-start.11 = (bf16[272,256]{1,0:T(8,128)(2,1)S(1)}, bf16[272,256]{1,0:T(8,128)(2,1)S(1)}, u32[]{:S(2)}, u32[]{:S(2)}) collective-permute-start(bf16[272,256]{1,0:T(8,128)(2,1)S(1)} %add_convert_fusion.refs_0_), channel_id=1, source_target_pairs={{0,2},{1,3},{2,0},{3,1},{4,6},{5,7},{6,4},{7,5},{8,10},{9,11},{10,... | collective-permute-start | bytes 417800 | tf_op jit(solution)/shard_map/ppermute | solution.py:267
  52.4 9.4 %collective-permute-start.2 = (bf16[256,256]{1,0:T(8,128)(2,1)S(1)}, bf16[256,256]{1,0:T(8,128)(2,1)S(1)}, u32[]{:S(2)}, u32[]{:S(2)}) collective-permute-start(bf16[256,256]{1,0:T(8,128)(2,1)S(1)} %get-tuple-element.19), channel_id=1, source_target_pairs={{0,4},{4,0},{8,12},{12,8},{16,20},{20,16},{24,28},{28,24},{1,5},{5... | collective-permute-start | bytes 393224 | tf_op jit(solution)/shard_map/ppermute | solution.py:270
  54.0 8.8 %collective-permute-start.3 = (bf16[256,256]{1,0:T(8,128)(2,1)S(1)}, bf16[256,256]{1,0:T(8,128)(2,1)S(1)}, u32[]{:S(2)}, u32[]{:S(2)}) collective-permute-start(bf16[256,256]{1,0:T(8,128)(2,1)S(1)} %get-tuple-element.20), channel_id=1, source_target_pairs={{0,28},{4,8},{8,4},{12,16},{16,12},{20,24},{24,20},{28,0},{1,29},{... | collective-permute-start | bytes 393224 | tf_op jit(solution)/shard_map/ppermute | solution.py:274
  61.8 1.8 %collective-permute-start.14 = (bf16[272,256]{1,0:T(8,128)(2,1)S(1)}, bf16[272,256]{1,0:T(8,128)(2,1)S(1)}, u32[]{:S(2)}, u32[]{:S(2)}) collective-permute-start(bf16[272,256]{1,0:T(8,128)(2,1)S(1)} %add_convert_fusion.refs_0_), channel_id=1, source_target_pairs={{0,1},{1,0},{2,3},{3,2},{4,5},{5,4},{6,7},{7,6},{8,9},{9,8},{10,11... | collective-permute-start | bytes 417800 | tf_op jit(solution)/shard_map/ppermute | solution.py:267
  61.8 1.8 %collective-permute-start.17 = (bf16[272,256]{1,0:T(8,128)(2,1)S(1)}, bf16[272,256]{1,0:T(8,128)(2,1)S(1)}, u32[]{:S(2)}, u32[]{:S(2)}) collective-permute-start(bf16[272,256]{1,0:T(8,128)(2,1)S(1)} %collective-permute-done.13.refs_3_), channel_id=1, source_target_pairs={{0,1},{1,0},{2,3},{3,2},{4,5},{5,4},{6,7},{7,6},{8,9},{9,8},{10,11... | collective-permute-start | bytes 417800 | tf_op jit(solution)/shard_map/ppermute | solution.py:267
  62.3 1.4 %collective-permute-start.16 = (bf16[272,256]{1,0:T(8,128)(2,1)S(1)}, bf16[272,256]{1,0:T(8,128)(2,1)S(1)}, u32[]{:S(2)}, u32[]{:S(2)}) collective-permute-start(bf16[272,256]{1,0:T(8,128)(2,1)S(1)} %collective-permute-done.12.refs_2_), channel_id=1, source_target_pairs={{0,1},{1,0},{2,3},{3,2},{4,5},{5,4},{6,7},{7,6},{8,9},{9,8},{10,11... | collective-permute-start | bytes 417800 | tf_op jit(solution)/shard_map/ppermute | solution.py:267
  62.4 1.5 %collective-permute-start.15 = (bf16[272,256]{1,0:T(8,128)(2,1)S(1)}, bf16[272,256]{1,0:T(8,128)(2,1)S(1)}, u32[]{:S(2)}, u32[]{:S(2)}) collective-permute-start(bf16[272,256]{1,0:T(8,128)(2,1)S(1)} %collective-permute-done.11.refs_1_), channel_id=1, source_target_pairs={{0,1},{1,0},{2,3},{3,2},{4,5},{5,4},{6,7},{7,6},{8,9},{9,8},{10,11... | collective-permute-start | bytes 417800 | tf_op jit(solution)/shard_map/ppermute | solution.py:267

commit v2 on v1

v2 whole, which is shorter than its diff:
```python
import functools
import math

import jax
import jax.numpy as jnp
from jax import lax
from jax.experimental import pallas as pl
from jax.experimental.pallas import tpu as pltpu
from jax.sharding import PartitionSpec as P

C = 256
HID = 1024
TAPS = 7
STEP = 2
HALO = 6
N = 16
ROWS = N + 2 * HALO
LANES = 128
FRAME = 32
LEFT = 8
GROUP = 4
JOIN_COST = 30_000_000_000
EXTRA = 16
F32 = jnp.float32
BF16 = jnp.bfloat16
GELU_A = math.sqrt(2.0 / math.pi)
GELU_B = 0.044715
SIDE_CELLS = 2 * HALO * N + 2 * LEFT * N
RIMS = (
    (slice(0, HALO), slice(LEFT, LEFT + N), slice(0, 96)),
    (slice(HALO + N, ROWS), slice(LEFT, LEFT + N), slice(96, 192)),
    (slice(HALO, HALO + N), slice(0, LEFT), slice(192, 320)),
    (slice(HALO, HALO + N), slice(LEFT + N, FRAME), slice(320, 448)),
)
VMEM = pl.BlockSpec(memory_space=pltpu.VMEM)
ANY = pl.BlockSpec(memory_space=pl.ANY)
HBM = pl.BlockSpec(memory_space=pltpu.HBM)
SMEM = pl.BlockSpec(memory_space=pltpu.SMEM)


def span(s):
    return s.stop - s.start


def dot(a, b, ca, cb):
    return lax.dot_general(a, b, (((ca,), (cb,)), ((), ())), preferred_element_type=F32)


def tap_offset(b):
    return LEFT - HALO + STEP * b


def span(s):
    return s.stop - s.start


def side_targets(owners, neighbour, code, position):
    targets = []
    for s in range(4):
        offset = lax.rem(neighbour[0, s] - position + 1 + owners, owners)
        first = (offset == 0) == (lax.rem(position, 2) == 1)
        source = jnp.where(offset == 1, 0, jnp.where(first, 1, 2))
        edge = code[0, s] & 3
        flipped = (code[0, s] >> 2) & 1
        along = jnp.where(edge < 2, 1, N)
        across = jnp.where(edge < 2, N, 1)
        far = edge & 1
        base = source * (N * N) + flipped * (N - 1) * along + far * (N - 1) * across
        step_k = across * (1 - 2 * far)
        step_m = along * (1 - 2 * flipped)
        n = HALO * N if s < 2 else LEFT * N
        rho = lax.broadcasted_iota(jnp.int32, (n, 1), 0)
        if s < 2:
            m = rho & (N - 1)
            k = rho >> 4
            if s == 0:
                k = HALO - 1 - k
            targets.append(base + step_k * k + step_m * m)
        else:
            m = rho >> 3
            q = rho & (LEFT - 1)
            k = LEFT - 1 - q if s == 2 else q
            targets.append(jnp.where(k < HALO, base + step_k * k + step_m * m, -1))
    return jnp.concatenate(targets, 0)


def prepare_kernel(
    owners, neighbour, code, position, own_hbm, cot_hbm, taps_hbm, win_hbm, wout_hbm,
    onehot, frame, d_hidden, cot_ref, taps_ref, win_ref, own_ref, wout_ref, sems,
):
    copies = [
        pltpu.make_async_copy(src, dst, sems.at[n])
        for n, (src, dst) in enumerate(
            (
                (own_hbm, own_ref),
                (cot_hbm, cot_ref),
                (wout_hbm, wout_ref),
                (win_hbm, win_ref),
                (taps_hbm, taps_ref),
            )
        )
    ]
    for copy in copies:
        copy.start()
    target = side_targets(owners, neighbour, code, position[0])
    lane = lax.broadcasted_iota(jnp.int32, (SIDE_CELLS, 3 * N * N), 1)
    onehot[...] = jnp.where(target == lane, 1.0, 0.0).astype(BF16)
    corner = jnp.zeros((HALO, LEFT, LANES), F32)
    copies[0].wait()
    own = own_ref[...]
    rims = dot(onehot[:, : N * N], own, 1, 0)
    inner = own.astype(F32).reshape(N, N, C)
    for l in range(C // LANES):
        lanes = slice(l * LANES, (l + 1) * LANES)
        for top in (0, HALO + N):
            for left in (0, LEFT + N):
                frame[l, top : top + HALO, left : left + LEFT, :] = corner
        for rows, cols, cells in RIMS:
            frame[l, rows, cols, :] = rims[cells, lanes].reshape(span(rows), span(cols), LANES)
        frame[l, HALO : HALO + N, LEFT : LEFT + N, :] = inner[:, :, lanes]
    copies[1].wait()
    copies[2].wait()
    d_hidden[...] = dot(cot_ref[...], wout_ref[...], 1, 1)
    copies[3].wait()
    copies[4].wait()


def add_rims(cells_to, tile_ref, onehot, frame):
    rims = dot(onehot[:, cells_to], tile_ref[...], 1, 0)
    for l in range(C // LANES):
        lanes = slice(l * LANES, (l + 1) * LANES)
        for rows, cols, cells in RIMS:
            frame[l, rows, cols, :] += rims[cells, lanes].reshape(span(rows), span(cols), LANES)


def one_kernel(start_ref, one_ref, onehot, frame):
    del start_ref
    add_rims(slice(N * N, 2 * N * N), one_ref, onehot, frame)


def forward_kernel(
    core, start_ref, two_ref, onehot, d_hidden_ref, cot_ref, taps_ref, win_ref,
    send_ref, keep_ref, dconv_ref, frame, conv,
):
    del start_ref
    add_rims(slice(2 * N * N, 3 * N * N), two_ref, onehot, frame)
    for l in range(C // LANES):
        lanes = slice(l * LANES, (l + 1) * LANES)
        acc = [None] * N
        for b in range(TAPS):
            off = tap_offset(b)
            coef = [taps_ref[a * TAPS + b : a * TAPS + b + 1, lanes] for a in range(TAPS)]
            for r in range(ROWS):
                x = frame[l, r, off : off + N, :]
                for a in range(TAPS):
                    i = r - STEP * a
                    if 0 <= i < N:
                        term = x * coef[a]
                        acc[i] = term if acc[i] is None else acc[i] + term
        for i in range(N):
            conv[i * N : (i + 1) * N, lanes] = acc[i]
    value = conv[...]
    centred = value - jnp.mean(value, -1, keepdims=True)
    inv_std = lax.rsqrt(jnp.mean(centred * centred, -1, keepdims=True) + 1e-06)
    normed_f = centred * inv_std
    normed = normed_f.astype(BF16)
    cot = cot_ref[...]
    first = core[0] == 0
    d_normed = None
    for h in range(GROUP):
        cols = slice(h * C, (h + 1) * C)
        w_in = win_ref[:, cols]
        pre = dot(normed, w_in, 1, 0)
        square = pre * pre
        t = jnp.tanh(pre * (GELU_A + (GELU_A * GELU_B) * square))
        half = 0.5 + 0.5 * t
        hidden = (pre * half).astype(BF16)
        slope = half + (0.5 * pre) * (1.0 - t * t) * (GELU_A + (3.0 * GELU_A * GELU_B) * square)
        d_pre = (d_hidden_ref[:, cols] * slope).astype(BF16)
        part_out = dot(hidden, cot, 0, 0).astype(BF16)
        part_in = dot(normed, d_pre, 0, 0).astype(BF16)
        send_ref[h] = jnp.where(first, part_out, part_in)
        keep_ref[h] = jnp.where(first, part_in, part_out)
        back = dot(d_pre, w_in, 1, 1)
        d_normed = back if d_normed is None else d_normed + back
    dconv_ref[...] = inv_std * (
        d_normed
        - jnp.mean(d_normed, -1, keepdims=True)
        - normed_f * jnp.mean(d_normed * normed_f, -1, keepdims=True)
    )


def taps_kernel(frame, dconv_ref, out_ref):
    out_ref[...] = jnp.zeros(out_ref.shape, F32)
    for l in range(C // LANES):
        lanes = slice(l * LANES, (l + 1) * LANES)
        grad = [dconv_ref[i * N : (i + 1) * N, lanes] for i in range(N)]
        for b in range(TAPS):
            off = tap_offset(b)
            acc = [None] * TAPS
            for r in range(ROWS):
                x = frame[l, r, off : off + N, :]
                for a in range(TAPS):
                    i = r - STEP * a
                    if 0 <= i < N:
                        term = x * grad[i]
                        acc[a] = term if acc[a] is None else acc[a] + term
            for a in range(TAPS):
                t = a * TAPS + b
                out_ref[t // EXTRA, t % EXTRA : t % EXTRA + 1, lanes] = jnp.sum(
                    acc[a], 0, keepdims=True
                )


def backward_kernel(onehot, dconv_ref, taps_ref, cot_ref, own_ref, one_ref, two_ref, shifted, rim):
    residues = (2, 4, 6, 0)
    pad = jnp.zeros((ROWS, 8, LANES), F32)
    for l in range(C // LANES):
        lanes = slice(l * LANES, (l + 1) * LANES)
        grad = [
            [dconv_ref[i * N + 8 * t : i * N + 8 * t + 8, lanes] for t in range(2)]
            for i in range(N)
        ]
        for n, s in enumerate(residues):
            shifted[l, n, :, 0:8, :] = pad
            shifted[l, n, :, 32:40, :] = pad
            pieces = [(b, tap_offset(b) // 8) for b in range(TAPS) if tap_offset(b) % 8 == s]
            coef = {
                (a, b): taps_ref[a * TAPS + b : a * TAPS + b + 1, lanes]
                for a in range(TAPS)
                for b, _ in pieces
            }
            for r in range(ROWS):
                acc = [None] * 3
                for a in range(TAPS):
                    i = r - STEP * a
                    if 0 <= i < N:
                        for b, up in pieces:
                            for t in range(2):
                                term = grad[i][t] * coef[a, b]
                                acc[t + up] = term if acc[t + up] is None else acc[t + up] + term
                for t in range(3):
                    shifted[l, n, r, 8 + 8 * t : 16 + 8 * t, :] = (
                        jnp.zeros((8, LANES), F32) if acc[t] is None else acc[t]
                    )

        def gather(rows, first_col, count):
            total = None
            for n, s in enumerate(residues):
                at = 8 + first_col - s
                piece = shifted[l, n, rows, at : at + count, :]
                total = piece if total is None else total + piece
            return total

        top = gather(slice(0, HALO), LEFT, N)
        bottom = gather(slice(HALO + N, ROWS), LEFT, N)
        middle = slice(HALO, HALO + N)
        left = gather(middle, 0, 8)
        right = gather(middle, LEFT + N, 8)
        inner = gather(middle, LEFT, N)
        at = 0
        for block in (top, bottom, left, right):
            n = block.shape[0] * block.shape[1]
            rim[at : at + n, lanes] = block.reshape(n, LANES).astype(BF16)
            at += n
        own_ref[:, lanes] = inner.reshape(N * N, LANES) + cot_ref[:, lanes].astype(F32)
    cells = rim[...]
    own_ref[...] += dot(onehot[:, : N * N], cells, 0, 0)
    one_ref[...] = dot(onehot[:, N * N : 2 * N * N], cells, 0, 0).astype(BF16)
    two_ref[...] = dot(onehot[:, 2 * N * N :], cells, 0, 0).astype(BF16)


def spread_kernel(place, keep_ref, got_ref, taps_ref, own_ref, one_ref, two_ref, three_ref):
    for d, out in enumerate((own_ref, one_ref, two_ref, three_ref)):
        j = place[0] ^ d
        out[:C, :] = (keep_ref[j].astype(F32) + got_ref[j].astype(F32)).astype(out.dtype)
        out[C:, :] = taps_ref[j].astype(out.dtype)


def store_blocks(scale, to_in, place, blocks, in_hbm, out_hbm, stage, sems):
    copies = []
    for d in range(GROUP):
        stage[d] = blocks[d][:C, :].astype(F32) * scale
        at = pl.ds(pl.multiple_of((place ^ d) * C, C), C)
        into_in = pltpu.make_async_copy(stage.at[d], in_hbm.at[:, at], sems.at[d])
        into_out = pltpu.make_async_copy(stage.at[d], out_hbm.at[at, :], sems.at[d])
        pl.when(to_in)(into_in.start)
        pl.when(jnp.logical_not(to_in))(into_out.start)
        copies.append((into_in, into_out))
    return copies


def wait_blocks(to_in, copies):
    for into_in, into_out in copies:
        pl.when(to_in)(into_in.wait)
        pl.when(jnp.logical_not(to_in))(into_out.wait)


def finish_mine_kernel(scale, core, place, *refs):
    blocks = refs[:GROUP]
    in_hbm, out_hbm, rows, stage, sems = refs[GROUP:]
    to_in = core[0] == 0
    copies = store_blocks(scale, to_in, place[0], blocks, in_hbm, out_hbm, stage, sems)
    for d in range(GROUP):
        rows[place[0] ^ d] = blocks[d][C:, :].astype(F32)
    wait_blocks(to_in, copies)


def finish_theirs_kernel(scale, core, place, *refs):
    blocks, (mine_ref, _, _) = refs[:GROUP], refs[GROUP : GROUP + 3]
    in_hbm, out_hbm, kernel_ref, rows, stage, sems = refs[GROUP + 3 :]
    to_in = core[0] != 0
    copies = store_blocks(scale, to_in, place[0], blocks, in_hbm, out_hbm, stage, sems)
    for d in range(GROUP):
        rows[place[0] ^ d] = blocks[d][C:, :].astype(F32)
    for j in range(GROUP):
        n = min(EXTRA, TAPS * TAPS - j * EXTRA)
        kernel_ref[j * EXTRA : j * EXTRA + n, :] = (mine_ref[j, :n, :] + rows[j, :n, :]) * scale
    wait_blocks(to_in, copies)


def join_kernel(own_ref, one_ref, two_ref, out_ref):
    out_ref[...] = (own_ref[...] + one_ref[...].astype(F32) + two_ref[...].astype(F32)).astype(BF16)


def in_hbm(x):
    return pltpu.with_memory_space_constraint(x, pltpu.HBM)


def call(kernel, outs, scratch=(), specs=(), flops=0, aliases={}, out_specs=None, vmem=16):
    return pl.pallas_call(
        kernel,
        out_shape=outs,
        in_specs=specs,
        out_specs=out_specs or jax.tree.map(lambda _: VMEM, outs),
        scratch_shapes=scratch,
        input_output_aliases=aliases,
        compiler_params=pltpu.CompilerParams(vmem_limit_bytes=vmem * 1024 * 1024),
        cost_estimate=pl.CostEstimate(flops=flops, bytes_accessed=0, transcendentals=0),
    )


def body(features, cotangent, kernel, weight_in, weight_out, tile_neighbour, edge_code):
    owners = lax.axis_size("tile")
    members = lax.axis_size("ens")
    position = lax.axis_index("tile")
    member = lax.axis_index("ens")
    devices = owners * members
    scale = 1.0 / math.sqrt(devices * N * N)
    both = ("tile", "ens")
    struct = jax.ShapeDtypeStruct

    def one_over(x):
        return lax.ppermute(x, "tile", [(i, i ^ 1) for i in range(owners)])

    def two_over(x):
        moves = [(i, (i + 1 if i % 2 else i - 1) % owners) for i in range(owners)]
        return lax.ppermute(x, "tile", moves)

    index = position * members + member
    free = [1 << n for n in range(2, members.bit_length() - 1)]
    free += [members << n for n in range(1, owners.bit_length() - 1)]
    pairs = ((2, members), (free[0], free[1]))
    later = [tuple(free[n : n + 2]) for n in range(2, len(free), 2)]

    def swap(x, even, odd):
        return lax.ppermute(x, both, [(i, i ^ (odd if i % 2 else even)) for i in range(devices)])

    def digit(pair):
        return jnp.where(index & pair[0], 1, 0) + jnp.where(index & pair[1], 2, 0)

    core = member % 2
    digits = (digit(pairs[0]), digit(pairs[1]))
    mine_at = jnp.where(core == 0, digits[0], digits[1]).astype(jnp.int32).reshape(1)
    theirs_at = jnp.where(core == 0, digits[1], digits[0]).astype(jnp.int32).reshape(1)
    core = core.reshape(1).astype(jnp.int32)
    combos = [[p[0], p[1], p[0] + p[1]] for p in pairs]

    own = features.reshape(N * N, C)
    one = one_over(own)
    two = two_over(own)

    frame = pltpu.VMEM((2, ROWS, FRAME, LANES), F32)
    onehot, frame_one, d_hidden, cot, taps, w_in = call(
        functools.partial(prepare_kernel, owners),
        (
            pltpu.VMEM((SIDE_CELLS, 3 * N * N), BF16),
            frame,
            pltpu.VMEM((N * N, HID), F32),
            pltpu.VMEM((N * N, C), BF16),
            pltpu.VMEM((TAPS * TAPS, C), F32),
            pltpu.VMEM((C, HID), BF16),
        ),
        [
            pltpu.VMEM((N * N, C), BF16),
            pltpu.VMEM((HID, C), BF16),
            pltpu.SemaphoreType.DMA((5,)),
        ],
        [SMEM] * 3 + [HBM] * 5,
    )(
        tile_neighbour, edge_code, position.reshape(1).astype(jnp.int32),
        *map(in_hbm, (own, cotangent.reshape(N * N, C), kernel, weight_in, weight_out)),
    )
    frame_one = call(
        one_kernel, frame, (), [VMEM] * 3, aliases={0: 0}
    )(frame_one, one, onehot)
    half = pltpu.VMEM((GROUP, C, C), BF16)
    send, keep, dconv, frame_two = call(
        forward_kernel,
        (half, half, pltpu.VMEM((N * N, C), F32), frame),
        [pltpu.VMEM((N * N, C), F32)],
        [SMEM] + [VMEM] * 7,
        aliases={1: 3},
    )(core, frame_one, two, onehot, d_hidden, cot, taps, w_in)
    got = swap(send, 1, 1)
    part_taps = call(
        taps_kernel, pltpu.VMEM((GROUP, EXTRA, C), F32), (), [VMEM] * 2
    )(frame_two, dconv)

    block = struct((C + EXTRA, C), BF16)
    pieces = call(
        spread_kernel, (block,) * GROUP, (), [SMEM] + [VMEM] * 3
    )(mine_at, keep, got, part_taps)
    total = pieces[0].astype(F32)
    for piece, even, odd in zip(pieces[1:], *combos):
        total = total + swap(piece, even, odd).astype(F32)
    total = total.astype(BF16)

    grad_own, grad_one, grad_two = call(
        backward_kernel,
        (pltpu.VMEM((N * N, C), F32), pltpu.VMEM((N * N, C), BF16), pltpu.VMEM((N * N, C), BF16)),
        [pltpu.VMEM((2, 4, ROWS, 40, LANES), F32), pltpu.VMEM((28 * N, C), BF16)],
        [VMEM] * 4,
    )(onehot, dconv, taps, cot)
    total, grad_one, grad_two = lax.optimization_barrier((total, grad_one, grad_two))

    back_two = two_over(grad_two)
    back_one = one_over(grad_one)
    for even, odd in [(pairs[1], pairs[0])] + [(p, p) for p in later]:
        got = [swap(total, a, b) for a, b in zip(even, odd)]
        summed = total.astype(F32) + got[0].astype(F32)
        if len(got) == 2:
            third = swap(total, sum(even), sum(odd))
            summed = summed + (got[1].astype(F32) + third.astype(F32))
        total = summed.astype(BF16)
    mine = [total] + [swap(total, even, odd) for even, odd in zip(*combos)]
    grad_features = call(
        join_kernel, struct((N * N, C), BF16), (), [VMEM] * 3, flops=JOIN_COST
    )(grad_own, back_one, back_two)
    mine, grad_features = lax.optimization_barrier((mine, grad_features))
    theirs = [swap(x, 1, 1) for x in mine]
    grads = (struct((C, HID), F32), struct((HID, C), F32))
    rows = struct((GROUP, EXTRA, C), F32)
    stage = [pltpu.VMEM((GROUP, C, C), F32), pltpu.SemaphoreType.DMA((GROUP,))]
    grad_in, grad_out, rows_mine = call(
        functools.partial(finish_mine_kernel, scale),
        (*grads, rows),
        stage,
        [SMEM] * 2 + [VMEM] * GROUP,
        out_specs=(ANY, ANY, VMEM),
    )(core, mine_at, *mine)
    grad_in, grad_out, grad_kernel = call(
        functools.partial(finish_theirs_kernel, scale),
        (*grads, struct((TAPS * TAPS, C), F32)),
        [pltpu.VMEM((GROUP, EXTRA, C), F32)] + stage,
        [SMEM] * 2 + [VMEM] * (GROUP + 1) + [ANY] * 2,
        out_specs=(ANY, ANY, VMEM),
        aliases={GROUP + 3: 0, GROUP + 4: 1},
    )(core, theirs_at, *theirs, rows_mine, grad_in, grad_out)
    return grad_features.reshape(features.shape), grad_kernel, grad_in, grad_out


def solution(mesh):
    halved = P("ens", "tile", None, None, None)
    in_specs = (halved, halved, P(), P(), P(), P("tile", None), P("tile", None))
    out_specs = (halved, P(), P(), P())
    return jax.shard_map(body, mesh=mesh, in_specs=in_specs, out_specs=out_specs, check_vma=False)
```

time: 65.5 us -> 52.1 us (0.80)
  the two profiles are of different devices: /device:TPU:0 before, /device:TPU:25 now
where the time goes in v2:
time: 52.1 us; the launch traced here: 52 us
  starting transfers between devices  23.2 us (45%)
  waiting for transfers between devices  15.1 us (29%)
  Pallas kernels  12.1 us (23%)
  between operations  0.72 us (1%)
  local copies, waits for them, and re-layouts  0.67 us (1%)
    ppermute x14, starting transfers between devices, swap(): lax.ppermute(x, both, [(i, i ^ (odd if i % 2 else even)) for i in range(d...  19.1 us
    ppermute x14, waiting for transfers between devices, swap(): lax.ppermute(x, both, [(i, i ^ (odd if i % 2 else even)) for i in range(d...  11.9 us
    pallas_call x1, Pallas kernels, body(): call(forward_kernel, (half, half, pltpu.VMEM((N * N, C), F32), frame), [p...  3.91 us
    ppermute x2, waiting for transfers between devices, two_over(): return lax.ppermute(x, 'tile', moves)  2.95 us
    pallas_call x1, Pallas kernels, body(): call(functools.partial(prepare_kernel, owners), (pltpu.VMEM((SIDE_CELLS,...  2.2 us
    ppermute x2, starting transfers between devices, one_over(): return lax.ppermute(x, 'tile', [(i, i ^ 1) for i in range(owners)])  2.18 us
    ppermute x2, starting transfers between devices, two_over(): return lax.ppermute(x, 'tile', moves)  1.89 us
    pallas_call x1, Pallas kernels, body(): call(functools.partial(finish_theirs_kernel, scale), (*grads, struct((TAP...  1.64 us
  transfers between devices with their start and end apart: 18, of which 11 were waited for; matrix products, arithmetic and copies ran while one was open for 0% of the time, Pallas kernels for 12%

profile of v2, /device:TPU:25, one launch (start us, length us, event | category | flops | bytes accessed | tf_op | source)
XLA Modules:
  0.0 52.0 jit_solution(3670402512545388765)
XLA Ops:
  0.6 1.3 %collective-permute-start = (bf16[256,256]{1,0:T(8,128)(2,1)}, bf16[256,256]{1,0:T(8,128)(2,1)S(1)}, u32[]{:S(2)}, u32[]{:S(2)}) collective-permute-start(bf16[256,256]{1,0:T(8,128)(2,1)} %bitcast.8), channel_id=1, source_target_pairs={{0,4},{4,0},{8,12},{12,8},{16,20},{20,16},{24,28},{28,24},{1,5},{5... | collective-permute-start | bytes 393224 | tf_op jit(solution)/shard_map/ppermute | solution.py:354
  1.9 0.1 collective-permute-start.1
  2.1 0.0 copy-start
  2.1 0.0 copy-start.1
  2.1 0.7 %copy-done = s32[1,4]{1,0:T(1,128)S(1)} copy-done((s32[1,4]{1,0:T(1,128)S(1)}, s32[1,4]{1,0:T(1,128)}, u32[]{:S(2)}) %copy-start) | copy-done | bytes 40
  2.7 0.0 copy-done.1
  2.7 2.2 %shard_map.102 = (bf16[448,768]{1,0:T(8,128)(2,1)S(1)}, f32[2,28,32,128]{3,2,1,0:T(8,128)S(1)}, f32[256,1024]{1,0:T(8,128)S(1)}, bf16[256,256]{1,0:T(8,128)(2,1)...) custom-call(s32[1,4]{1,0:T(1,128)S(1)} %copy-done, s32[1,4]{1,0:T(1,128)S(1)} %copy-done.1, ...), custom_call_target="tpu_custom_call" | custom-call | tf_op jit(solution)/shard_map/pallas_call | solution.py:384
  4.9 0.3 collective-permute-done.one_ref
  5.3 0.2 shard_map.103.start_ref
  5.5 1.4 %collective-permute-done.1.two_ref = bf16[256,256]{1,0:T(8,128)(2,1)S(1)} collective-permute-done((bf16[256,256]{1,0:T(8,128)(2,1)}, bf16[256,256]{1,0:T(8,128)(2,1)S(1)}, u32[]{:S(2)}, u32[]{:S(2)}) %collective-permute-start.1) | collective-permute-done | bytes 131104 | tf_op jit(solution)/shard_map/ppermute | solution.py:358
  6.9 3.9 %shard_map.104 = (bf16[4,256,256]{2,1,0:T(8,128)(2,1)}, bf16[4,256,256]{2,1,0:T(8,128)(2,1)S(1)}, f32[256,256]{1,0:T(8,128)S(1)}, f32[2,28,32,128]{3,2,1,0:T(8,128)S(1)}) custom-call(s32[1]{0:T(128)} %bitcast.1.core, f32[2,28,32,128]{3,2,1,0:T(8,128)S(1)} %shard_map.103.start_ref, ...), custom_call_target="tpu_custom_call", output_to_operand_aliasing={{3}: (1, {})} | custom-call | tf_op jit(solution)/shard_map/pallas_call | solution.py:408
  10.8 2.9 %collective-permute-start.2 = (bf16[4,256,256]{2,1,0:T(8,128)(2,1)}, bf16[4,256,256]{2,1,0:T(8,128)(2,1)S(1)}, u32[]{:S(2)}, u32[]{:S(2)}) collective-permute-start(bf16[4,256,256]{2,1,0:T(8,128)(2,1)} %get-tuple-element.42), channel_id=1, source_target_pairs={{0,1},{1,0},{2,3},{3,2},{4,5},{5,4},{6,7},{7,6},{8,9},{9,8},{10,11... | collective-permute-start | bytes 1572872 | tf_op jit(solution)/shard_map/ppermute | solution.py:367
  13.8 0.9 %shard_map.105.taps_ref = f32[4,16,256]{2,1,0:T(8,128)S(1)} custom-call(f32[2,28,32,128]{3,2,1,0:T(8,128)S(1)} %get-tuple-element.43.frame, f32[256,256]{1,0:T(8,128)S(1)} %get-tuple-element.44.dconv_ref), custom_call_target="tpu_custom_call" | custom-call | tf_op jit(solution)/shard_map/pallas_call | solution.py:416
  14.7 0.8 %collective-permute-done.2.got_ref = bf16[4,256,256]{2,1,0:T(8,128)(2,1)S(1)} collective-permute-done((bf16[4,256,256]{2,1,0:T(8,128)(2,1)}, bf16[4,256,256]{2,1,0:T(8,128)(2,1)S(1)}, u32[]{:S(2)}, u32[]{:S(2)}) %collective-permute-start.2) | collective-permute-done | bytes 524320 | tf_op jit(solution)/shard_map/ppermute | solution.py:367
  15.5 0.1 shard_map.106
  15.6 0.2 collective-permute-start.3
  15.9 0.9 %collective-permute-start.4 = (bf16[272,256]{1,0:T(8,128)(2,1)S(1)}, bf16[272,256]{1,0:T(8,128)(2,1)S(1)}, u32[]{:S(2)}, u32[]{:S(2)}) collective-permute-start(bf16[272,256]{1,0:T(8,128)(2,1)S(1)} %get-tuple-element.47), channel_id=1, source_target_pairs={{0,4},{1,17},{2,6},{3,19},{4,0},{5,21},{6,2},{7,23},{8,12},{9,25},... | collective-permute-start | bytes 417800 | tf_op jit(solution)/shard_map/ppermute | solution.py:367
  16.8 2.4 %collective-permute-start.5 = (bf16[272,256]{1,0:T(8,128)(2,1)S(1)}, bf16[272,256]{1,0:T(8,128)(2,1)S(1)}, u32[]{:S(2)}, u32[]{:S(2)}) collective-permute-start(bf16[272,256]{1,0:T(8,128)(2,1)S(1)} %get-tuple-element.48), channel_id=1, source_target_pairs={{0,6},{1,25},{2,4},{3,27},{4,2},{5,29},{6,0},{7,31},{8,14},{9,17},... | collective-permute-start | bytes 417800 | tf_op jit(solution)/shard_map/ppermute | solution.py:367
  19.3 1.4 %shard_map.107 = (f32[256,256]{1,0:T(8,128)S(1)}, bf16[256,256]{1,0:T(8,128)(2,1)S(1)}, bf16[256,256]{1,0:T(8,128)(2,1)S(1)}) custom-call(bf16[448,768]{1,0:T(8,128)(2,1)S(1)} %get-tuple-element.36.onehot, f32[256,256]{1,0:T(8,128)S(1)} %get-tuple-element.44.dconv_ref, f32[49,256]{1,0:T(8,128)S(1)} %get-tuple-element.39.taps_ref, ...), custom_call_target="tpu_custom_call" | custom-call | tf_op jit(solution)/shard_map/pallas_call | solution.py:429
  20.6 0.3 collective-permute-done.3
  21.0 3.0 %collective-permute-done.4 = bf16[272,256]{1,0:T(8,128)(2,1)S(1)} collective-permute-done((bf16[272,256]{1,0:T(8,128)(2,1)S(1)}, bf16[272,256]{1,0:T(8,128)(2,1)S(1)}, u32[]{:S(2)}, u32[]{:S(2)}) %collective-permute-start.4) | collective-permute-done | bytes 139296 | tf_op jit(solution)/shard_map/ppermute | solution.py:367
  24.0 0.0 collective-permute-done.5
  24.0 0.1 add_convert_fusion.1
  24.1 1.9 %collective-permute-start.8 = (bf16[272,256]{1,0:T(8,128)(2,1)S(1)}, bf16[272,256]{1,0:T(8,128)(2,1)S(1)}, u32[]{:S(2)}, u32[]{:S(2)}) collective-permute-start(bf16[272,256]{1,0:T(8,128)(2,1)S(1)} %add_convert_fusion.1), channel_id=1, source_target_pairs={{0,24},{1,7},{2,26},{3,5},{4,28},{5,3},{6,30},{7,1},{8,16},{9,15},... | collective-permute-start | bytes 417800 | tf_op jit(solution)/shard_map/ppermute | solution.py:367
  26.0 0.3 collective-permute-start.7
  26.3 0.5 collective-permute-start.6
  26.8 0.9 %collective-permute-start.12 = (bf16[256,256]{1,0:T(8,128)(2,1)S(1)}, bf16[256,256]{1,0:T(8,128)(2,1)S(1)}, u32[]{:S(2)}, u32[]{:S(2)}) collective-permute-start(bf16[256,256]{1,0:T(8,128)(2,1)S(1)} %get-tuple-element.53), channel_id=1, source_target_pairs={{0,4},{4,0},{8,12},{12,8},{16,20},{20,16},{24,28},{28,24},{1,5},{5... | collective-permute-start | bytes 393224 | tf_op jit(solution)/shard_map/ppermute | solution.py:354
  27.7 1.8 %collective-permute-start.13 = (bf16[256,256]{1,0:T(8,128)(2,1)S(1)}, bf16[256,256]{1,0:T(8,128)(2,1)S(1)}, u32[]{:S(2)}, u32[]{:S(2)}) collective-permute-start(bf16[256,256]{1,0:T(8,128)(2,1)S(1)} %get-tuple-element.54), channel_id=1, source_target_pairs={{0,28},{4,8},{8,4},{12,16},{16,12},{20,24},{24,20},{28,0},{1,29},{... | collective-permute-start | bytes 393224 | tf_op jit(solution)/shard_map/ppermute | solution.py:358
  29.5 0.0 collective-permute-done.8
  29.5 1.0 %collective-permute-done.7 = bf16[272,256]{1,0:T(8,128)(2,1)S(1)} collective-permute-done((bf16[272,256]{1,0:T(8,128)(2,1)S(1)}, bf16[272,256]{1,0:T(8,128)(2,1)S(1)}, u32[]{:S(2)}, u32[]{:S(2)}) %collective-permute-start.7) | collective-permute-done | bytes 139296 | tf_op jit(solution)/shard_map/ppermute | solution.py:367
  30.5 0.2 collective-permute-done.6
  30.8 0.1 add_convert_fusion.refs_0_
  30.8 1.0 %collective-permute-start.11 = (bf16[272,256]{1,0:T(8,128)(2,1)S(1)}, bf16[272,256]{1,0:T(8,128)(2,1)S(1)}, u32[]{:S(2)}, u32[]{:S(2)}) collective-permute-start(bf16[272,256]{1,0:T(8,128)(2,1)S(1)} %add_convert_fusion.refs_0_), channel_id=1, source_target_pairs={{0,6},{1,25},{2,4},{3,27},{4,2},{5,29},{6,0},{7,31},{8,14},{9,17},... | collective-permute-start | bytes 417800 | tf_op jit(solution)/shard_map/ppermute | solution.py:367
  31.8 1.9 %collective-permute-start.10 = (bf16[272,256]{1,0:T(8,128)(2,1)S(1)}, bf16[272,256]{1,0:T(8,128)(2,1)S(1)}, u32[]{:S(2)}, u32[]{:S(2)}) collective-permute-start(bf16[272,256]{1,0:T(8,128)(2,1)S(1)} %add_convert_fusion.refs_0_), channel_id=1, source_target_pairs={{0,4},{1,17},{2,6},{3,19},{4,0},{5,21},{6,2},{7,23},{8,12},{9,25},... | collective-permute-start | bytes 417800 | tf_op jit(solution)/shard_map/ppermute | solution.py:367
  33.7 0.7 %collective-permute-start.9 = (bf16[272,256]{1,0:T(8,128)(2,1)S(1)}, bf16[272,256]{1,0:T(8,128)(2,1)S(1)}, u32[]{:S(2)}, u32[]{:S(2)}) collective-permute-start(bf16[272,256]{1,0:T(8,128)(2,1)S(1)} %add_convert_fusion.refs_0_), channel_id=1, source_target_pairs={{0,2},{1,9},{2,0},{3,11},{4,6},{5,13},{6,4},{7,15},{8,10},{9,1},{1... | collective-permute-start | bytes 417800 | tf_op jit(solution)/shard_map/ppermute | solution.py:367
  34.5 0.0 collective-permute-done.12.one_ref
  34.5 1.5 %collective-permute-done.13.two_ref = bf16[256,256]{1,0:T(8,128)(2,1)S(1)} collective-permute-done((bf16[256,256]{1,0:T(8,128)(2,1)S(1)}, bf16[256,256]{1,0:T(8,128)(2,1)S(1)}, u32[]{:S(2)}, u32[]{:S(2)}) %collective-permute-start.13) | collective-permute-done | bytes 131104 | tf_op jit(solution)/shard_map/ppermute | solution.py:358
  36.0 0.7 %shard_map.108 = bf16[256,256]{1,0:T(8,128)(2,1)} custom-call(f32[256,256]{1,0:T(8,128)S(1)} %get-tuple-element.52.own_ref, bf16[256,256]{1,0:T(8,128)(2,1)S(1)} %collective-permute-done.12.one_ref, bf16[256,256]{1,0:T(8,128)(2,1)S(1)} %collective-permute-done.13.two_ref), custom_call_target="tpu_custom_call" | custom-call | flops 30000001024 | tf_op jit(solution)/shard_map/pallas_call | solution.py:447
  36.7 1.6 %collective-permute-done.11.refs_3_ = bf16[272,256]{1,0:T(8,128)(2,1)S(1)} collective-permute-done((bf16[272,256]{1,0:T(8,128)(2,1)S(1)}, bf16[272,256]{1,0:T(8,128)(2,1)S(1)}, u32[]{:S(2)}, u32[]{:S(2)}) %collective-permute-start.11) | collective-permute-done | bytes 139296 | tf_op jit(solution)/shard_map/ppermute | solution.py:367
  38.2 4.5 %collective-permute-done.10.refs_2_ = bf16[272,256]{1,0:T(8,128)(2,1)S(1)} collective-permute-done((bf16[272,256]{1,0:T(8,128)(2,1)S(1)}, bf16[272,256]{1,0:T(8,128)(2,1)S(1)}, u32[]{:S(2)}, u32[]{:S(2)}) %collective-permute-start.10) | collective-permute-done | bytes 139296 | tf_op jit(solution)/shard_map/ppermute | solution.py:367
  42.7 0.0 collective-permute-done.9.refs_1_
  42.7 5.7 %collective-permute-start.14 = (bf16[272,256]{1,0:T(8,128)(2,1)S(1)}, bf16[272,256]{1,0:T(8,128)(2,1)S(1)}, u32[]{:S(2)}, u32[]{:S(2)}) collective-permute-start(bf16[272,256]{1,0:T(8,128)(2,1)S(1)} %add_convert_fusion.refs_0_), channel_id=1, source_target_pairs={{0,1},{1,0},{2,3},{3,2},{4,5},{5,4},{6,7},{7,6},{8,9},{9,8},{10,11... | collective-permute-start | bytes 417800 | tf_op jit(solution)/shard_map/ppermute | solution.py:367
  48.4 0.0 collective-permute-start.15
  48.4 0.5 collective-permute-start.16
  49.0 0.0 collective-permute-start.17
  49.0 1.0 %shard_map.109 = (f32[256,1024]{1,0:T(8,128)}, f32[1024,256]{1,0:T(8,128)}, f32[4,16,256]{2,1,0:T(8,128)S(1)}) custom-call(s32[1]{0:T(128)} %bitcast.1.core, s32[1]{0:T(128)} %bitcast.place, bf16[272,256]{1,0:T(8,128)(2,1)S(1)} %add_convert_fusion.refs_0_, bf16[272,256]{1,0:T(8,128)(2,1)S(1)} %collective-permute-done.9.refs_1_, ...), custom_call_target="tpu_custom_call" | custom-call | tf_op jit(solution)/shard_map/pallas_call | solution.py:455
  50.0 0.0 collective-permute-done.14.refs_0_
  50.0 0.0 collective-permute-done.15.refs_1_
  50.0 0.0 collective-permute-done.16.refs_2_
  50.0 0.3 collective-permute-done.17.refs_3_
  50.3 1.6 %shard_map.110 = (f32[256,1024]{1,0:T(8,128)}, f32[1024,256]{1,0:T(8,128)}, f32[49,256]{1,0:T(8,128)}) custom-call(s32[1]{0:T(128)} %bitcast.1.core, s32[1]{0:T(128)} %bitcast.6.place, bf16[272,256]{1,0:T(8,128)(2,1)S(1)} %collective-permute-done.14.refs_0_, ...), custom_call_target="tpu_custom_call", output_to_operand_aliasing={{0}: (7, {}), {1}: (8, {})} | custom-call | tf_op jit(solution)/shard_map/pallas_call | solution.py:462
Async XLA Ops:
  0.6 4.6 %collective-permute-start = (bf16[256,256]{1,0:T(8,128)(2,1)}, bf16[256,256]{1,0:T(8,128)(2,1)S(1)}, u32[]{:S(2)}, u32[]{:S(2)}) collective-permute-start(bf16[256,256]{1,0:T(8,128)(2,1)} %bitcast.8), channel_id=1, source_target_pairs={{0,4},{4,0},{8,12},{12,8},{16,20},{20,16},{24,28},{28,24},{1,5},{5... | collective-permute-start | bytes 393224 | tf_op jit(solution)/shard_map/ppermute | solution.py:354
  1.9 5.0 %collective-permute-start.1 = (bf16[256,256]{1,0:T(8,128)(2,1)}, bf16[256,256]{1,0:T(8,128)(2,1)S(1)}, u32[]{:S(2)}, u32[]{:S(2)}) collective-permute-start(bf16[256,256]{1,0:T(8,128)(2,1)} %bitcast.9), channel_id=1, source_target_pairs={{0,28},{4,8},{8,4},{12,16},{16,12},{20,24},{24,20},{28,0},{1,29},{... | collective-permute-start | bytes 393224 | tf_op jit(solution)/shard_map/ppermute | solution.py:358
  2.1 0.7 %copy-start = (s32[1,4]{1,0:T(1,128)S(1)}, s32[1,4]{1,0:T(1,128)}, u32[]{:S(2)}) copy-start(s32[1,4]{1,0:T(1,128)} %neighbour.1) | copy-start | bytes 52
  2.1 0.7 %copy-start.1 = (s32[1,4]{1,0:T(1,128)S(1)}, s32[1,4]{1,0:T(1,128)}, u32[]{:S(2)}) copy-start(s32[1,4]{1,0:T(1,128)} %code.1) | copy-start | bytes 52
  10.8 4.7 %collective-permute-start.2 = (bf16[4,256,256]{2,1,0:T(8,128)(2,1)}, bf16[4,256,256]{2,1,0:T(8,128)(2,1)S(1)}, u32[]{:S(2)}, u32[]{:S(2)}) collective-permute-start(bf16[4,256,256]{2,1,0:T(8,128)(2,1)} %get-tuple-element.42), channel_id=1, source_target_pairs={{0,1},{1,0},{2,3},{3,2},{4,5},{5,4},{6,7},{7,6},{8,9},{9,8},{10,11... | collective-permute-start | bytes 1572872 | tf_op jit(solution)/shard_map/ppermute | solution.py:367
  15.6 5.3 %collective-permute-start.3 = (bf16[272,256]{1,0:T(8,128)(2,1)S(1)}, bf16[272,256]{1,0:T(8,128)(2,1)S(1)}, u32[]{:S(2)}, u32[]{:S(2)}) collective-permute-start(bf16[272,256]{1,0:T(8,128)(2,1)S(1)} %get-tuple-element.46), channel_id=1, source_target_pairs={{0,2},{1,9},{2,0},{3,11},{4,6},{5,13},{6,4},{7,15},{8,10},{9,1},{1... | collective-permute-start | bytes 417800 | tf_op jit(solution)/shard_map/ppermute | solution.py:367
  15.9 8.1 %collective-permute-start.4 = (bf16[272,256]{1,0:T(8,128)(2,1)S(1)}, bf16[272,256]{1,0:T(8,128)(2,1)S(1)}, u32[]{:S(2)}, u32[]{:S(2)}) collective-permute-start(bf16[272,256]{1,0:T(8,128)(2,1)S(1)} %get-tuple-element.47), channel_id=1, source_target_pairs={{0,4},{1,17},{2,6},{3,19},{4,0},{5,21},{6,2},{7,23},{8,12},{9,25},... | collective-permute-start | bytes 417800 | tf_op jit(solution)/shard_map/ppermute | solution.py:367
  16.8 7.2 %collective-permute-start.5 = (bf16[272,256]{1,0:T(8,128)(2,1)S(1)}, bf16[272,256]{1,0:T(8,128)(2,1)S(1)}, u32[]{:S(2)}, u32[]{:S(2)}) collective-permute-start(bf16[272,256]{1,0:T(8,128)(2,1)S(1)} %get-tuple-element.48), channel_id=1, source_target_pairs={{0,6},{1,25},{2,4},{3,27},{4,2},{5,29},{6,0},{7,31},{8,14},{9,17},... | collective-permute-start | bytes 417800 | tf_op jit(solution)/shard_map/ppermute | solution.py:367
  24.1 5.4 %collective-permute-start.8 = (bf16[272,256]{1,0:T(8,128)(2,1)S(1)}, bf16[272,256]{1,0:T(8,128)(2,1)S(1)}, u32[]{:S(2)}, u32[]{:S(2)}) collective-permute-start(bf16[272,256]{1,0:T(8,128)(2,1)S(1)} %add_convert_fusion.1), channel_id=1, source_target_pairs={{0,24},{1,7},{2,26},{3,5},{4,28},{5,3},{6,30},{7,1},{8,16},{9,15},... | collective-permute-start | bytes 417800 | tf_op jit(solution)/shard_map/ppermute | solution.py:367
  26.0 4.5 %collective-permute-start.7 = (bf16[272,256]{1,0:T(8,128)(2,1)S(1)}, bf16[272,256]{1,0:T(8,128)(2,1)S(1)}, u32[]{:S(2)}, u32[]{:S(2)}) collective-permute-start(bf16[272,256]{1,0:T(8,128)(2,1)S(1)} %add_convert_fusion.1), channel_id=1, source_target_pairs={{0,16},{1,5},{2,18},{3,7},{4,20},{5,1},{6,22},{7,3},{8,24},{9,13},... | collective-permute-start | bytes 417800 | tf_op jit(solution)/shard_map/ppermute | solution.py:367
  26.3 4.5 %collective-permute-start.6 = (bf16[272,256]{1,0:T(8,128)(2,1)S(1)}, bf16[272,256]{1,0:T(8,128)(2,1)S(1)}, u32[]{:S(2)}, u32[]{:S(2)}) collective-permute-start(bf16[272,256]{1,0:T(8,128)(2,1)S(1)} %add_convert_fusion.1), channel_id=1, source_target_pairs={{0,8},{1,3},{2,10},{3,1},{4,12},{5,7},{6,14},{7,5},{8,0},{9,11},{1... | collective-permute-start | bytes 417800 | tf_op jit(solution)/shard_map/ppermute | solution.py:367
  26.8 7.6 %collective-permute-start.12 = (bf16[256,256]{1,0:T(8,128)(2,1)S(1)}, bf16[256,256]{1,0:T(8,128)(2,1)S(1)}, u32[]{:S(2)}, u32[]{:S(2)}) collective-permute-start(bf16[256,256]{1,0:T(8,128)(2,1)S(1)} %get-tuple-element.53), channel_id=1, source_target_pairs={{0,4},{4,0},{8,12},{12,8},{16,20},{20,16},{24,28},{28,24},{1,5},{5... | collective-permute-start | bytes 393224 | tf_op jit(solution)/shard_map/ppermute | solution.py:354
  27.7 8.2 %collective-permute-start.13 = (bf16[256,256]{1,0:T(8,128)(2,1)S(1)}, bf16[256,256]{1,0:T(8,128)(2,1)S(1)}, u32[]{:S(2)}, u32[]{:S(2)}) collective-permute-start(bf16[256,256]{1,0:T(8,128)(2,1)S(1)} %get-tuple-element.54), channel_id=1, source_target_pairs={{0,28},{4,8},{8,4},{12,16},{16,12},{20,24},{24,20},{28,0},{1,29},{... | collective-permute-start | bytes 393224 | tf_op jit(solution)/shard_map/ppermute | solution.py:358
  30.8 7.4 %collective-permute-start.11 = (bf16[272,256]{1,0:T(8,128)(2,1)S(1)}, bf16[272,256]{1,0:T(8,128)(2,1)S(1)}, u32[]{:S(2)}, u32[]{:S(2)}) collective-permute-start(bf16[272,256]{1,0:T(8,128)(2,1)S(1)} %add_convert_fusion.refs_0_), channel_id=1, source_target_pairs={{0,6},{1,25},{2,4},{3,27},{4,2},{5,29},{6,0},{7,31},{8,14},{9,17},... | collective-permute-start | bytes 417800 | tf_op jit(solution)/shard_map/ppermute | solution.py:367
  31.8 10.9 %collective-permute-start.10 = (bf16[272,256]{1,0:T(8,128)(2,1)S(1)}, bf16[272,256]{1,0:T(8,128)(2,1)S(1)}, u32[]{:S(2)}, u32[]{:S(2)}) collective-permute-start(bf16[272,256]{1,0:T(8,128)(2,1)S(1)} %add_convert_fusion.refs_0_), channel_id=1, source_target_pairs={{0,4},{1,17},{2,6},{3,19},{4,0},{5,21},{6,2},{7,23},{8,12},{9,25},... | collective-permute-start | bytes 417800 | tf_op jit(solution)/shard_map/ppermute | solution.py:367
  33.7 9.0 %collective-permute-start.9 = (bf16[272,256]{1,0:T(8,128)(2,1)S(1)}, bf16[272,256]{1,0:T(8,128)(2,1)S(1)}, u32[]{:S(2)}, u32[]{:S(2)}) collective-permute-start(bf16[272,256]{1,0:T(8,128)(2,1)S(1)} %add_convert_fusion.refs_0_), channel_id=1, source_target_pairs={{0,2},{1,9},{2,0},{3,11},{4,6},{5,13},{6,4},{7,15},{8,10},{9,1},{1... | collective-permute-start | bytes 417800 | tf_op jit(solution)/shard_map/ppermute | solution.py:367
  42.7 7.2 %collective-permute-start.14 = (bf16[272,256]{1,0:T(8,128)(2,1)S(1)}, bf16[272,256]{1,0:T(8,128)(2,1)S(1)}, u32[]{:S(2)}, u32[]{:S(2)}) collective-permute-start(bf16[272,256]{1,0:T(8,128)(2,1)S(1)} %add_convert_fusion.refs_0_), channel_id=1, source_target_pairs={{0,1},{1,0},{2,3},{3,2},{4,5},{5,4},{6,7},{7,6},{8,9},{9,8},{10,11... | collective-permute-start | bytes 417800 | tf_op jit(solution)/shard_map/ppermute | solution.py:367
  48.4 1.6 %collective-permute-start.15 = (bf16[272,256]{1,0:T(8,128)(2,1)S(1)}, bf16[272,256]{1,0:T(8,128)(2,1)S(1)}, u32[]{:S(2)}, u32[]{:S(2)}) collective-permute-start(bf16[272,256]{1,0:T(8,128)(2,1)S(1)} %collective-permute-done.9.refs_1_), channel_id=1, source_target_pairs={{0,1},{1,0},{2,3},{3,2},{4,5},{5,4},{6,7},{7,6},{8,9},{9,8},{10,11... | collective-permute-start | bytes 417800 | tf_op jit(solution)/shard_map/ppermute | solution.py:367
  48.4 1.6 %collective-permute-start.16 = (bf16[272,256]{1,0:T(8,128)(2,1)S(1)}, bf16[272,256]{1,0:T(8,128)(2,1)S(1)}, u32[]{:S(2)}, u32[]{:S(2)}) collective-permute-start(bf16[272,256]{1,0:T(8,128)(2,1)S(1)} %collective-permute-done.10.refs_2_), channel_id=1, source_target_pairs={{0,1},{1,0},{2,3},{3,2},{4,5},{5,4},{6,7},{7,6},{8,9},{9,8},{10,11... | collective-permute-start | bytes 417800 | tf_op jit(solution)/shard_map/ppermute | solution.py:367
  49.0 1.4 %collective-permute-start.17 = (bf16[272,256]{1,0:T(8,128)(2,1)S(1)}, bf16[272,256]{1,0:T(8,128)(2,1)S(1)}, u32[]{:S(2)}, u32[]{:S(2)}) collective-permute-start(bf16[272,256]{1,0:T(8,128)(2,1)S(1)} %collective-permute-done.11.refs_3_), channel_id=1, source_target_pairs={{0,1},{1,0},{2,3},{3,2},{4,5},{5,4},{6,7},{7,6},{8,9},{9,8},{10,11... | collective-permute-start | bytes 417800 | tf_op jit(solution)/shard_map/ppermute | solution.py:367

commit v3 on v2

--- a/solution.py
+++ b/solution.py
@@ -190,7 +190,7 @@
     )
 
 
-def taps_kernel(frame, dconv_ref, out_ref):
+def tap_sums(frame, dconv_ref, out_ref):
     out_ref[...] = jnp.zeros(out_ref.shape, F32)
     for l in range(C // LANES):
         lanes = slice(l * LANES, (l + 1) * LANES)
@@ -212,7 +212,14 @@
                 )
 
 
-def backward_kernel(onehot, dconv_ref, taps_ref, cot_ref, own_ref, one_ref, two_ref, shifted, rim):
+def backward_kernel(
+    frame, onehot, dconv_ref, taps_ref, cot_hbm, _, sums_ref, own_ref, one_ref, two_ref, keep_ref,
+    shifted, rim, cot_ref, sem,
+):
+    del keep_ref
+    copy = pltpu.make_async_copy(cot_hbm, cot_ref, sem)
+    copy.start()
+    tap_sums(frame, dconv_ref, sums_ref)
     residues = (2, 4, 6, 0)
     pad = jnp.zeros((ROWS, 8, LANES), F32)
     for l in range(C // LANES):
@@ -263,9 +270,10 @@
             n = block.shape[0] * block.shape[1]
             rim[at : at + n, lanes] = block.reshape(n, LANES).astype(BF16)
             at += n
-        own_ref[:, lanes] = inner.reshape(N * N, LANES) + cot_ref[:, lanes].astype(F32)
+        own_ref[:, lanes] = inner.reshape(N * N, LANES)
+    copy.wait()
     cells = rim[...]
-    own_ref[...] += dot(onehot[:, : N * N], cells, 0, 0)
+    own_ref[...] += cot_ref[...].astype(F32) + dot(onehot[:, : N * N], cells, 0, 0)
     one_ref[...] = dot(onehot[:, N * N : 2 * N * N], cells, 0, 0).astype(BF16)
     two_ref[...] = dot(onehot[:, 2 * N * N :], cells, 0, 0).astype(BF16)
 
@@ -277,48 +285,42 @@
         out[C:, :] = taps_ref[j].astype(out.dtype)
 
 
-def store_blocks(scale, to_in, place, blocks, in_hbm, out_hbm, stage, sems):
+def store_kernel(scale, picks, given, last, core, mine_at, theirs_at, *refs):
+    count = len(picks) + (2 * GROUP if last else 0)
+    blocks, taps = refs[: len(picks)], refs[len(picks) : count]
+    refs = refs[count + given :]
+    in_hbm, out_hbm = refs[:2]
     copies = []
-    for d in range(GROUP):
-        stage[d] = blocks[d][:C, :].astype(F32) * scale
-        at = pl.ds(pl.multiple_of((place ^ d) * C, C), C)
-        into_in = pltpu.make_async_copy(stage.at[d], in_hbm.at[:, at], sems.at[d])
-        into_out = pltpu.make_async_copy(stage.at[d], out_hbm.at[at, :], sems.at[d])
+    if last:
+        kernel_hbm, stage, sems, rows, kernel_ref = refs[2:]
+        for n, block in enumerate(taps):
+            at = (mine_at if n < GROUP else theirs_at)[0] ^ (n % GROUP)
+            rows[n // GROUP, at] = block[C:, :].astype(F32)
+        for j in range(GROUP):
+            n = min(EXTRA, TAPS * TAPS - j * EXTRA)
+            kernel_ref[j * EXTRA : j * EXTRA + n, :] = (rows[0, j, :n, :] + rows[1, j, :n, :]) * scale
+        copies.append(pltpu.make_async_copy(kernel_ref, kernel_hbm, sems.at[GROUP]))
+        copies[0].start()
+    else:
+        stage, sems = refs[2:]
+    first = core[0] == 0
+    pairs = []
+    for n, (half, d) in enumerate(picks):
+        stage[n] = blocks[n][:C, :].astype(F32) * scale
+        at = pl.ds(pl.multiple_of(((theirs_at if half else mine_at)[0] ^ d) * C, C), C)
+        into_in = pltpu.make_async_copy(stage.at[n], in_hbm.at[:, at], sems.at[n])
+        into_out = pltpu.make_async_copy(stage.at[n], out_hbm.at[at, :], sems.at[n])
+        to_in = jnp.logical_not(first) if half else first
         pl.when(to_in)(into_in.start)
         pl.when(jnp.logical_not(to_in))(into_out.start)
-        copies.append((into_in, into_out))
-    return copies
-
-
-def wait_blocks(to_in, copies):
-    for into_in, into_out in copies:
+        pairs.append((to_in, into_in, into_out))
+    for copy in copies:
+        copy.wait()
+    for to_in, into_in, into_out in pairs:
         pl.when(to_in)(into_in.wait)
         pl.when(jnp.logical_not(to_in))(into_out.wait)
 
 
-def finish_mine_kernel(scale, core, place, *refs):
-    blocks = refs[:GROUP]
-    in_hbm, out_hbm, rows, stage, sems = refs[GROUP:]
-    to_in = core[0] == 0
-    copies = store_blocks(scale, to_in, place[0], blocks, in_hbm, out_hbm, stage, sems)
-    for d in range(GROUP):
-        rows[place[0] ^ d] = blocks[d][C:, :].astype(F32)
-    wait_blocks(to_in, copies)
-
-
-def finish_theirs_kernel(scale, core, place, *refs):
-    blocks, (mine_ref, _, _) = refs[:GROUP], refs[GROUP : GROUP + 3]
-    in_hbm, out_hbm, kernel_ref, rows, stage, sems = refs[GROUP + 3 :]
-    to_in = core[0] != 0
-    copies = store_blocks(scale, to_in, place[0], blocks, in_hbm, out_hbm, stage, sems)
-    for d in range(GROUP):
-        rows[place[0] ^ d] = blocks[d][C:, :].astype(F32)
-    for j in range(GROUP):
-        n = min(EXTRA, TAPS * TAPS - j * EXTRA)
-        kernel_ref[j * EXTRA : j * EXTRA + n, :] = (mine_ref[j, :n, :] + rows[j, :n, :]) * scale
-    wait_blocks(to_in, copies)
-
-
 def join_kernel(own_ref, one_ref, two_ref, out_ref):
     out_ref[...] = (own_ref[...] + one_ref[...].astype(F32) + two_ref[...].astype(F32)).astype(BF16)
 
@@ -327,7 +329,7 @@
     return pltpu.with_memory_space_constraint(x, pltpu.HBM)
 
 
-def call(kernel, outs, scratch=(), specs=(), flops=0, aliases={}, out_specs=None, vmem=16):
+def call(kernel, outs, scratch=(), specs=(), flops=700_000_000, aliases={}, out_specs=None, vmem=16):
     return pl.pallas_call(
         kernel,
         out_shape=outs,
@@ -336,7 +338,7 @@
         scratch_shapes=scratch,
         input_output_aliases=aliases,
         compiler_params=pltpu.CompilerParams(vmem_limit_bytes=vmem * 1024 * 1024),
-        cost_estimate=pl.CostEstimate(flops=flops, bytes_accessed=0, transcendentals=0),
+        cost_estimate=pl.CostEstimate(flops=flops, bytes_accessed=4_000_000, transcendentals=0),
     )
 
 
@@ -377,6 +379,7 @@
     combos = [[p[0], p[1], p[0] + p[1]] for p in pairs]
 
     own = features.reshape(N * N, C)
+    cot_rows = cotangent.reshape(N * N, C)
     one = one_over(own)
     two = two_over(own)
 
@@ -399,7 +402,7 @@
         [SMEM] * 3 + [HBM] * 5,
     )(
         tile_neighbour, edge_code, position.reshape(1).astype(jnp.int32),
-        *map(in_hbm, (own, cotangent.reshape(N * N, C), kernel, weight_in, weight_out)),
+        *map(in_hbm, (own, cot_rows, kernel, weight_in, weight_out)),
     )
     frame_one = call(
         one_kernel, frame, (), [VMEM] * 3, aliases={0: 0}
@@ -410,29 +413,37 @@
         (half, half, pltpu.VMEM((N * N, C), F32), frame),
         [pltpu.VMEM((N * N, C), F32)],
         [SMEM] + [VMEM] * 7,
+        flops=1_000_000_000,
         aliases={1: 3},
     )(core, frame_one, two, onehot, d_hidden, cot, taps, w_in)
     got = swap(send, 1, 1)
-    part_taps = call(
-        taps_kernel, pltpu.VMEM((GROUP, EXTRA, C), F32), (), [VMEM] * 2
-    )(frame_two, dconv)
+    part_taps, grad_own, grad_one, grad_two, keep = call(
+        backward_kernel,
+        (
+            pltpu.VMEM((GROUP, EXTRA, C), F32),
+            pltpu.VMEM((N * N, C), F32),
+            pltpu.VMEM((N * N, C), BF16),
+            pltpu.VMEM((N * N, C), BF16),
+            half,
+        ),
+        [
+            pltpu.VMEM((2, 4, ROWS, 40, LANES), F32),
+            pltpu.VMEM((SIDE_CELLS, C), BF16),
+            pltpu.VMEM((N * N, C), BF16),
+            pltpu.SemaphoreType.DMA,
+        ],
+        [VMEM] * 4 + [HBM, VMEM],
+        aliases={5: 4},
+    )(frame_two, onehot, dconv, taps, in_hbm(cot_rows), keep)
 
     block = struct((C + EXTRA, C), BF16)
     pieces = call(
         spread_kernel, (block,) * GROUP, (), [SMEM] + [VMEM] * 3
     )(mine_at, keep, got, part_taps)
     total = pieces[0].astype(F32)
-    for piece, even, odd in zip(pieces[1:], *combos):
+    for piece, even, odd in reversed(list(zip(pieces[1:], *combos))):
         total = total + swap(piece, even, odd).astype(F32)
     total = total.astype(BF16)
-
-    grad_own, grad_one, grad_two = call(
-        backward_kernel,
-        (pltpu.VMEM((N * N, C), F32), pltpu.VMEM((N * N, C), BF16), pltpu.VMEM((N * N, C), BF16)),
-        [pltpu.VMEM((2, 4, ROWS, 40, LANES), F32), pltpu.VMEM((28 * N, C), BF16)],
-        [VMEM] * 4,
-    )(onehot, dconv, taps, cot)
-    total, grad_one, grad_two = lax.optimization_barrier((total, grad_one, grad_two))
 
     back_two = two_over(grad_two)
     back_one = one_over(grad_one)
@@ -443,30 +454,35 @@
             third = swap(total, sum(even), sum(odd))
             summed = summed + (got[1].astype(F32) + third.astype(F32))
         total = summed.astype(BF16)
-    mine = [total] + [swap(total, even, odd) for even, odd in zip(*combos)]
     grad_features = call(
         join_kernel, struct((N * N, C), BF16), (), [VMEM] * 3, flops=JOIN_COST
     )(grad_own, back_one, back_two)
-    mine, grad_features = lax.optimization_barrier((mine, grad_features))
+    total, grad_features = lax.optimization_barrier((total, grad_features))
+    mine = [total] + [swap(total, even, odd) for even, odd in zip(*combos)]
     theirs = [swap(x, 1, 1) for x in mine]
     grads = (struct((C, HID), F32), struct((HID, C), F32))
-    rows = struct((GROUP, EXTRA, C), F32)
-    stage = [pltpu.VMEM((GROUP, C, C), F32), pltpu.SemaphoreType.DMA((GROUP,))]
-    grad_in, grad_out, rows_mine = call(
-        functools.partial(finish_mine_kernel, scale),
-        (*grads, rows),
-        stage,
-        [SMEM] * 2 + [VMEM] * GROUP,
-        out_specs=(ANY, ANY, VMEM),
-    )(core, mine_at, *mine)
-    grad_in, grad_out, grad_kernel = call(
-        functools.partial(finish_theirs_kernel, scale),
-        (*grads, struct((TAPS * TAPS, C), F32)),
-        [pltpu.VMEM((GROUP, EXTRA, C), F32)] + stage,
-        [SMEM] * 2 + [VMEM] * (GROUP + 1) + [ANY] * 2,
-        out_specs=(ANY, ANY, VMEM),
-        aliases={GROUP + 3: 0, GROUP + 4: 1},
-    )(core, theirs_at, *theirs, rows_mine, grad_in, grad_out)
+    stage = [pltpu.VMEM((GROUP, C, C), F32), pltpu.SemaphoreType.DMA((GROUP + 1,))]
+    halves = (mine, theirs)
+
+    def store(picks, given, last=False):
+        blocks = [halves[half][d] for half, d in picks] + ([*mine, *theirs] if last else [])
+        count = 3 + len(blocks)
+        return call(
+            functools.partial(store_kernel, scale, picks, len(given), last),
+            (*grads, struct((TAPS * TAPS, C), F32)) if last else grads,
+            stage
+            + (
+                [pltpu.VMEM((2, GROUP, EXTRA, C), F32), pltpu.VMEM((TAPS * TAPS, C), F32)]
+                if last
+                else []
+            ),
+            [SMEM] * 3 + [VMEM] * len(blocks) + [ANY] * len(given),
+            out_specs=(ANY,) * (3 if last else 2),
+            aliases={count + n: n for n in range(len(given))},
+        )(core, mine_at, theirs_at, *blocks, *given)
+
+    given = store([(0, d) for d in range(GROUP)], ())
+    grad_in, grad_out, grad_kernel = store([(1, d) for d in range(GROUP)], given, True)
     return grad_features.reshape(features.shape), grad_kernel, grad_in, grad_out
 
 

time: 52.1 us -> 47 us (0.902)
  the two profiles are of different devices: /device:TPU:25 before, /device:TPU:0 now
where the time goes in v3:
time: 47 us; the launch traced here: 46.9 us
  starting transfers between devices  24.2 us (51%)
  Pallas kernels  10.8 us (23%)
  waiting for transfers between devices  10.2 us (22%)
  between operations  0.79 us (2%)
  local copies, waits for them, and re-layouts  0.67 us (1%)
    ppermute x14, starting transfers between devices, swap(): lax.ppermute(x, both, [(i, i ^ (odd if i % 2 else even)) for i in range(d...  13.4 us
    ppermute x14, waiting for transfers between devices, swap(): lax.ppermute(x, both, [(i, i ^ (odd if i % 2 else even)) for i in range(d...  8.8 us
    ppermute x2, starting transfers between devices, two_over(): return lax.ppermute(x, 'tile', moves)  7.14 us
    ppermute x2, starting transfers between devices, one_over(): return lax.ppermute(x, 'tile', [(i, i ^ 1) for i in range(owners)])  3.62 us
    pallas_call x1, Pallas kernels, body(): call(forward_kernel, (half, half, pltpu.VMEM((N * N, C), F32), frame), [p...  3.22 us
    pallas_call x1, Pallas kernels, body(): call(backward_kernel, (pltpu.VMEM((GROUP, EXTRA, C), F32), pltpu.VMEM((N...  2.29 us
    pallas_call x1, Pallas kernels, body(): call(functools.partial(prepare_kernel, owners), (pltpu.VMEM((SIDE_CELLS,...  2.2 us
    pallas_call x2, Pallas kernels, store(): call(functools.partial(store_kernel, scale, picks, len(given), last), (*g...  2.08 us
  transfers between devices with their start and end apart: 18, of which 8 were waited for; matrix products, arithmetic and copies ran while one was open for 0% of the time, Pallas kernels for 14%

profile of v3, /device:TPU:0, one launch (start us, length us, event | category | flops | bytes accessed | tf_op | source)
XLA Modules:
  0.0 46.9 jit_solution(1397578160829084277)
XLA Ops:
  0.6 3.0 %collective-permute-start = (bf16[256,256]{1,0:T(8,128)(2,1)}, bf16[256,256]{1,0:T(8,128)(2,1)S(1)}, u32[]{:S(2)}, u32[]{:S(2)}) collective-permute-start(bf16[256,256]{1,0:T(8,128)(2,1)} %bitcast.7), channel_id=1, source_target_pairs={{0,4},{4,0},{8,12},{12,8},{16,20},{20,16},{24,28},{28,24},{1,5},{5... | collective-permute-start | bytes 393224 | tf_op jit(solution)/shard_map/ppermute | solution.py:356
  3.6 3.6 %collective-permute-start.1 = (bf16[256,256]{1,0:T(8,128)(2,1)}, bf16[256,256]{1,0:T(8,128)(2,1)S(1)}, u32[]{:S(2)}, u32[]{:S(2)}) collective-permute-start(bf16[256,256]{1,0:T(8,128)(2,1)} %bitcast.8), channel_id=1, source_target_pairs={{0,28},{4,8},{8,4},{12,16},{16,12},{20,24},{24,20},{28,0},{1,29},{... | collective-permute-start | bytes 393224 | tf_op jit(solution)/shard_map/ppermute | solution.py:360
  7.2 0.0 copy-start
  7.2 0.0 copy-start.1
  7.2 0.7 %copy-done = s32[1,4]{1,0:T(1,128)S(1)} copy-done((s32[1,4]{1,0:T(1,128)S(1)}, s32[1,4]{1,0:T(1,128)}, u32[]{:S(2)}) %copy-start) | copy-done | bytes 40
  7.9 0.0 copy-done.1
  7.9 2.2 %shard_map.102 = (bf16[448,768]{1,0:T(8,128)(2,1)S(1)}, f32[2,28,32,128]{3,2,1,0:T(8,128)S(1)}, f32[256,1024]{1,0:T(8,128)S(1)}, bf16[256,256]{1,0:T(8,128)(2,1)...) custom-call(s32[1,4]{1,0:T(1,128)S(1)} %copy-done, s32[1,4]{1,0:T(1,128)S(1)} %copy-done.1, ...), custom_call_target="tpu_custom_call" | custom-call | flops 700000000 | bytes 4000000 | tf_op jit(solution)/shard_map/pallas_call | solution.py:387
  10.1 0.0 collective-permute-done.one_ref
  10.1 0.2 shard_map.103.start_ref
  10.3 1.2 %collective-permute-done.1.two_ref = bf16[256,256]{1,0:T(8,128)(2,1)S(1)} collective-permute-done((bf16[256,256]{1,0:T(8,128)(2,1)}, bf16[256,256]{1,0:T(8,128)(2,1)S(1)}, u32[]{:S(2)}, u32[]{:S(2)}) %collective-permute-start.1) | collective-permute-done | bytes 131104 | tf_op jit(solution)/shard_map/ppermute | solution.py:360
  11.5 3.2 %shard_map.104 = (bf16[4,256,256]{2,1,0:T(8,128)(2,1)S(1)}, bf16[4,256,256]{2,1,0:T(8,128)(2,1)S(1)}, f32[256,256]{1,0:T(8,128)S(1)}, f32[2,28,32,128]{3,2,1,0:T(8,128)S(1)}) custom-call(s32[1]{0:T(128)} %bitcast.1.core, f32[2,28,32,128]{3,2,1,0:T(8,128)S(1)} %shard_map.103.start_ref, ...), custom_call_target="tpu_custom_call", output_to_operand_aliasing={{3}: (1, {})} | custom-call | flops 1000000000 | bytes 4000000 | tf_op jit(solution)/shard_map/pallas_call | solution.py:411
  14.7 0.1 collective-permute-start.2
  14.8 2.3 %shard_map.105 = (f32[4,16,256]{2,1,0:T(8,128)S(1)}, f32[256,256]{1,0:T(8,128)S(1)}, bf16[256,256]{1,0:T(8,128)(2,1)S(1)}, bf16[256,256]{1,0:T(8,128)(2,1)S(1)}, bf16[4,256,256]{2,1,0:T(8,128)(2,1)S(1)}) custom-call(f32[2,28,32,128]{3,2,1,0:T(8,128)S(1)} %get-tuple-element.36.frame, ...), custom_call_target="tpu_custom_call", output_to_operand_aliasing={{4}: (5, {})} | custom-call | flops 700000000 | bytes 4000000 | tf_op jit(solution)/shard_map/pallas_call | solution.py:420
  17.1 0.0 collective-permute-done.2.got_ref
  17.2 0.1 shard_map.106
  17.3 1.6 %collective-permute-start.3 = (bf16[272,256]{1,0:T(8,128)(2,1)S(1)}, bf16[272,256]{1,0:T(8,128)(2,1)S(1)}, u32[]{:S(2)}, u32[]{:S(2)}) collective-permute-start(bf16[272,256]{1,0:T(8,128)(2,1)S(1)} %get-tuple-element.43), channel_id=1, source_target_pairs={{0,6},{1,25},{2,4},{3,27},{4,2},{5,29},{6,0},{7,31},{8,14},{9,17},... | collective-permute-start | bytes 417800 | tf_op jit(solution)/shard_map/ppermute | solution.py:369
  18.9 1.4 %collective-permute-start.4 = (bf16[272,256]{1,0:T(8,128)(2,1)S(1)}, bf16[272,256]{1,0:T(8,128)(2,1)S(1)}, u32[]{:S(2)}, u32[]{:S(2)}) collective-permute-start(bf16[272,256]{1,0:T(8,128)(2,1)S(1)} %get-tuple-element.44), channel_id=1, source_target_pairs={{0,4},{1,17},{2,6},{3,19},{4,0},{5,21},{6,2},{7,23},{8,12},{9,25},... | collective-permute-start | bytes 417800 | tf_op jit(solution)/shard_map/ppermute | solution.py:369
  20.3 0.5 %collective-permute-start.5 = (bf16[272,256]{1,0:T(8,128)(2,1)S(1)}, bf16[272,256]{1,0:T(8,128)(2,1)S(1)}, u32[]{:S(2)}, u32[]{:S(2)}) collective-permute-start(bf16[272,256]{1,0:T(8,128)(2,1)S(1)} %get-tuple-element.45), channel_id=1, source_target_pairs={{0,2},{1,9},{2,0},{3,11},{4,6},{5,13},{6,4},{7,15},{8,10},{9,1},{1... | collective-permute-start | bytes 417800 | tf_op jit(solution)/shard_map/ppermute | solution.py:369
  20.8 0.6 %collective-permute-start.9 = (bf16[256,256]{1,0:T(8,128)(2,1)S(1)}, bf16[256,256]{1,0:T(8,128)(2,1)S(1)}, u32[]{:S(2)}, u32[]{:S(2)}) collective-permute-start(bf16[256,256]{1,0:T(8,128)(2,1)S(1)} %get-tuple-element.47), channel_id=1, source_target_pairs={{0,4},{4,0},{8,12},{12,8},{16,20},{20,16},{24,28},{28,24},{1,5},{5... | collective-permute-start | bytes 393224 | tf_op jit(solution)/shard_map/ppermute | solution.py:356
  21.5 3.6 %collective-permute-start.10 = (bf16[256,256]{1,0:T(8,128)(2,1)S(1)}, bf16[256,256]{1,0:T(8,128)(2,1)S(1)}, u32[]{:S(2)}, u32[]{:S(2)}) collective-permute-start(bf16[256,256]{1,0:T(8,128)(2,1)S(1)} %get-tuple-element.48), channel_id=1, source_target_pairs={{0,28},{4,8},{8,4},{12,16},{16,12},{20,24},{24,20},{28,0},{1,29},{... | collective-permute-start | bytes 393224 | tf_op jit(solution)/shard_map/ppermute | solution.py:360
  25.0 0.0 collective-permute-done.3
  25.0 0.7 %collective-permute-done.4 = bf16[272,256]{1,0:T(8,128)(2,1)S(1)} collective-permute-done((bf16[272,256]{1,0:T(8,128)(2,1)S(1)}, bf16[272,256]{1,0:T(8,128)(2,1)S(1)}, u32[]{:S(2)}, u32[]{:S(2)}) %collective-permute-start.4) | collective-permute-done | bytes 139296 | tf_op jit(solution)/shard_map/ppermute | solution.py:369
  25.7 0.0 collective-permute-done.5
  25.7 0.1 add_convert_fusion.1
  25.8 2.8 %collective-permute-start.8 = (bf16[272,256]{1,0:T(8,128)(2,1)S(1)}, bf16[272,256]{1,0:T(8,128)(2,1)S(1)}, u32[]{:S(2)}, u32[]{:S(2)}) collective-permute-start(bf16[272,256]{1,0:T(8,128)(2,1)S(1)} %add_convert_fusion.1), channel_id=1, source_target_pairs={{0,24},{1,7},{2,26},{3,5},{4,28},{5,3},{6,30},{7,1},{8,16},{9,15},... | collective-permute-start | bytes 417800 | tf_op jit(solution)/shard_map/ppermute | solution.py:369
  28.6 0.0 collective-permute-start.7
  28.6 1.7 %collective-permute-start.6 = (bf16[272,256]{1,0:T(8,128)(2,1)S(1)}, bf16[272,256]{1,0:T(8,128)(2,1)S(1)}, u32[]{:S(2)}, u32[]{:S(2)}) collective-permute-start(bf16[272,256]{1,0:T(8,128)(2,1)S(1)} %add_convert_fusion.1), channel_id=1, source_target_pairs={{0,8},{1,3},{2,10},{3,1},{4,12},{5,7},{6,14},{7,5},{8,0},{9,11},{1... | collective-permute-start | bytes 417800 | tf_op jit(solution)/shard_map/ppermute | solution.py:369
  30.2 0.2 collective-permute-done.9.one_ref
  30.5 0.0 collective-permute-done.10.two_ref
  30.5 0.7 %shard_map.107 = bf16[256,256]{1,0:T(8,128)(2,1)} custom-call(f32[256,256]{1,0:T(8,128)S(1)} %get-tuple-element.46.own_ref, bf16[256,256]{1,0:T(8,128)(2,1)S(1)} %collective-permute-done.9.one_ref, bf16[256,256]{1,0:T(8,128)(2,1)S(1)} %collective-permute-done.10.two_ref), custom_call_target="tpu_custom_call" | custom-call | flops 30000001024 | bytes 4000000 | tf_op jit(solution)/shard_map/pallas_call | solution.py:457
  31.2 1.6 %collective-permute-done.8 = bf16[272,256]{1,0:T(8,128)(2,1)S(1)} collective-permute-done((bf16[272,256]{1,0:T(8,128)(2,1)S(1)}, bf16[272,256]{1,0:T(8,128)(2,1)S(1)}, u32[]{:S(2)}, u32[]{:S(2)}) %collective-permute-start.8) | collective-permute-done | bytes 139296 | tf_op jit(solution)/shard_map/ppermute | solution.py:369
  32.8 2.9 %collective-permute-done.7 = bf16[272,256]{1,0:T(8,128)(2,1)S(1)} collective-permute-done((bf16[272,256]{1,0:T(8,128)(2,1)S(1)}, bf16[272,256]{1,0:T(8,128)(2,1)S(1)}, u32[]{:S(2)}, u32[]{:S(2)}) %collective-permute-start.7) | collective-permute-done | bytes 139296 | tf_op jit(solution)/shard_map/ppermute | solution.py:369
  35.7 0.0 collective-permute-done.6
  35.7 0.1 add_convert_fusion.refs_0_.refs_4_
  35.8 2.1 %collective-permute-start.16 = (bf16[272,256]{1,0:T(8,128)(2,1)S(1)}, bf16[272,256]{1,0:T(8,128)(2,1)S(1)}, u32[]{:S(2)}, u32[]{:S(2)}) collective-permute-start(bf16[272,256]{1,0:T(8,128)(2,1)S(1)} %add_convert_fusion.refs_0_.refs_4_), channel_id=1, source_target_pairs={{0,6},{1,25},{2,4},{3,27},{4,2},{5,29},{6,0},{7,31},{8,14},{9,17},... | collective-permute-start | bytes 417800 | tf_op jit(solution)/shard_map/ppermute | solution.py:369
  37.9 0.8 %collective-permute-start.14 = (bf16[272,256]{1,0:T(8,128)(2,1)S(1)}, bf16[272,256]{1,0:T(8,128)(2,1)S(1)}, u32[]{:S(2)}, u32[]{:S(2)}) collective-permute-start(bf16[272,256]{1,0:T(8,128)(2,1)S(1)} %add_convert_fusion.refs_0_.refs_4_), channel_id=1, source_target_pairs={{0,4},{1,17},{2,6},{3,19},{4,0},{5,21},{6,2},{7,23},{8,12},{9,25},... | collective-permute-start | bytes 417800 | tf_op jit(solution)/shard_map/ppermute | solution.py:369
  38.6 1.1 %collective-permute-start.12 = (bf16[272,256]{1,0:T(8,128)(2,1)S(1)}, bf16[272,256]{1,0:T(8,128)(2,1)S(1)}, u32[]{:S(2)}, u32[]{:S(2)}) collective-permute-start(bf16[272,256]{1,0:T(8,128)(2,1)S(1)} %add_convert_fusion.refs_0_.refs_4_), channel_id=1, source_target_pairs={{0,2},{1,9},{2,0},{3,11},{4,6},{5,13},{6,4},{7,15},{8,10},{9,1},{1... | collective-permute-start | bytes 417800 | tf_op jit(solution)/shard_map/ppermute | solution.py:369
  39.8 0.0 collective-permute-start.11
  39.8 2.0 %collective-permute-done.16.refs_3_.refs_7_ = bf16[272,256]{1,0:T(8,128)(2,1)S(1)} collective-permute-done((bf16[272,256]{1,0:T(8,128)(2,1)S(1)}, bf16[272,256]{1,0:T(8,128)(2,1)S(1)}, u32[]{:S(2)}, u32[]{:S(2)}) %collective-permute-start.16) | collective-permute-done | bytes 139296 | tf_op jit(solution)/shard_map/ppermute | solution.py:369
  41.8 0.1 collective-permute-start.17
  41.9 1.3 %collective-permute-done.14.refs_2_.refs_6_ = bf16[272,256]{1,0:T(8,128)(2,1)S(1)} collective-permute-done((bf16[272,256]{1,0:T(8,128)(2,1)S(1)}, bf16[272,256]{1,0:T(8,128)(2,1)S(1)}, u32[]{:S(2)}, u32[]{:S(2)}) %collective-permute-start.14) | collective-permute-done | bytes 139296 | tf_op jit(solution)/shard_map/ppermute | solution.py:369
  43.2 1.3 %collective-permute-start.15 = (bf16[272,256]{1,0:T(8,128)(2,1)S(1)}, bf16[272,256]{1,0:T(8,128)(2,1)S(1)}, u32[]{:S(2)}, u32[]{:S(2)}) collective-permute-start(bf16[272,256]{1,0:T(8,128)(2,1)S(1)} %collective-permute-done.14.refs_2_.refs_6_), channel_id=1, source_target_pairs={{0,1},{1,0},{2,3},{3,2},{4,5},{5,4},{6,7},{7,6},{8,9},{9,8},{10,11... | collective-permute-start | bytes 417800 | tf_op jit(solution)/shard_map/ppermute | solution.py:369
  44.4 0.0 collective-permute-done.12.refs_1_.refs_5_
  44.4 0.0 collective-permute-start.13
  44.4 1.0 %shard_map.108 = (f32[256,1024]{1,0:T(8,128)}, f32[1024,256]{1,0:T(8,128)}) custom-call(s32[1]{0:T(128)} %bitcast.1.core, s32[1]{0:T(128)} %bitcast.place.mine_at, s32[1]{0:T(128)} %bitcast.6.theirs_at, bf16[272,256]{1,0:T(8,128)(2,1)S(1)} %add_convert_fusion.refs_0_.refs_4_, bf16[272,256]{1,0:T(8,128)(2,1)S(1)} %collective-permute-done.12.refs_1_.refs_5_, ...), custom_call_target="tpu_custom_call" | custom-call | flops 700000000 | bytes 4000000 | tf_op jit(solution)/shard_map/pallas_call | solution.py:470
  45.5 0.0 collective-permute-done.11.refs_0_.refs_8_
  45.5 0.0 collective-permute-done.17.refs_3_.refs_11_
  45.5 0.0 collective-permute-done.15.refs_2_.refs_10_
  45.5 0.3 collective-permute-done.13.refs_1_.refs_9_
  45.8 1.1 %shard_map.109 = (f32[256,1024]{1,0:T(8,128)}, f32[1024,256]{1,0:T(8,128)}, f32[49,256]{1,0:T(8,128)}) custom-call(s32[1]{0:T(128)} %bitcast.1.core, s32[1]{0:T(128)} %bitcast.place.mine_at, s32[1]{0:T(128)} %bitcast.6.theirs_at, bf16[272,256]{1,0:T(8,128)(2,1)S(1)} %collective-permute-done.11.refs_0_.refs_8_, ...), custom_call_target="tpu_custom_call", output_to_operand_aliasing={{0}: (15, {}), {1}: (16, {})} | custom-call | flops 700000000 | bytes 4000000 | tf_op jit(solution)/shard_map/pallas_call | solution.py:470
Async XLA Ops:
  0.6 9.5 %collective-permute-start = (bf16[256,256]{1,0:T(8,128)(2,1)}, bf16[256,256]{1,0:T(8,128)(2,1)S(1)}, u32[]{:S(2)}, u32[]{:S(2)}) collective-permute-start(bf16[256,256]{1,0:T(8,128)(2,1)} %bitcast.7), channel_id=1, source_target_pairs={{0,4},{4,0},{8,12},{12,8},{16,20},{20,16},{24,28},{28,24},{1,5},{5... | collective-permute-start | bytes 393224 | tf_op jit(solution)/shard_map/ppermute | solution.py:356
  3.6 7.9 %collective-permute-start.1 = (bf16[256,256]{1,0:T(8,128)(2,1)}, bf16[256,256]{1,0:T(8,128)(2,1)S(1)}, u32[]{:S(2)}, u32[]{:S(2)}) collective-permute-start(bf16[256,256]{1,0:T(8,128)(2,1)} %bitcast.8), channel_id=1, source_target_pairs={{0,28},{4,8},{8,4},{12,16},{16,12},{20,24},{24,20},{28,0},{1,29},{... | collective-permute-start | bytes 393224 | tf_op jit(solution)/shard_map/ppermute | solution.py:360
  7.2 0.7 %copy-start = (s32[1,4]{1,0:T(1,128)S(1)}, s32[1,4]{1,0:T(1,128)}, u32[]{:S(2)}) copy-start(s32[1,4]{1,0:T(1,128)} %neighbour.1) | copy-start | bytes 52
  7.2 0.7 %copy-start.1 = (s32[1,4]{1,0:T(1,128)S(1)}, s32[1,4]{1,0:T(1,128)}, u32[]{:S(2)}) copy-start(s32[1,4]{1,0:T(1,128)} %code.1) | copy-start | bytes 52
  14.7 2.4 %collective-permute-start.2 = (bf16[4,256,256]{2,1,0:T(8,128)(2,1)S(1)}, bf16[4,256,256]{2,1,0:T(8,128)(2,1)S(1)}, u32[]{:S(2)}, u32[]{:S(2)}) collective-permute-start(bf16[4,256,256]{2,1,0:T(8,128)(2,1)S(1)} %get-tuple-element.40), channel_id=1, source_target_pairs={{0,1},{1,0},{2,3},{3,2},{4,5},{5,4},{6,7},{7,6},{8,9},{9,8},{10,11... | collective-permute-start | bytes 1572872 | tf_op jit(solution)/shard_map/ppermute | solution.py:369
  17.3 7.7 %collective-permute-start.3 = (bf16[272,256]{1,0:T(8,128)(2,1)S(1)}, bf16[272,256]{1,0:T(8,128)(2,1)S(1)}, u32[]{:S(2)}, u32[]{:S(2)}) collective-permute-start(bf16[272,256]{1,0:T(8,128)(2,1)S(1)} %get-tuple-element.43), channel_id=1, source_target_pairs={{0,6},{1,25},{2,4},{3,27},{4,2},{5,29},{6,0},{7,31},{8,14},{9,17},... | collective-permute-start | bytes 417800 | tf_op jit(solution)/shard_map/ppermute | solution.py:369
  18.9 6.8 %collective-permute-start.4 = (bf16[272,256]{1,0:T(8,128)(2,1)S(1)}, bf16[272,256]{1,0:T(8,128)(2,1)S(1)}, u32[]{:S(2)}, u32[]{:S(2)}) collective-permute-start(bf16[272,256]{1,0:T(8,128)(2,1)S(1)} %get-tuple-element.44), channel_id=1, source_target_pairs={{0,4},{1,17},{2,6},{3,19},{4,0},{5,21},{6,2},{7,23},{8,12},{9,25},... | collective-permute-start | bytes 417800 | tf_op jit(solution)/shard_map/ppermute | solution.py:369
  20.3 5.4 %collective-permute-start.5 = (bf16[272,256]{1,0:T(8,128)(2,1)S(1)}, bf16[272,256]{1,0:T(8,128)(2,1)S(1)}, u32[]{:S(2)}, u32[]{:S(2)}) collective-permute-start(bf16[272,256]{1,0:T(8,128)(2,1)S(1)} %get-tuple-element.45), channel_id=1, source_target_pairs={{0,2},{1,9},{2,0},{3,11},{4,6},{5,13},{6,4},{7,15},{8,10},{9,1},{1... | collective-permute-start | bytes 417800 | tf_op jit(solution)/shard_map/ppermute | solution.py:369
  20.8 9.6 %collective-permute-start.9 = (bf16[256,256]{1,0:T(8,128)(2,1)S(1)}, bf16[256,256]{1,0:T(8,128)(2,1)S(1)}, u32[]{:S(2)}, u32[]{:S(2)}) collective-permute-start(bf16[256,256]{1,0:T(8,128)(2,1)S(1)} %get-tuple-element.47), channel_id=1, source_target_pairs={{0,4},{4,0},{8,12},{12,8},{16,20},{20,16},{24,28},{28,24},{1,5},{5... | collective-permute-start | bytes 393224 | tf_op jit(solution)/shard_map/ppermute | solution.py:356
  21.5 9.0 %collective-permute-start.10 = (bf16[256,256]{1,0:T(8,128)(2,1)S(1)}, bf16[256,256]{1,0:T(8,128)(2,1)S(1)}, u32[]{:S(2)}, u32[]{:S(2)}) collective-permute-start(bf16[256,256]{1,0:T(8,128)(2,1)S(1)} %get-tuple-element.48), channel_id=1, source_target_pairs={{0,28},{4,8},{8,4},{12,16},{16,12},{20,24},{24,20},{28,0},{1,29},{... | collective-permute-start | bytes 393224 | tf_op jit(solution)/shard_map/ppermute | solution.py:360
  25.8 7.0 %collective-permute-start.8 = (bf16[272,256]{1,0:T(8,128)(2,1)S(1)}, bf16[272,256]{1,0:T(8,128)(2,1)S(1)}, u32[]{:S(2)}, u32[]{:S(2)}) collective-permute-start(bf16[272,256]{1,0:T(8,128)(2,1)S(1)} %add_convert_fusion.1), channel_id=1, source_target_pairs={{0,24},{1,7},{2,26},{3,5},{4,28},{5,3},{6,30},{7,1},{8,16},{9,15},... | collective-permute-start | bytes 417800 | tf_op jit(solution)/shard_map/ppermute | solution.py:369
  28.6 7.1 %collective-permute-start.7 = (bf16[272,256]{1,0:T(8,128)(2,1)S(1)}, bf16[272,256]{1,0:T(8,128)(2,1)S(1)}, u32[]{:S(2)}, u32[]{:S(2)}) collective-permute-start(bf16[272,256]{1,0:T(8,128)(2,1)S(1)} %add_convert_fusion.1), channel_id=1, source_target_pairs={{0,16},{1,5},{2,18},{3,7},{4,20},{5,1},{6,22},{7,3},{8,24},{9,13},... | collective-permute-start | bytes 417800 | tf_op jit(solution)/shard_map/ppermute | solution.py:369
  28.6 7.1 %collective-permute-start.6 = (bf16[272,256]{1,0:T(8,128)(2,1)S(1)}, bf16[272,256]{1,0:T(8,128)(2,1)S(1)}, u32[]{:S(2)}, u32[]{:S(2)}) collective-permute-start(bf16[272,256]{1,0:T(8,128)(2,1)S(1)} %add_convert_fusion.1), channel_id=1, source_target_pairs={{0,8},{1,3},{2,10},{3,1},{4,12},{5,7},{6,14},{7,5},{8,0},{9,11},{1... | collective-permute-start | bytes 417800 | tf_op jit(solution)/shard_map/ppermute | solution.py:369
  35.8 6.0 %collective-permute-start.16 = (bf16[272,256]{1,0:T(8,128)(2,1)S(1)}, bf16[272,256]{1,0:T(8,128)(2,1)S(1)}, u32[]{:S(2)}, u32[]{:S(2)}) collective-permute-start(bf16[272,256]{1,0:T(8,128)(2,1)S(1)} %add_convert_fusion.refs_0_.refs_4_), channel_id=1, source_target_pairs={{0,6},{1,25},{2,4},{3,27},{4,2},{5,29},{6,0},{7,31},{8,14},{9,17},... | collective-permute-start | bytes 417800 | tf_op jit(solution)/shard_map/ppermute | solution.py:369
  37.9 5.3 %collective-permute-start.14 = (bf16[272,256]{1,0:T(8,128)(2,1)S(1)}, bf16[272,256]{1,0:T(8,128)(2,1)S(1)}, u32[]{:S(2)}, u32[]{:S(2)}) collective-permute-start(bf16[272,256]{1,0:T(8,128)(2,1)S(1)} %add_convert_fusion.refs_0_.refs_4_), channel_id=1, source_target_pairs={{0,4},{1,17},{2,6},{3,19},{4,0},{5,21},{6,2},{7,23},{8,12},{9,25},... | collective-permute-start | bytes 417800 | tf_op jit(solution)/shard_map/ppermute | solution.py:369
  38.6 5.8 %collective-permute-start.12 = (bf16[272,256]{1,0:T(8,128)(2,1)S(1)}, bf16[272,256]{1,0:T(8,128)(2,1)S(1)}, u32[]{:S(2)}, u32[]{:S(2)}) collective-permute-start(bf16[272,256]{1,0:T(8,128)(2,1)S(1)} %add_convert_fusion.refs_0_.refs_4_), channel_id=1, source_target_pairs={{0,2},{1,9},{2,0},{3,11},{4,6},{5,13},{6,4},{7,15},{8,10},{9,1},{1... | collective-permute-start | bytes 417800 | tf_op jit(solution)/shard_map/ppermute | solution.py:369
  39.8 5.7 %collective-permute-start.11 = (bf16[272,256]{1,0:T(8,128)(2,1)S(1)}, bf16[272,256]{1,0:T(8,128)(2,1)S(1)}, u32[]{:S(2)}, u32[]{:S(2)}) collective-permute-start(bf16[272,256]{1,0:T(8,128)(2,1)S(1)} %add_convert_fusion.refs_0_.refs_4_), channel_id=1, source_target_pairs={{0,1},{1,0},{2,3},{3,2},{4,5},{5,4},{6,7},{7,6},{8,9},{9,8},{10,11... | collective-permute-start | bytes 417800 | tf_op jit(solution)/shard_map/ppermute | solution.py:369
  41.8 3.7 %collective-permute-start.17 = (bf16[272,256]{1,0:T(8,128)(2,1)S(1)}, bf16[272,256]{1,0:T(8,128)(2,1)S(1)}, u32[]{:S(2)}, u32[]{:S(2)}) collective-permute-start(bf16[272,256]{1,0:T(8,128)(2,1)S(1)} %collective-permute-done.16.refs_3_.refs_7_), channel_id=1, source_target_pairs={{0,1},{1,0},{2,3},{3,2},{4,5},{5,4},{6,7},{7,6},{8,9},{9,8},{10,11... | collective-permute-start | bytes 417800 | tf_op jit(solution)/shard_map/ppermute | solution.py:369
  43.2 2.3 %collective-permute-start.15 = (bf16[272,256]{1,0:T(8,128)(2,1)S(1)}, bf16[272,256]{1,0:T(8,128)(2,1)S(1)}, u32[]{:S(2)}, u32[]{:S(2)}) collective-permute-start(bf16[272,256]{1,0:T(8,128)(2,1)S(1)} %collective-permute-done.14.refs_2_.refs_6_), channel_id=1, source_target_pairs={{0,1},{1,0},{2,3},{3,2},{4,5},{5,4},{6,7},{7,6},{8,9},{9,8},{10,11... | collective-permute-start | bytes 417800 | tf_op jit(solution)/shard_map/ppermute | solution.py:369
  44.4 1.4 %collective-permute-start.13 = (bf16[272,256]{1,0:T(8,128)(2,1)S(1)}, bf16[272,256]{1,0:T(8,128)(2,1)S(1)}, u32[]{:S(2)}, u32[]{:S(2)}) collective-permute-start(bf16[272,256]{1,0:T(8,128)(2,1)S(1)} %collective-permute-done.12.refs_1_.refs_5_), channel_id=1, source_target_pairs={{0,1},{1,0},{2,3},{3,2},{4,5},{5,4},{6,7},{7,6},{8,9},{9,8},{10,11... | collective-permute-start | bytes 417800 | tf_op jit(solution)/shard_map/ppermute | solution.py:369

commit v4 on v3

--- a/solution.py
+++ b/solution.py
@@ -19,6 +19,7 @@
 FRAME = 32
 LEFT = 8
 GROUP = 4
+STARTS = ((3, 2, 1), (3, 2, 1), (3, 2, 1))
 JOIN_COST = 30_000_000_000
 EXTRA = 16
 F32 = jnp.float32
@@ -85,28 +86,33 @@
 
 
 def prepare_kernel(
-    owners, neighbour, code, position, own_hbm, cot_hbm, taps_hbm, win_hbm, wout_hbm,
-    onehot, frame, d_hidden, cot_ref, taps_ref, win_ref, own_ref, wout_ref, sems,
+    owners, position, neighbour_hbm, code_hbm, own_hbm, taps_hbm, cot_hbm, wout_hbm, win_hbm,
+    onehot, frame, conv, d_hidden, cot_ref, taps_ref, win_ref,
+    neighbour, code, own_ref, wout_ref, sems,
 ):
     copies = [
         pltpu.make_async_copy(src, dst, sems.at[n])
         for n, (src, dst) in enumerate(
             (
+                (neighbour_hbm, neighbour),
+                (code_hbm, code),
                 (own_hbm, own_ref),
+                (taps_hbm, taps_ref),
                 (cot_hbm, cot_ref),
                 (wout_hbm, wout_ref),
                 (win_hbm, win_ref),
-                (taps_hbm, taps_ref),
             )
         )
     ]
     for copy in copies:
         copy.start()
+    copies[0].wait()
+    copies[1].wait()
     target = side_targets(owners, neighbour, code, position[0])
     lane = lax.broadcasted_iota(jnp.int32, (SIDE_CELLS, 3 * N * N), 1)
     onehot[...] = jnp.where(target == lane, 1.0, 0.0).astype(BF16)
     corner = jnp.zeros((HALO, LEFT, LANES), F32)
-    copies[0].wait()
+    copies[2].wait()
     own = own_ref[...]
     rims = dot(onehot[:, : N * N], own, 1, 0)
     inner = own.astype(F32).reshape(N, N, C)
@@ -118,32 +124,7 @@
         for rows, cols, cells in RIMS:
             frame[l, rows, cols, :] = rims[cells, lanes].reshape(span(rows), span(cols), LANES)
         frame[l, HALO : HALO + N, LEFT : LEFT + N, :] = inner[:, :, lanes]
-    copies[1].wait()
-    copies[2].wait()
-    d_hidden[...] = dot(cot_ref[...], wout_ref[...], 1, 1)
     copies[3].wait()
-    copies[4].wait()
-
-
-def add_rims(cells_to, tile_ref, onehot, frame):
-    rims = dot(onehot[:, cells_to], tile_ref[...], 1, 0)
-    for l in range(C // LANES):
-        lanes = slice(l * LANES, (l + 1) * LANES)
-        for rows, cols, cells in RIMS:
-            frame[l, rows, cols, :] += rims[cells, lanes].reshape(span(rows), span(cols), LANES)
-
-
-def one_kernel(start_ref, one_ref, onehot, frame):
-    del start_ref
-    add_rims(slice(N * N, 2 * N * N), one_ref, onehot, frame)
-
-
-def forward_kernel(
-    core, start_ref, two_ref, onehot, d_hidden_ref, cot_ref, taps_ref, win_ref,
-    send_ref, keep_ref, dconv_ref, frame, conv,
-):
-    del start_ref
-    add_rims(slice(2 * N * N, 3 * N * N), two_ref, onehot, frame)
     for l in range(C // LANES):
         lanes = slice(l * LANES, (l + 1) * LANES)
         acc = [None] * N
@@ -159,6 +140,53 @@
                         acc[i] = term if acc[i] is None else acc[i] + term
         for i in range(N):
             conv[i * N : (i + 1) * N, lanes] = acc[i]
+    copies[4].wait()
+    copies[5].wait()
+    d_hidden[...] = dot(cot_ref[...], wout_ref[...], 1, 1)
+    copies[6].wait()
+
+
+def one_kernel(one_ref, onehot, rims):
+    rims[...] = dot(onehot[:, N * N : 2 * N * N], one_ref[...], 1, 0)
+
+
+def add_rims(rims_ref, two_ref, onehot, taps_ref, frame, conv, alone):
+    rims = rims_ref[...] + dot(onehot[:, 2 * N * N :], two_ref[...], 1, 0)
+    alone[...] = jnp.zeros(alone.shape, F32)
+    for l in range(C // LANES):
+        lanes = slice(l * LANES, (l + 1) * LANES)
+        for rows, cols, cells in RIMS:
+            block = rims[cells, lanes].reshape(span(rows), span(cols), LANES)
+            frame[l, rows, cols, :] += block
+            alone[l, rows, cols, :] = block
+    for l in range(C // LANES):
+        lanes = slice(l * LANES, (l + 1) * LANES)
+        acc = [[conv[i * N + 8 * t : i * N + 8 * t + 8, lanes] for t in range(2)] for i in range(N)]
+        for b in range(TAPS):
+            off = tap_offset(b)
+            coef = [taps_ref[a * TAPS + b : a * TAPS + b + 1, lanes] for a in range(TAPS)]
+            for r in range(ROWS):
+                middle = HALO <= r < HALO + N
+                for t in range(2):
+                    start = off + 8 * t
+                    if middle and start >= LEFT and start + 8 <= LEFT + N:
+                        continue
+                    x = alone[l, r, start : start + 8, :]
+                    for a in range(TAPS):
+                        i = r - STEP * a
+                        if 0 <= i < N:
+                            acc[i][t] = acc[i][t] + x * coef[a]
+        for i in range(N):
+            for t in range(2):
+                conv[i * N + 8 * t : i * N + 8 * t + 8, lanes] = acc[i][t]
+
+
+def forward_kernel(
+    core, frame_in, conv_in, rims_ref, two_ref, onehot, d_hidden_ref, cot_ref, taps_ref, win_ref,
+    send_ref, keep_ref, dconv_ref, frame, conv, alone,
+):
+    del frame_in, conv_in
+    add_rims(rims_ref, two_ref, onehot, taps_ref, frame, conv, alone)
     value = conv[...]
     centred = value - jnp.mean(value, -1, keepdims=True)
     inv_std = lax.rsqrt(jnp.mean(centred * centred, -1, keepdims=True) + 1e-06)
@@ -174,8 +202,9 @@
         square = pre * pre
         t = jnp.tanh(pre * (GELU_A + (GELU_A * GELU_B) * square))
         half = 0.5 + 0.5 * t
-        hidden = (pre * half).astype(BF16)
-        slope = half + (0.5 * pre) * (1.0 - t * t) * (GELU_A + (3.0 * GELU_A * GELU_B) * square)
+        value = pre * half
+        hidden = value.astype(BF16)
+        slope = half + value * ((1.0 - t) * (GELU_A + (3.0 * GELU_A * GELU_B) * square))
         d_pre = (d_hidden_ref[:, cols] * slope).astype(BF16)
         part_out = dot(hidden, cot, 0, 0).astype(BF16)
         part_in = dot(normed, d_pre, 0, 0).astype(BF16)
@@ -212,14 +241,16 @@
                 )
 
 
+def tap_kernel(frame, dconv_in, keep_in, sums_ref, dconv_ref, keep_ref):
+    del dconv_in, keep_in, keep_ref
+    tap_sums(frame, dconv_ref, sums_ref)
+
+
 def backward_kernel(
-    frame, onehot, dconv_ref, taps_ref, cot_hbm, _, sums_ref, own_ref, one_ref, two_ref, keep_ref,
-    shifted, rim, cot_ref, sem,
+    onehot, dconv_ref, taps_ref, cot_hbm, own_ref, one_ref, two_ref, shifted, rim, cot_ref, sem,
 ):
-    del keep_ref
     copy = pltpu.make_async_copy(cot_hbm, cot_ref, sem)
     copy.start()
-    tap_sums(frame, dconv_ref, sums_ref)
     residues = (2, 4, 6, 0)
     pad = jnp.zeros((ROWS, 8, LANES), F32)
     for l in range(C // LANES):
@@ -321,15 +352,19 @@
         pl.when(jnp.logical_not(to_in))(into_out.wait)
 
 
-def join_kernel(own_ref, one_ref, two_ref, out_ref):
-    out_ref[...] = (own_ref[...] + one_ref[...].astype(F32) + two_ref[...].astype(F32)).astype(BF16)
+def join_kernel(own_ref, other_ref, out_ref):
+    out_ref[...] = (own_ref[...] + other_ref[...].astype(F32)).astype(out_ref.dtype)
 
 
 def in_hbm(x):
     return pltpu.with_memory_space_constraint(x, pltpu.HBM)
 
 
-def call(kernel, outs, scratch=(), specs=(), flops=700_000_000, aliases={}, out_specs=None, vmem=16):
+def in_vmem(x):
+    return pltpu.with_memory_space_constraint(x, pltpu.VMEM)
+
+
+def call(kernel, outs, scratch=(), specs=(), flops=300_000_000, aliases={}, out_specs=None, vmem=16):
     return pl.pallas_call(
         kernel,
         out_shape=outs,
@@ -384,81 +419,89 @@
     two = two_over(own)
 
     frame = pltpu.VMEM((2, ROWS, FRAME, LANES), F32)
-    onehot, frame_one, d_hidden, cot, taps, w_in = call(
+    cells = pltpu.VMEM((N * N, C), F32)
+    onehot, frame_own, conv_own, d_hidden, cot, taps, w_in = call(
         functools.partial(prepare_kernel, owners),
         (
             pltpu.VMEM((SIDE_CELLS, 3 * N * N), BF16),
             frame,
+            cells,
             pltpu.VMEM((N * N, HID), F32),
             pltpu.VMEM((N * N, C), BF16),
             pltpu.VMEM((TAPS * TAPS, C), F32),
             pltpu.VMEM((C, HID), BF16),
         ),
         [
+            pltpu.SMEM((1, 4), jnp.int32),
+            pltpu.SMEM((1, 4), jnp.int32),
             pltpu.VMEM((N * N, C), BF16),
             pltpu.VMEM((HID, C), BF16),
-            pltpu.SemaphoreType.DMA((5,)),
+            pltpu.SemaphoreType.DMA((7,)),
         ],
-        [SMEM] * 3 + [HBM] * 5,
+        [SMEM] + [HBM] * 7,
     )(
-        tile_neighbour, edge_code, position.reshape(1).astype(jnp.int32),
-        *map(in_hbm, (own, cot_rows, kernel, weight_in, weight_out)),
+        position.reshape(1).astype(jnp.int32),
+        *map(in_hbm, (tile_neighbour, edge_code, own, kernel, cot_rows, weight_out, weight_in)),
     )
-    frame_one = call(
-        one_kernel, frame, (), [VMEM] * 3, aliases={0: 0}
-    )(frame_one, one, onehot)
+    rims = call(one_kernel, pltpu.VMEM((SIDE_CELLS, C), F32), (), [VMEM] * 2)(one, onehot)
     half = pltpu.VMEM((GROUP, C, C), BF16)
-    send, keep, dconv, frame_two = call(
+    send, keep, dconv, frame_two, _ = call(
         forward_kernel,
-        (half, half, pltpu.VMEM((N * N, C), F32), frame),
-        [pltpu.VMEM((N * N, C), F32)],
-        [SMEM] + [VMEM] * 7,
+        (half, half, cells, frame, cells),
+        [frame],
+        [SMEM] + [VMEM] * 9,
         flops=1_000_000_000,
-        aliases={1: 3},
-    )(core, frame_one, two, onehot, d_hidden, cot, taps, w_in)
+        aliases={1: 3, 2: 4},
+    )(core, frame_own, conv_own, rims, two, onehot, d_hidden, cot, taps, w_in)
     got = swap(send, 1, 1)
-    part_taps, grad_own, grad_one, grad_two, keep = call(
+    part_taps, dconv, keep = call(
+        tap_kernel,
+        (pltpu.VMEM((GROUP, EXTRA, C), F32), cells, half),
+        (),
+        [VMEM] * 3,
+        aliases={1: 1, 2: 2},
+    )(frame_two, dconv, keep)
+    block = pltpu.VMEM((C + EXTRA, C), BF16)
+    pieces = call(
+        spread_kernel, (block,) * GROUP, (), [SMEM] + [VMEM] * 3
+    )(mine_at, keep, in_vmem(got), part_taps)
+    total = pieces[0].astype(F32)
+    for d in STARTS[0]:
+        total = total + swap(pieces[d], combos[0][d - 1], combos[1][d - 1]).astype(F32)
+    total = total.astype(BF16)
+
+    grad_own, grad_one, grad_two = call(
         backward_kernel,
-        (
-            pltpu.VMEM((GROUP, EXTRA, C), F32),
-            pltpu.VMEM((N * N, C), F32),
-            pltpu.VMEM((N * N, C), BF16),
-            pltpu.VMEM((N * N, C), BF16),
-            half,
-        ),
+        (cells, pltpu.VMEM((N * N, C), BF16), pltpu.VMEM((N * N, C), BF16)),
         [
             pltpu.VMEM((2, 4, ROWS, 40, LANES), F32),
             pltpu.VMEM((SIDE_CELLS, C), BF16),
             pltpu.VMEM((N * N, C), BF16),
             pltpu.SemaphoreType.DMA,
         ],
-        [VMEM] * 4 + [HBM, VMEM],
-        aliases={5: 4},
-    )(frame_two, onehot, dconv, taps, in_hbm(cot_rows), keep)
-
-    block = struct((C + EXTRA, C), BF16)
-    pieces = call(
-        spread_kernel, (block,) * GROUP, (), [SMEM] + [VMEM] * 3
-    )(mine_at, keep, got, part_taps)
-    total = pieces[0].astype(F32)
-    for piece, even, odd in reversed(list(zip(pieces[1:], *combos))):
-        total = total + swap(piece, even, odd).astype(F32)
-    total = total.astype(BF16)
-
+        [VMEM] * 3 + [HBM],
+    )(onehot, dconv, taps, in_hbm(cot_rows))
     back_two = two_over(grad_two)
     back_one = one_over(grad_one)
     for even, odd in [(pairs[1], pairs[0])] + [(p, p) for p in later]:
-        got = [swap(total, a, b) for a, b in zip(even, odd)]
-        summed = total.astype(F32) + got[0].astype(F32)
-        if len(got) == 2:
-            third = swap(total, sum(even), sum(odd))
-            summed = summed + (got[1].astype(F32) + third.astype(F32))
+        if len(even) == 2:
+            even, odd = (*even, sum(even)), (*odd, sum(odd))
+        order = [d for d in reversed(STARTS[1]) if d <= len(even)]
+        got = {d: swap(total, even[d - 1], odd[d - 1]).astype(F32) for d in order}
+        summed = total.astype(F32) + got[1]
+        if len(even) == 3:
+            summed = summed + (got[2] + got[3])
         total = summed.astype(BF16)
+    joined = call(
+        join_kernel, pltpu.VMEM((N * N, C), F32), (), [VMEM] * 2, flops=JOIN_COST
+    )(grad_own, back_one)
+    total, joined = lax.optimization_barrier((total, joined))
+    mine = {d: swap(total, combos[0][d - 1], combos[1][d - 1]) for d in reversed(STARTS[2])}
+    mine = [total, mine[1], mine[2], mine[3]]
     grad_features = call(
-        join_kernel, struct((N * N, C), BF16), (), [VMEM] * 3, flops=JOIN_COST
-    )(grad_own, back_one, back_two)
-    total, grad_features = lax.optimization_barrier((total, grad_features))
-    mine = [total] + [swap(total, even, odd) for even, odd in zip(*combos)]
+        join_kernel, struct((N * N, C), BF16), (), [VMEM] * 2, flops=JOIN_COST
+    )(joined, back_two)
+    mine[0], grad_features = lax.optimization_barrier((mine[0], grad_features))
     theirs = [swap(x, 1, 1) for x in mine]
     grads = (struct((C, HID), F32), struct((HID, C), F32))
     stage = [pltpu.VMEM((GROUP, C, C), F32), pltpu.SemaphoreType.DMA((GROUP + 1,))]

time: 47 us -> 46.4 us (0.987)
  waiting for transfers between devices: 10.2 us -> 11.9 us
  starting transfers between devices: 24.2 us -> 22.5 us
  local copies, waits for them, and re-layouts: 0.67 us -> 0 us
    ppermute x14, starting transfers between devices: 13.4 us -> 11.6 us  [swap(): lax.ppermute(x, both, [(i, i ^ (odd if i % 2 else even)) for i in range(d...]
    ppermute x14, waiting for transfers between devices: 8.8 us -> 10.5 us  [swap(): lax.ppermute(x, both, [(i, i ^ (odd if i % 2 else even)) for i in range(d...]
    unnamed x4 -> x0, local copies, waits for them, and re-layouts: 0.67 us -> none
    pallas_call x4 -> x6, Pallas kernels: 6.43 us -> 6.02 us  [the longest x1 2.76 us: body(): call(forward_kernel, (half, half, cells, frame, cells), [frame], [SMEM] +...]
  transfers between devices with their start and end apart: 18 -> 18, of which waited for: 8 -> 8; matrix products, arithmetic and copies ran while one was open for 0% -> 0% of each run, Pallas kernels for 14% -> 15%
where the time goes in v4:
time: 46.4 us; the launch traced here: 46.2 us
  starting transfers between devices  22.5 us (48%)
  waiting for transfers between devices  11.9 us (26%)
  Pallas kernels  10.9 us (23%)
  between operations  0.78 us (2%)
    ppermute x14, starting transfers between devices, swap(): lax.ppermute(x, both, [(i, i ^ (odd if i % 2 else even)) for i in range(d...  11.6 us
    ppermute x14, waiting for transfers between devices, swap(): lax.ppermute(x, both, [(i, i ^ (odd if i % 2 else even)) for i in range(d...  10.5 us
    ppermute x2, starting transfers between devices, two_over(): return lax.ppermute(x, 'tile', moves)  7.13 us
    ppermute x2, starting transfers between devices, one_over(): return lax.ppermute(x, 'tile', [(i, i ^ 1) for i in range(owners)])  3.7 us
    pallas_call x1, Pallas kernels, body(): call(forward_kernel, (half, half, cells, frame, cells), [frame], [SMEM] +...  2.76 us
    pallas_call x1, Pallas kernels, body(): call(functools.partial(prepare_kernel, owners), (pltpu.VMEM((SIDE_CELLS,...  2.66 us
    pallas_call x2, Pallas kernels, store(): call(functools.partial(store_kernel, scale, picks, len(given), last), (*g...  2.08 us
    ppermute x2, waiting for transfers between devices, two_over(): return lax.ppermute(x, 'tile', moves)  1.41 us
  transfers between devices with their start and end apart: 18, of which 8 were waited for; matrix products, arithmetic and copies ran while one was open for 0% of the time, Pallas kernels for 15%

profile of v4, /device:TPU:0, one launch (start us, length us, event | category | flops | bytes accessed | tf_op | source)
XLA Modules:
  0.0 46.2 jit_solution(9522214559542148088)
XLA Ops:
  0.6 3.0 %collective-permute-start = (bf16[256,256]{1,0:T(8,128)(2,1)}, bf16[256,256]{1,0:T(8,128)(2,1)S(1)}, u32[]{:S(2)}, u32[]{:S(2)}) collective-permute-start(bf16[256,256]{1,0:T(8,128)(2,1)} %bitcast.9), channel_id=1, source_target_pairs={{0,4},{4,0},{8,12},{12,8},{16,20},{20,16},{24,28},{28,24},{1,5},{5... | collective-permute-start | bytes 393224 | tf_op jit(solution)/shard_map/ppermute | solution.py:391
  3.6 3.6 %collective-permute-start.1 = (bf16[256,256]{1,0:T(8,128)(2,1)}, bf16[256,256]{1,0:T(8,128)(2,1)S(1)}, u32[]{:S(2)}, u32[]{:S(2)}) collective-permute-start(bf16[256,256]{1,0:T(8,128)(2,1)} %bitcast.10), channel_id=1, source_target_pairs={{0,28},{4,8},{8,4},{12,16},{16,12},{20,24},{24,20},{28,0},{1,29},{... | collective-permute-start | bytes 393224 | tf_op jit(solution)/shard_map/ppermute | solution.py:395
  7.2 2.7 %shard_map.102 = (bf16[448,768]{1,0:T(8,128)(2,1)S(1)}, f32[2,28,32,128]{3,2,1,0:T(8,128)S(1)}, f32[256,256]{1,0:T(8,128)S(1)}, f32[256,1024]{1,0:T(8,128)S(1)},...) custom-call(s32[1]{0:T(128)} %bitcast.2.position, s32[1,4]{1,0:T(1,128)} %neighbour_hbm.1, ...), custom_call_target="tpu_custom_call" | custom-call | flops 300000000 | bytes 4000000 | tf_op jit(solution)/shard_map/pallas_call | solution.py:423
  9.9 0.0 collective-permute-done.one_ref
  9.9 0.2 shard_map.103.rims_ref
  10.1 1.4 %collective-permute-done.1.two_ref = bf16[256,256]{1,0:T(8,128)(2,1)S(1)} collective-permute-done((bf16[256,256]{1,0:T(8,128)(2,1)}, bf16[256,256]{1,0:T(8,128)(2,1)S(1)}, u32[]{:S(2)}, u32[]{:S(2)}) %collective-permute-start.1) | collective-permute-done | bytes 131104 | tf_op jit(solution)/shard_map/ppermute | solution.py:395
  11.5 2.8 %shard_map.104 = (bf16[4,256,256]{2,1,0:T(8,128)(2,1)S(1)}, bf16[4,256,256]{2,1,0:T(8,128)(2,1)S(1)}, f32[256,256]{1,0:T(8,128)S(1)}, f32[2,28,32,128]{3,2,1,0:T(8,128)S(1)}, f32[256,256]{1,0:T(8,128)S(1)}) custom-call(s32[1]{0:T(128)} %bitcast.1.core, ...), custom_call_target="tpu_custom_call", output_to_operand_aliasing={{3}: (1, {}), {4}: (2, {})} | custom-call | flops 1000000000 | bytes 4000000 | tf_op jit(solution)/shard_map/pallas_call | solution.py:448
  14.3 0.1 collective-permute-start.2
  14.4 0.9 %shard_map.105 = (f32[4,16,256]{2,1,0:T(8,128)S(1)}, f32[256,256]{1,0:T(8,128)S(1)}, bf16[4,256,256]{2,1,0:T(8,128)(2,1)S(1)}) custom-call(f32[2,28,32,128]{3,2,1,0:T(8,128)S(1)} %get-tuple-element.41.frame, f32[256,256]{1,0:T(8,128)S(1)} %get-tuple-element.42.dconv_in, ...), custom_call_target="tpu_custom_call", output_to_operand_aliasing={{1}: (1, {}), {2}: (2, {})} | custom-call | flops 300000000 | bytes 4000000 | tf_op jit(solution)/shard_map/pallas_call | solution.py:457
  15.3 0.9 %collective-permute-done.2.got_ref = bf16[4,256,256]{2,1,0:T(8,128)(2,1)S(1)} collective-permute-done((bf16[4,256,256]{2,1,0:T(8,128)(2,1)S(1)}, bf16[4,256,256]{2,1,0:T(8,128)(2,1)S(1)}, u32[]{:S(2)}, u32[]{:S(2)}) %collective-permute-start.2) | collective-permute-done | bytes 524320 | tf_op jit(solution)/shard_map/ppermute | solution.py:404
  16.3 0.1 shard_map.106
  16.4 1.6 %collective-permute-start.3 = (bf16[272,256]{1,0:T(8,128)(2,1)S(1)}, bf16[272,256]{1,0:T(8,128)(2,1)S(1)}, u32[]{:S(2)}, u32[]{:S(2)}) collective-permute-start(bf16[272,256]{1,0:T(8,128)(2,1)S(1)} %get-tuple-element.48), channel_id=1, source_target_pairs={{0,6},{1,25},{2,4},{3,27},{4,2},{5,29},{6,0},{7,31},{8,14},{9,17},... | collective-permute-start | bytes 417800 | tf_op jit(solution)/shard_map/ppermute | solution.py:404
  18.0 1.4 %collective-permute-start.4 = (bf16[272,256]{1,0:T(8,128)(2,1)S(1)}, bf16[272,256]{1,0:T(8,128)(2,1)S(1)}, u32[]{:S(2)}, u32[]{:S(2)}) collective-permute-start(bf16[272,256]{1,0:T(8,128)(2,1)S(1)} %get-tuple-element.49), channel_id=1, source_target_pairs={{0,4},{1,17},{2,6},{3,19},{4,0},{5,21},{6,2},{7,23},{8,12},{9,25},... | collective-permute-start | bytes 417800 | tf_op jit(solution)/shard_map/ppermute | solution.py:404
  19.4 0.5 %collective-permute-start.5 = (bf16[272,256]{1,0:T(8,128)(2,1)S(1)}, bf16[272,256]{1,0:T(8,128)(2,1)S(1)}, u32[]{:S(2)}, u32[]{:S(2)}) collective-permute-start(bf16[272,256]{1,0:T(8,128)(2,1)S(1)} %get-tuple-element.50), channel_id=1, source_target_pairs={{0,2},{1,9},{2,0},{3,11},{4,6},{5,13},{6,4},{7,15},{8,10},{9,1},{1... | collective-permute-start | bytes 417800 | tf_op jit(solution)/shard_map/ppermute | solution.py:404
  19.9 1.4 %shard_map.107 = (f32[256,256]{1,0:T(8,128)S(1)}, bf16[256,256]{1,0:T(8,128)(2,1)S(1)}, bf16[256,256]{1,0:T(8,128)(2,1)S(1)}) custom-call(bf16[448,768]{1,0:T(8,128)(2,1)S(1)} %get-tuple-element.36.onehot, f32[256,256]{1,0:T(8,128)S(1)} %get-tuple-element.51.dconv_ref, f32[49,256]{1,0:T(8,128)S(1)} %get-tuple-element.39.taps_ref, bf16[256,256]{1,0:T(8,128)(2,1)} %bitcast.8), custom_call_target="tpu_custom_call" | custom-call | flops 300000000 | bytes 4000000 | tf_op jit(solution)/shard_map/pallas_call | solution.py:473
  21.3 0.7 %collective-permute-start.9 = (bf16[256,256]{1,0:T(8,128)(2,1)S(1)}, bf16[256,256]{1,0:T(8,128)(2,1)S(1)}, u32[]{:S(2)}, u32[]{:S(2)}) collective-permute-start(bf16[256,256]{1,0:T(8,128)(2,1)S(1)} %get-tuple-element.53), channel_id=1, source_target_pairs={{0,4},{4,0},{8,12},{12,8},{16,20},{20,16},{24,28},{28,24},{1,5},{5... | collective-permute-start | bytes 393224 | tf_op jit(solution)/shard_map/ppermute | solution.py:391
  22.0 3.6 %collective-permute-start.10 = (bf16[256,256]{1,0:T(8,128)(2,1)S(1)}, bf16[256,256]{1,0:T(8,128)(2,1)S(1)}, u32[]{:S(2)}, u32[]{:S(2)}) collective-permute-start(bf16[256,256]{1,0:T(8,128)(2,1)S(1)} %get-tuple-element.56), channel_id=1, source_target_pairs={{0,28},{4,8},{8,4},{12,16},{16,12},{20,24},{24,20},{28,0},{1,29},{... | collective-permute-start | bytes 393224 | tf_op jit(solution)/shard_map/ppermute | solution.py:395
  25.6 0.0 collective-permute-done.3
  25.6 0.0 collective-permute-done.4
  25.6 0.0 collective-permute-done.5
  25.6 0.1 add_convert_fusion.1
  25.7 1.7 %collective-permute-start.8 = (bf16[272,256]{1,0:T(8,128)(2,1)S(1)}, bf16[272,256]{1,0:T(8,128)(2,1)S(1)}, u32[]{:S(2)}, u32[]{:S(2)}) collective-permute-start(bf16[272,256]{1,0:T(8,128)(2,1)S(1)} %add_convert_fusion.1), channel_id=1, source_target_pairs={{0,24},{1,7},{2,26},{3,5},{4,28},{5,3},{6,30},{7,1},{8,16},{9,15},... | collective-permute-start | bytes 417800 | tf_op jit(solution)/shard_map/ppermute | solution.py:404
  27.4 0.0 collective-permute-start.7
  27.4 2.8 %collective-permute-start.6 = (bf16[272,256]{1,0:T(8,128)(2,1)S(1)}, bf16[272,256]{1,0:T(8,128)(2,1)S(1)}, u32[]{:S(2)}, u32[]{:S(2)}) collective-permute-start(bf16[272,256]{1,0:T(8,128)(2,1)S(1)} %add_convert_fusion.1), channel_id=1, source_target_pairs={{0,8},{1,3},{2,10},{3,1},{4,12},{5,7},{6,14},{7,5},{8,0},{9,11},{1... | collective-permute-start | bytes 417800 | tf_op jit(solution)/shard_map/ppermute | solution.py:404
  30.1 0.0 collective-permute-done.9.other_ref
  30.2 2.6 %collective-permute-done.8 = bf16[272,256]{1,0:T(8,128)(2,1)S(1)} collective-permute-done((bf16[272,256]{1,0:T(8,128)(2,1)S(1)}, bf16[272,256]{1,0:T(8,128)(2,1)S(1)}, u32[]{:S(2)}, u32[]{:S(2)}) %collective-permute-start.8) | collective-permute-done | bytes 139296 | tf_op jit(solution)/shard_map/ppermute | solution.py:404
  32.8 2.8 %collective-permute-done.7 = bf16[272,256]{1,0:T(8,128)(2,1)S(1)} collective-permute-done((bf16[272,256]{1,0:T(8,128)(2,1)S(1)}, bf16[272,256]{1,0:T(8,128)(2,1)S(1)}, u32[]{:S(2)}, u32[]{:S(2)}) %collective-permute-start.7) | collective-permute-done | bytes 139296 | tf_op jit(solution)/shard_map/ppermute | solution.py:404
  35.6 0.0 collective-permute-done.6
  35.6 0.1 add_convert_fusion.refs_0_.refs_4_
  35.7 2.1 %collective-permute-start.16 = (bf16[272,256]{1,0:T(8,128)(2,1)S(1)}, bf16[272,256]{1,0:T(8,128)(2,1)S(1)}, u32[]{:S(2)}, u32[]{:S(2)}) collective-permute-start(bf16[272,256]{1,0:T(8,128)(2,1)S(1)} %add_convert_fusion.refs_0_.refs_4_), channel_id=1, source_target_pairs={{0,6},{1,25},{2,4},{3,27},{4,2},{5,29},{6,0},{7,31},{8,14},{9,17},... | collective-permute-start | bytes 417800 | tf_op jit(solution)/shard_map/ppermute | solution.py:404
  37.7 1.0 %collective-permute-start.14 = (bf16[272,256]{1,0:T(8,128)(2,1)S(1)}, bf16[272,256]{1,0:T(8,128)(2,1)S(1)}, u32[]{:S(2)}, u32[]{:S(2)}) collective-permute-start(bf16[272,256]{1,0:T(8,128)(2,1)S(1)} %add_convert_fusion.refs_0_.refs_4_), channel_id=1, source_target_pairs={{0,4},{1,17},{2,6},{3,19},{4,0},{5,21},{6,2},{7,23},{8,12},{9,25},... | collective-permute-start | bytes 417800 | tf_op jit(solution)/shard_map/ppermute | solution.py:404
  38.7 0.5 %collective-permute-start.12 = (bf16[272,256]{1,0:T(8,128)(2,1)S(1)}, bf16[272,256]{1,0:T(8,128)(2,1)S(1)}, u32[]{:S(2)}, u32[]{:S(2)}) collective-permute-start(bf16[272,256]{1,0:T(8,128)(2,1)S(1)} %add_convert_fusion.refs_0_.refs_4_), channel_id=1, source_target_pairs={{0,2},{1,9},{2,0},{3,11},{4,6},{5,13},{6,4},{7,15},{8,10},{9,1},{1... | collective-permute-start | bytes 417800 | tf_op jit(solution)/shard_map/ppermute | solution.py:404
  39.2 0.0 collective-permute-done.10.other_ref
  39.2 0.7 %shard_map.109 = bf16[256,256]{1,0:T(8,128)(2,1)} custom-call(f32[256,256]{1,0:T(8,128)S(1)} %shard_map.108.own_ref, bf16[256,256]{1,0:T(8,128)(2,1)S(1)} %collective-permute-done.10.other_ref), custom_call_target="tpu_custom_call" | custom-call | flops 30000001024 | bytes 4000000 | tf_op jit(solution)/shard_map/pallas_call | solution.py:501
  39.9 0.0 collective-permute-start.11
  39.9 1.8 %collective-permute-done.16.refs_3_.refs_7_ = bf16[272,256]{1,0:T(8,128)(2,1)S(1)} collective-permute-done((bf16[272,256]{1,0:T(8,128)(2,1)S(1)}, bf16[272,256]{1,0:T(8,128)(2,1)S(1)}, u32[]{:S(2)}, u32[]{:S(2)}) %collective-permute-start.16) | collective-permute-done | bytes 139296 | tf_op jit(solution)/shard_map/ppermute | solution.py:404
  41.7 0.0 collective-permute-start.17
  41.7 1.6 %collective-permute-done.14.refs_2_.refs_6_ = bf16[272,256]{1,0:T(8,128)(2,1)S(1)} collective-permute-done((bf16[272,256]{1,0:T(8,128)(2,1)S(1)}, bf16[272,256]{1,0:T(8,128)(2,1)S(1)}, u32[]{:S(2)}, u32[]{:S(2)}) %collective-permute-start.14) | collective-permute-done | bytes 139296 | tf_op jit(solution)/shard_map/ppermute | solution.py:404
  43.3 0.0 collective-permute-start.15
  43.3 0.5 %collective-permute-done.12.refs_1_.refs_5_ = bf16[272,256]{1,0:T(8,128)(2,1)S(1)} collective-permute-done((bf16[272,256]{1,0:T(8,128)(2,1)S(1)}, bf16[272,256]{1,0:T(8,128)(2,1)S(1)}, u32[]{:S(2)}, u32[]{:S(2)}) %collective-permute-start.12) | collective-permute-done | bytes 139296 | tf_op jit(solution)/shard_map/ppermute | solution.py:404
  43.8 0.0 collective-permute-start.13
  43.8 1.0 %shard_map.110 = (f32[256,1024]{1,0:T(8,128)}, f32[1024,256]{1,0:T(8,128)}) custom-call(s32[1]{0:T(128)} %bitcast.1.core, s32[1]{0:T(128)} %bitcast.place.mine_at, s32[1]{0:T(128)} %bitcast.6.theirs_at, bf16[272,256]{1,0:T(8,128)(2,1)S(1)} %add_convert_fusion.refs_0_.refs_4_, bf16[272,256]{1,0:T(8,128)(2,1)S(1)} %collective-permute-done.12.refs_1_.refs_5_, ...), custom_call_target="tpu_custom_call" | custom-call | flops 300000000 | bytes 4000000 | tf_op jit(solution)/shard_map/pallas_call | solution.py:513
  44.8 0.0 collective-permute-done.11.refs_0_.refs_8_
  44.8 0.0 collective-permute-done.17.refs_3_.refs_11_
  44.9 0.0 collective-permute-done.15.refs_2_.refs_10_
  44.9 0.3 collective-permute-done.13.refs_1_.refs_9_
  45.2 1.1 %shard_map.111 = (f32[256,1024]{1,0:T(8,128)}, f32[1024,256]{1,0:T(8,128)}, f32[49,256]{1,0:T(8,128)}) custom-call(s32[1]{0:T(128)} %bitcast.1.core, s32[1]{0:T(128)} %bitcast.place.mine_at, s32[1]{0:T(128)} %bitcast.6.theirs_at, bf16[272,256]{1,0:T(8,128)(2,1)S(1)} %collective-permute-done.11.refs_0_.refs_8_, ...), custom_call_target="tpu_custom_call", output_to_operand_aliasing={{0}: (15, {}), {1}: (16, {})} | custom-call | flops 300000000 | bytes 4000000 | tf_op jit(solution)/shard_map/pallas_call | solution.py:513
  (1 shorter events, 0.0 us)
Async XLA Ops:
  0.6 9.3 %collective-permute-start = (bf16[256,256]{1,0:T(8,128)(2,1)}, bf16[256,256]{1,0:T(8,128)(2,1)S(1)}, u32[]{:S(2)}, u32[]{:S(2)}) collective-permute-start(bf16[256,256]{1,0:T(8,128)(2,1)} %bitcast.9), channel_id=1, source_target_pairs={{0,4},{4,0},{8,12},{12,8},{16,20},{20,16},{24,28},{28,24},{1,5},{5... | collective-permute-start | bytes 393224 | tf_op jit(solution)/shard_map/ppermute | solution.py:391
  3.6 7.9 %collective-permute-start.1 = (bf16[256,256]{1,0:T(8,128)(2,1)}, bf16[256,256]{1,0:T(8,128)(2,1)S(1)}, u32[]{:S(2)}, u32[]{:S(2)}) collective-permute-start(bf16[256,256]{1,0:T(8,128)(2,1)} %bitcast.10), channel_id=1, source_target_pairs={{0,28},{4,8},{8,4},{12,16},{16,12},{20,24},{24,20},{28,0},{1,29},{... | collective-permute-start | bytes 393224 | tf_op jit(solution)/shard_map/ppermute | solution.py:395
  14.3 2.0 %collective-permute-start.2 = (bf16[4,256,256]{2,1,0:T(8,128)(2,1)S(1)}, bf16[4,256,256]{2,1,0:T(8,128)(2,1)S(1)}, u32[]{:S(2)}, u32[]{:S(2)}) collective-permute-start(bf16[4,256,256]{2,1,0:T(8,128)(2,1)S(1)} %get-tuple-element.45), channel_id=1, source_target_pairs={{0,1},{1,0},{2,3},{3,2},{4,5},{5,4},{6,7},{7,6},{8,9},{9,8},{10,11... | collective-permute-start | bytes 1572872 | tf_op jit(solution)/shard_map/ppermute | solution.py:404
  16.4 9.2 %collective-permute-start.3 = (bf16[272,256]{1,0:T(8,128)(2,1)S(1)}, bf16[272,256]{1,0:T(8,128)(2,1)S(1)}, u32[]{:S(2)}, u32[]{:S(2)}) collective-permute-start(bf16[272,256]{1,0:T(8,128)(2,1)S(1)} %get-tuple-element.48), channel_id=1, source_target_pairs={{0,6},{1,25},{2,4},{3,27},{4,2},{5,29},{6,0},{7,31},{8,14},{9,17},... | collective-permute-start | bytes 417800 | tf_op jit(solution)/shard_map/ppermute | solution.py:404
  18.0 7.6 %collective-permute-start.4 = (bf16[272,256]{1,0:T(8,128)(2,1)S(1)}, bf16[272,256]{1,0:T(8,128)(2,1)S(1)}, u32[]{:S(2)}, u32[]{:S(2)}) collective-permute-start(bf16[272,256]{1,0:T(8,128)(2,1)S(1)} %get-tuple-element.49), channel_id=1, source_target_pairs={{0,4},{1,17},{2,6},{3,19},{4,0},{5,21},{6,2},{7,23},{8,12},{9,25},... | collective-permute-start | bytes 417800 | tf_op jit(solution)/shard_map/ppermute | solution.py:404
  19.4 6.2 %collective-permute-start.5 = (bf16[272,256]{1,0:T(8,128)(2,1)S(1)}, bf16[272,256]{1,0:T(8,128)(2,1)S(1)}, u32[]{:S(2)}, u32[]{:S(2)}) collective-permute-start(bf16[272,256]{1,0:T(8,128)(2,1)S(1)} %get-tuple-element.50), channel_id=1, source_target_pairs={{0,2},{1,9},{2,0},{3,11},{4,6},{5,13},{6,4},{7,15},{8,10},{9,1},{1... | collective-permute-start | bytes 417800 | tf_op jit(solution)/shard_map/ppermute | solution.py:404
  21.3 8.8 %collective-permute-start.9 = (bf16[256,256]{1,0:T(8,128)(2,1)S(1)}, bf16[256,256]{1,0:T(8,128)(2,1)S(1)}, u32[]{:S(2)}, u32[]{:S(2)}) collective-permute-start(bf16[256,256]{1,0:T(8,128)(2,1)S(1)} %get-tuple-element.53), channel_id=1, source_target_pairs={{0,4},{4,0},{8,12},{12,8},{16,20},{20,16},{24,28},{28,24},{1,5},{5... | collective-permute-start | bytes 393224 | tf_op jit(solution)/shard_map/ppermute | solution.py:391
  22.0 17.2 %collective-permute-start.10 = (bf16[256,256]{1,0:T(8,128)(2,1)S(1)}, bf16[256,256]{1,0:T(8,128)(2,1)S(1)}, u32[]{:S(2)}, u32[]{:S(2)}) collective-permute-start(bf16[256,256]{1,0:T(8,128)(2,1)S(1)} %get-tuple-element.56), channel_id=1, source_target_pairs={{0,28},{4,8},{8,4},{12,16},{16,12},{20,24},{24,20},{28,0},{1,29},{... | collective-permute-start | bytes 393224 | tf_op jit(solution)/shard_map/ppermute | solution.py:395
  25.7 7.1 %collective-permute-start.8 = (bf16[272,256]{1,0:T(8,128)(2,1)S(1)}, bf16[272,256]{1,0:T(8,128)(2,1)S(1)}, u32[]{:S(2)}, u32[]{:S(2)}) collective-permute-start(bf16[272,256]{1,0:T(8,128)(2,1)S(1)} %add_convert_fusion.1), channel_id=1, source_target_pairs={{0,24},{1,7},{2,26},{3,5},{4,28},{5,3},{6,30},{7,1},{8,16},{9,15},... | collective-permute-start | bytes 417800 | tf_op jit(solution)/shard_map/ppermute | solution.py:404
  27.4 8.2 %collective-permute-start.7 = (bf16[272,256]{1,0:T(8,128)(2,1)S(1)}, bf16[272,256]{1,0:T(8,128)(2,1)S(1)}, u32[]{:S(2)}, u32[]{:S(2)}) collective-permute-start(bf16[272,256]{1,0:T(8,128)(2,1)S(1)} %add_convert_fusion.1), channel_id=1, source_target_pairs={{0,16},{1,5},{2,18},{3,7},{4,20},{5,1},{6,22},{7,3},{8,24},{9,13},... | collective-permute-start | bytes 417800 | tf_op jit(solution)/shard_map/ppermute | solution.py:404
  27.4 8.2 %collective-permute-start.6 = (bf16[272,256]{1,0:T(8,128)(2,1)S(1)}, bf16[272,256]{1,0:T(8,128)(2,1)S(1)}, u32[]{:S(2)}, u32[]{:S(2)}) collective-permute-start(bf16[272,256]{1,0:T(8,128)(2,1)S(1)} %add_convert_fusion.1), channel_id=1, source_target_pairs={{0,8},{1,3},{2,10},{3,1},{4,12},{5,7},{6,14},{7,5},{8,0},{9,11},{1... | collective-permute-start | bytes 417800 | tf_op jit(solution)/shard_map/ppermute | solution.py:404
  35.7 6.0 %collective-permute-start.16 = (bf16[272,256]{1,0:T(8,128)(2,1)S(1)}, bf16[272,256]{1,0:T(8,128)(2,1)S(1)}, u32[]{:S(2)}, u32[]{:S(2)}) collective-permute-start(bf16[272,256]{1,0:T(8,128)(2,1)S(1)} %add_convert_fusion.refs_0_.refs_4_), channel_id=1, source_target_pairs={{0,6},{1,25},{2,4},{3,27},{4,2},{5,29},{6,0},{7,31},{8,14},{9,17},... | collective-permute-start | bytes 417800 | tf_op jit(solution)/shard_map/ppermute | solution.py:404
  37.7 5.5 %collective-permute-start.14 = (bf16[272,256]{1,0:T(8,128)(2,1)S(1)}, bf16[272,256]{1,0:T(8,128)(2,1)S(1)}, u32[]{:S(2)}, u32[]{:S(2)}) collective-permute-start(bf16[272,256]{1,0:T(8,128)(2,1)S(1)} %add_convert_fusion.refs_0_.refs_4_), channel_id=1, source_target_pairs={{0,4},{1,17},{2,6},{3,19},{4,0},{5,21},{6,2},{7,23},{8,12},{9,25},... | collective-permute-start | bytes 417800 | tf_op jit(solution)/shard_map/ppermute | solution.py:404
  38.7 5.1 %collective-permute-start.12 = (bf16[272,256]{1,0:T(8,128)(2,1)S(1)}, bf16[272,256]{1,0:T(8,128)(2,1)S(1)}, u32[]{:S(2)}, u32[]{:S(2)}) collective-permute-start(bf16[272,256]{1,0:T(8,128)(2,1)S(1)} %add_convert_fusion.refs_0_.refs_4_), channel_id=1, source_target_pairs={{0,2},{1,9},{2,0},{3,11},{4,6},{5,13},{6,4},{7,15},{8,10},{9,1},{1... | collective-permute-start | bytes 417800 | tf_op jit(solution)/shard_map/ppermute | solution.py:404
  39.9 4.9 %collective-permute-start.11 = (bf16[272,256]{1,0:T(8,128)(2,1)S(1)}, bf16[272,256]{1,0:T(8,128)(2,1)S(1)}, u32[]{:S(2)}, u32[]{:S(2)}) collective-permute-start(bf16[272,256]{1,0:T(8,128)(2,1)S(1)} %add_convert_fusion.refs_0_.refs_4_), channel_id=1, source_target_pairs={{0,1},{1,0},{2,3},{3,2},{4,5},{5,4},{6,7},{7,6},{8,9},{9,8},{10,11... | collective-permute-start | bytes 417800 | tf_op jit(solution)/shard_map/ppermute | solution.py:404
  41.7 3.1 %collective-permute-start.17 = (bf16[272,256]{1,0:T(8,128)(2,1)S(1)}, bf16[272,256]{1,0:T(8,128)(2,1)S(1)}, u32[]{:S(2)}, u32[]{:S(2)}) collective-permute-start(bf16[272,256]{1,0:T(8,128)(2,1)S(1)} %collective-permute-done.16.refs_3_.refs_7_), channel_id=1, source_target_pairs={{0,1},{1,0},{2,3},{3,2},{4,5},{5,4},{6,7},{7,6},{8,9},{9,8},{10,11... | collective-permute-start | bytes 417800 | tf_op jit(solution)/shard_map/ppermute | solution.py:404
  43.3 1.6 %collective-permute-start.15 = (bf16[272,256]{1,0:T(8,128)(2,1)S(1)}, bf16[272,256]{1,0:T(8,128)(2,1)S(1)}, u32[]{:S(2)}, u32[]{:S(2)}) collective-permute-start(bf16[272,256]{1,0:T(8,128)(2,1)S(1)} %collective-permute-done.14.refs_2_.refs_6_), channel_id=1, source_target_pairs={{0,1},{1,0},{2,3},{3,2},{4,5},{5,4},{6,7},{7,6},{8,9},{9,8},{10,11... | collective-permute-start | bytes 417800 | tf_op jit(solution)/shard_map/ppermute | solution.py:404
  43.8 1.4 %collective-permute-start.13 = (bf16[272,256]{1,0:T(8,128)(2,1)S(1)}, bf16[272,256]{1,0:T(8,128)(2,1)S(1)}, u32[]{:S(2)}, u32[]{:S(2)}) collective-permute-start(bf16[272,256]{1,0:T(8,128)(2,1)S(1)} %collective-permute-done.12.refs_1_.refs_5_), channel_id=1, source_target_pairs={{0,1},{1,0},{2,3},{3,2},{4,5},{5,4},{6,7},{7,6},{8,9},{9,8},{10,11... | collective-permute-start | bytes 417800 | tf_op jit(solution)/shard_map/ppermute | solution.py:404

commit v5 on v4

--- a/solution.py
+++ b/solution.py
@@ -86,16 +86,14 @@
 
 
 def prepare_kernel(
-    owners, position, neighbour_hbm, code_hbm, own_hbm, taps_hbm, cot_hbm, wout_hbm, win_hbm,
+    owners, position, neighbour, code, own_hbm, taps_hbm, cot_hbm, wout_hbm, win_hbm,
     onehot, frame, conv, d_hidden, cot_ref, taps_ref, win_ref,
-    neighbour, code, own_ref, wout_ref, sems,
+    own_ref, wout_ref, sems,
 ):
     copies = [
         pltpu.make_async_copy(src, dst, sems.at[n])
         for n, (src, dst) in enumerate(
             (
-                (neighbour_hbm, neighbour),
-                (code_hbm, code),
                 (own_hbm, own_ref),
                 (taps_hbm, taps_ref),
                 (cot_hbm, cot_ref),
@@ -106,13 +104,11 @@
     ]
     for copy in copies:
         copy.start()
-    copies[0].wait()
-    copies[1].wait()
     target = side_targets(owners, neighbour, code, position[0])
     lane = lax.broadcasted_iota(jnp.int32, (SIDE_CELLS, 3 * N * N), 1)
     onehot[...] = jnp.where(target == lane, 1.0, 0.0).astype(BF16)
     corner = jnp.zeros((HALO, LEFT, LANES), F32)
-    copies[2].wait()
+    copies[0].wait()
     own = own_ref[...]
     rims = dot(onehot[:, : N * N], own, 1, 0)
     inner = own.astype(F32).reshape(N, N, C)
@@ -124,7 +120,7 @@
         for rows, cols, cells in RIMS:
             frame[l, rows, cols, :] = rims[cells, lanes].reshape(span(rows), span(cols), LANES)
         frame[l, HALO : HALO + N, LEFT : LEFT + N, :] = inner[:, :, lanes]
-    copies[3].wait()
+    copies[1].wait()
     for l in range(C // LANES):
         lanes = slice(l * LANES, (l + 1) * LANES)
         acc = [None] * N
@@ -140,10 +136,10 @@
                         acc[i] = term if acc[i] is None else acc[i] + term
         for i in range(N):
             conv[i * N : (i + 1) * N, lanes] = acc[i]
+    copies[2].wait()
+    copies[3].wait()
+    d_hidden[...] = dot(cot_ref[...], wout_ref[...], 1, 1)
     copies[4].wait()
-    copies[5].wait()
-    d_hidden[...] = dot(cot_ref[...], wout_ref[...], 1, 1)
-    copies[6].wait()
 
 
 def one_kernel(one_ref, onehot, rims):
@@ -432,16 +428,16 @@
             pltpu.VMEM((C, HID), BF16),
         ),
         [
-            pltpu.SMEM((1, 4), jnp.int32),
-            pltpu.SMEM((1, 4), jnp.int32),
             pltpu.VMEM((N * N, C), BF16),
             pltpu.VMEM((HID, C), BF16),
-            pltpu.SemaphoreType.DMA((7,)),
+            pltpu.SemaphoreType.DMA((5,)),
         ],
-        [SMEM] + [HBM] * 7,
+        [SMEM] * 3 + [HBM] * 5,
     )(
         position.reshape(1).astype(jnp.int32),
-        *map(in_hbm, (tile_neighbour, edge_code, own, kernel, cot_rows, weight_out, weight_in)),
+        tile_neighbour,
+        edge_code,
+        *map(in_hbm, (own, kernel, cot_rows, weight_out, weight_in)),
     )
     rims = call(one_kernel, pltpu.VMEM((SIDE_CELLS, C), F32), (), [VMEM] * 2)(one, onehot)
     half = pltpu.VMEM((GROUP, C, C), BF16)

time: 46.4 us -> 46.4 us (level)
  waiting for transfers between devices: 11.9 us -> 10.7 us
  local copies, waits for them, and re-layouts: 0 us -> 0.67 us
  Pallas kernels: 10.9 us -> 11.4 us
    ppermute x2, waiting for transfers between devices: 1.41 us -> 0.18 us  [two_over(): return lax.ppermute(x, 'tile', moves)]
    unnamed x0 -> x4, local copies, waits for them, and re-layouts: none -> 0.67 us
    pallas_call x1, Pallas kernels: 2.66 us -> 3.21 us  [body(): call(functools.partial(prepare_kernel, owners), (pltpu.VMEM((SIDE_CELLS,...]
  transfers between devices with their start and end apart: 18 -> 18, of which waited for: 8 -> 8; matrix products, arithmetic and copies ran while one was open for 0% -> 0% of each run, Pallas kernels for 15% -> 16%
where the time goes in v5:
time: 46.4 us; the launch traced here: 46.2 us
  starting transfers between devices  22.5 us (48%)
  Pallas kernels  11.4 us (25%)
  waiting for transfers between devices  10.7 us (23%)
  between operations  0.78 us (2%)
  local copies, waits for them, and re-layouts  0.67 us (1%)
    ppermute x14, starting transfers between devices, swap(): lax.ppermute(x, both, [(i, i ^ (odd if i % 2 else even)) for i in range(d...  11.6 us
    ppermute x14, waiting for transfers between devices, swap(): lax.ppermute(x, both, [(i, i ^ (odd if i % 2 else even)) for i in range(d...  10.5 us
    ppermute x2, starting transfers between devices, two_over(): return lax.ppermute(x, 'tile', moves)  7.14 us
    ppermute x2, starting transfers between devices, one_over(): return lax.ppermute(x, 'tile', [(i, i ^ 1) for i in range(owners)])  3.68 us
    pallas_call x1, Pallas kernels, body(): call(functools.partial(prepare_kernel, owners), (pltpu.VMEM((SIDE_CELLS,...  3.21 us
    pallas_call x1, Pallas kernels, body(): call(forward_kernel, (half, half, cells, frame, cells), [frame], [SMEM] +...  2.77 us
    pallas_call x2, Pallas kernels, store(): call(functools.partial(store_kernel, scale, picks, len(given), last), (*g...  2.08 us
    pallas_call x1, Pallas kernels, body(): call(backward_kernel, (cells, pltpu.VMEM((N * N, C), BF16), pltpu.VMEM((N...  1.4 us
  transfers between devices with their start and end apart: 18, of which 8 were waited for; matrix products, arithmetic and copies ran while one was open for 0% of the time, Pallas kernels for 16%

profile of v5, /device:TPU:0, one launch (start us, length us, event | category | flops | bytes accessed | tf_op | source)
XLA Modules:
  0.0 46.2 jit_solution(16681972383144723935)
XLA Ops:
  0.6 3.0 %collective-permute-start = (bf16[256,256]{1,0:T(8,128)(2,1)}, bf16[256,256]{1,0:T(8,128)(2,1)S(1)}, u32[]{:S(2)}, u32[]{:S(2)}) collective-permute-start(bf16[256,256]{1,0:T(8,128)(2,1)} %bitcast.9), channel_id=1, source_target_pairs={{0,4},{4,0},{8,12},{12,8},{16,20},{20,16},{24,28},{28,24},{1,5},{5... | collective-permute-start | bytes 393224 | tf_op jit(solution)/shard_map/ppermute | solution.py:387
  3.6 3.6 %collective-permute-start.1 = (bf16[256,256]{1,0:T(8,128)(2,1)}, bf16[256,256]{1,0:T(8,128)(2,1)S(1)}, u32[]{:S(2)}, u32[]{:S(2)}) collective-permute-start(bf16[256,256]{1,0:T(8,128)(2,1)} %bitcast.10), channel_id=1, source_target_pairs={{0,28},{4,8},{8,4},{12,16},{16,12},{20,24},{24,20},{28,0},{1,29},{... | collective-permute-start | bytes 393224 | tf_op jit(solution)/shard_map/ppermute | solution.py:391
  7.2 0.0 copy-start
  7.2 0.0 copy-start.1
  7.2 0.7 %copy-done = s32[1,4]{1,0:T(1,128)S(1)} copy-done((s32[1,4]{1,0:T(1,128)S(1)}, s32[1,4]{1,0:T(1,128)}, u32[]{:S(2)}) %copy-start) | copy-done | bytes 40
  7.9 0.0 copy-done.1
  7.9 3.2 %shard_map.102 = (bf16[448,768]{1,0:T(8,128)(2,1)S(1)}, f32[2,28,32,128]{3,2,1,0:T(8,128)S(1)}, f32[256,256]{1,0:T(8,128)S(1)}, f32[256,1024]{1,0:T(8,128)S(1)},...) custom-call(s32[1]{0:T(128)} %bitcast.2.position, s32[1,4]{1,0:T(1,128)S(1)} %copy-done, ...), custom_call_target="tpu_custom_call" | custom-call | flops 300000000 | bytes 4000000 | tf_op jit(solution)/shard_map/pallas_call | solution.py:419
  11.1 0.0 collective-permute-done.one_ref
  11.1 0.2 shard_map.103.rims_ref
  11.3 0.2 collective-permute-done.1.two_ref
  11.5 2.8 %shard_map.104 = (bf16[4,256,256]{2,1,0:T(8,128)(2,1)S(1)}, bf16[4,256,256]{2,1,0:T(8,128)(2,1)S(1)}, f32[256,256]{1,0:T(8,128)S(1)}, f32[2,28,32,128]{3,2,1,0:T(8,128)S(1)}, f32[256,256]{1,0:T(8,128)S(1)}) custom-call(s32[1]{0:T(128)} %bitcast.1.core, ...), custom_call_target="tpu_custom_call", output_to_operand_aliasing={{3}: (1, {}), {4}: (2, {})} | custom-call | flops 1000000000 | bytes 4000000 | tf_op jit(solution)/shard_map/pallas_call | solution.py:444
  14.3 0.1 collective-permute-start.2
  14.4 0.9 %shard_map.105 = (f32[4,16,256]{2,1,0:T(8,128)S(1)}, f32[256,256]{1,0:T(8,128)S(1)}, bf16[4,256,256]{2,1,0:T(8,128)(2,1)S(1)}) custom-call(f32[2,28,32,128]{3,2,1,0:T(8,128)S(1)} %get-tuple-element.41.frame, f32[256,256]{1,0:T(8,128)S(1)} %get-tuple-element.42.dconv_in, ...), custom_call_target="tpu_custom_call", output_to_operand_aliasing={{1}: (1, {}), {2}: (2, {})} | custom-call | flops 300000000 | bytes 4000000 | tf_op jit(solution)/shard_map/pallas_call | solution.py:453
  15.3 0.9 %collective-permute-done.2.got_ref = bf16[4,256,256]{2,1,0:T(8,128)(2,1)S(1)} collective-permute-done((bf16[4,256,256]{2,1,0:T(8,128)(2,1)S(1)}, bf16[4,256,256]{2,1,0:T(8,128)(2,1)S(1)}, u32[]{:S(2)}, u32[]{:S(2)}) %collective-permute-start.2) | collective-permute-done | bytes 524320 | tf_op jit(solution)/shard_map/ppermute | solution.py:400
  16.3 0.1 shard_map.106
  16.4 1.6 %collective-permute-start.3 = (bf16[272,256]{1,0:T(8,128)(2,1)S(1)}, bf16[272,256]{1,0:T(8,128)(2,1)S(1)}, u32[]{:S(2)}, u32[]{:S(2)}) collective-permute-start(bf16[272,256]{1,0:T(8,128)(2,1)S(1)} %get-tuple-element.48), channel_id=1, source_target_pairs={{0,6},{1,25},{2,4},{3,27},{4,2},{5,29},{6,0},{7,31},{8,14},{9,17},... | collective-permute-start | bytes 417800 | tf_op jit(solution)/shard_map/ppermute | solution.py:400
  18.0 1.4 %collective-permute-start.4 = (bf16[272,256]{1,0:T(8,128)(2,1)S(1)}, bf16[272,256]{1,0:T(8,128)(2,1)S(1)}, u32[]{:S(2)}, u32[]{:S(2)}) collective-permute-start(bf16[272,256]{1,0:T(8,128)(2,1)S(1)} %get-tuple-element.49), channel_id=1, source_target_pairs={{0,4},{1,17},{2,6},{3,19},{4,0},{5,21},{6,2},{7,23},{8,12},{9,25},... | collective-permute-start | bytes 417800 | tf_op jit(solution)/shard_map/ppermute | solution.py:400
  19.4 0.5 %collective-permute-start.5 = (bf16[272,256]{1,0:T(8,128)(2,1)S(1)}, bf16[272,256]{1,0:T(8,128)(2,1)S(1)}, u32[]{:S(2)}, u32[]{:S(2)}) collective-permute-start(bf16[272,256]{1,0:T(8,128)(2,1)S(1)} %get-tuple-element.50), channel_id=1, source_target_pairs={{0,2},{1,9},{2,0},{3,11},{4,6},{5,13},{6,4},{7,15},{8,10},{9,1},{1... | collective-permute-start | bytes 417800 | tf_op jit(solution)/shard_map/ppermute | solution.py:400
  19.9 1.4 %shard_map.107 = (f32[256,256]{1,0:T(8,128)S(1)}, bf16[256,256]{1,0:T(8,128)(2,1)S(1)}, bf16[256,256]{1,0:T(8,128)(2,1)S(1)}) custom-call(bf16[448,768]{1,0:T(8,128)(2,1)S(1)} %get-tuple-element.36.onehot, f32[256,256]{1,0:T(8,128)S(1)} %get-tuple-element.51.dconv_ref, f32[49,256]{1,0:T(8,128)S(1)} %get-tuple-element.39.taps_ref, bf16[256,256]{1,0:T(8,128)(2,1)} %bitcast.8), custom_call_target="tpu_custom_call" | custom-call | flops 300000000 | bytes 4000000 | tf_op jit(solution)/shard_map/pallas_call | solution.py:469
  21.3 0.7 %collective-permute-start.9 = (bf16[256,256]{1,0:T(8,128)(2,1)S(1)}, bf16[256,256]{1,0:T(8,128)(2,1)S(1)}, u32[]{:S(2)}, u32[]{:S(2)}) collective-permute-start(bf16[256,256]{1,0:T(8,128)(2,1)S(1)} %get-tuple-element.53), channel_id=1, source_target_pairs={{0,4},{4,0},{8,12},{12,8},{16,20},{20,16},{24,28},{28,24},{1,5},{5... | collective-permute-start | bytes 393224 | tf_op jit(solution)/shard_map/ppermute | solution.py:387
  22.0 3.6 %collective-permute-start.10 = (bf16[256,256]{1,0:T(8,128)(2,1)S(1)}, bf16[256,256]{1,0:T(8,128)(2,1)S(1)}, u32[]{:S(2)}, u32[]{:S(2)}) collective-permute-start(bf16[256,256]{1,0:T(8,128)(2,1)S(1)} %get-tuple-element.56), channel_id=1, source_target_pairs={{0,28},{4,8},{8,4},{12,16},{16,12},{20,24},{24,20},{28,0},{1,29},{... | collective-permute-start | bytes 393224 | tf_op jit(solution)/shard_map/ppermute | solution.py:391
  25.6 0.0 collective-permute-done.3
  25.6 0.0 collective-permute-done.4
  25.6 0.0 collective-permute-done.5
  25.6 0.1 add_convert_fusion.1
  25.7 1.7 %collective-permute-start.8 = (bf16[272,256]{1,0:T(8,128)(2,1)S(1)}, bf16[272,256]{1,0:T(8,128)(2,1)S(1)}, u32[]{:S(2)}, u32[]{:S(2)}) collective-permute-start(bf16[272,256]{1,0:T(8,128)(2,1)S(1)} %add_convert_fusion.1), channel_id=1, source_target_pairs={{0,24},{1,7},{2,26},{3,5},{4,28},{5,3},{6,30},{7,1},{8,16},{9,15},... | collective-permute-start | bytes 417800 | tf_op jit(solution)/shard_map/ppermute | solution.py:400
  27.4 0.0 collective-permute-start.7
  27.4 2.8 %collective-permute-start.6 = (bf16[272,256]{1,0:T(8,128)(2,1)S(1)}, bf16[272,256]{1,0:T(8,128)(2,1)S(1)}, u32[]{:S(2)}, u32[]{:S(2)}) collective-permute-start(bf16[272,256]{1,0:T(8,128)(2,1)S(1)} %add_convert_fusion.1), channel_id=1, source_target_pairs={{0,8},{1,3},{2,10},{3,1},{4,12},{5,7},{6,14},{7,5},{8,0},{9,11},{1... | collective-permute-start | bytes 417800 | tf_op jit(solution)/shard_map/ppermute | solution.py:400
  30.1 0.0 collective-permute-done.9.other_ref
  30.2 2.6 %collective-permute-done.8 = bf16[272,256]{1,0:T(8,128)(2,1)S(1)} collective-permute-done((bf16[272,256]{1,0:T(8,128)(2,1)S(1)}, bf16[272,256]{1,0:T(8,128)(2,1)S(1)}, u32[]{:S(2)}, u32[]{:S(2)}) %collective-permute-start.8) | collective-permute-done | bytes 139296 | tf_op jit(solution)/shard_map/ppermute | solution.py:400
  32.8 2.8 %collective-permute-done.7 = bf16[272,256]{1,0:T(8,128)(2,1)S(1)} collective-permute-done((bf16[272,256]{1,0:T(8,128)(2,1)S(1)}, bf16[272,256]{1,0:T(8,128)(2,1)S(1)}, u32[]{:S(2)}, u32[]{:S(2)}) %collective-permute-start.7) | collective-permute-done | bytes 139296 | tf_op jit(solution)/shard_map/ppermute | solution.py:400
  35.6 0.0 collective-permute-done.6
  35.6 0.1 add_convert_fusion.refs_0_.refs_4_
  35.7 2.1 %collective-permute-start.16 = (bf16[272,256]{1,0:T(8,128)(2,1)S(1)}, bf16[272,256]{1,0:T(8,128)(2,1)S(1)}, u32[]{:S(2)}, u32[]{:S(2)}) collective-permute-start(bf16[272,256]{1,0:T(8,128)(2,1)S(1)} %add_convert_fusion.refs_0_.refs_4_), channel_id=1, source_target_pairs={{0,6},{1,25},{2,4},{3,27},{4,2},{5,29},{6,0},{7,31},{8,14},{9,17},... | collective-permute-start | bytes 417800 | tf_op jit(solution)/shard_map/ppermute | solution.py:400
  37.7 1.0 %collective-permute-start.14 = (bf16[272,256]{1,0:T(8,128)(2,1)S(1)}, bf16[272,256]{1,0:T(8,128)(2,1)S(1)}, u32[]{:S(2)}, u32[]{:S(2)}) collective-permute-start(bf16[272,256]{1,0:T(8,128)(2,1)S(1)} %add_convert_fusion.refs_0_.refs_4_), channel_id=1, source_target_pairs={{0,4},{1,17},{2,6},{3,19},{4,0},{5,21},{6,2},{7,23},{8,12},{9,25},... | collective-permute-start | bytes 417800 | tf_op jit(solution)/shard_map/ppermute | solution.py:400
  38.7 0.5 %collective-permute-start.12 = (bf16[272,256]{1,0:T(8,128)(2,1)S(1)}, bf16[272,256]{1,0:T(8,128)(2,1)S(1)}, u32[]{:S(2)}, u32[]{:S(2)}) collective-permute-start(bf16[272,256]{1,0:T(8,128)(2,1)S(1)} %add_convert_fusion.refs_0_.refs_4_), channel_id=1, source_target_pairs={{0,2},{1,9},{2,0},{3,11},{4,6},{5,13},{6,4},{7,15},{8,10},{9,1},{1... | collective-permute-start | bytes 417800 | tf_op jit(solution)/shard_map/ppermute | solution.py:400
  39.2 0.0 collective-permute-done.10.other_ref
  39.2 0.7 %shard_map.109 = bf16[256,256]{1,0:T(8,128)(2,1)} custom-call(f32[256,256]{1,0:T(8,128)S(1)} %shard_map.108.own_ref, bf16[256,256]{1,0:T(8,128)(2,1)S(1)} %collective-permute-done.10.other_ref), custom_call_target="tpu_custom_call" | custom-call | flops 30000001024 | bytes 4000000 | tf_op jit(solution)/shard_map/pallas_call | solution.py:497
  39.9 0.0 collective-permute-start.11
  39.9 1.8 %collective-permute-done.16.refs_3_.refs_7_ = bf16[272,256]{1,0:T(8,128)(2,1)S(1)} collective-permute-done((bf16[272,256]{1,0:T(8,128)(2,1)S(1)}, bf16[272,256]{1,0:T(8,128)(2,1)S(1)}, u32[]{:S(2)}, u32[]{:S(2)}) %collective-permute-start.16) | collective-permute-done | bytes 139296 | tf_op jit(solution)/shard_map/ppermute | solution.py:400
  41.7 0.0 collective-permute-start.17
  41.7 1.5 %collective-permute-done.14.refs_2_.refs_6_ = bf16[272,256]{1,0:T(8,128)(2,1)S(1)} collective-permute-done((bf16[272,256]{1,0:T(8,128)(2,1)S(1)}, bf16[272,256]{1,0:T(8,128)(2,1)S(1)}, u32[]{:S(2)}, u32[]{:S(2)}) %collective-permute-start.14) | collective-permute-done | bytes 139296 | tf_op jit(solution)/shard_map/ppermute | solution.py:400
  43.2 0.0 collective-permute-start.15
  43.2 0.5 %collective-permute-done.12.refs_1_.refs_5_ = bf16[272,256]{1,0:T(8,128)(2,1)S(1)} collective-permute-done((bf16[272,256]{1,0:T(8,128)(2,1)S(1)}, bf16[272,256]{1,0:T(8,128)(2,1)S(1)}, u32[]{:S(2)}, u32[]{:S(2)}) %collective-permute-start.12) | collective-permute-done | bytes 139296 | tf_op jit(solution)/shard_map/ppermute | solution.py:400
  43.8 0.0 collective-permute-start.13
  43.8 1.0 %shard_map.110 = (f32[256,1024]{1,0:T(8,128)}, f32[1024,256]{1,0:T(8,128)}) custom-call(s32[1]{0:T(128)} %bitcast.1.core, s32[1]{0:T(128)} %bitcast.place.mine_at, s32[1]{0:T(128)} %bitcast.6.theirs_at, bf16[272,256]{1,0:T(8,128)(2,1)S(1)} %add_convert_fusion.refs_0_.refs_4_, bf16[272,256]{1,0:T(8,128)(2,1)S(1)} %collective-permute-done.12.refs_1_.refs_5_, ...), custom_call_target="tpu_custom_call" | custom-call | flops 300000000 | bytes 4000000 | tf_op jit(solution)/shard_map/pallas_call | solution.py:509
  44.8 0.0 collective-permute-done.11.refs_0_.refs_8_
  44.8 0.0 collective-permute-done.17.refs_3_.refs_11_
  44.8 0.0 collective-permute-done.15.refs_2_.refs_10_
  44.8 0.3 collective-permute-done.13.refs_1_.refs_9_
  45.1 1.1 %shard_map.111 = (f32[256,1024]{1,0:T(8,128)}, f32[1024,256]{1,0:T(8,128)}, f32[49,256]{1,0:T(8,128)}) custom-call(s32[1]{0:T(128)} %bitcast.1.core, s32[1]{0:T(128)} %bitcast.place.mine_at, s32[1]{0:T(128)} %bitcast.6.theirs_at, bf16[272,256]{1,0:T(8,128)(2,1)S(1)} %collective-permute-done.11.refs_0_.refs_8_, ...), custom_call_target="tpu_custom_call", output_to_operand_aliasing={{0}: (15, {}), {1}: (16, {})} | custom-call | flops 300000000 | bytes 4000000 | tf_op jit(solution)/shard_map/pallas_call | solution.py:509
  (1 shorter events, 0.0 us)
Async XLA Ops:
  0.6 10.5 %collective-permute-start = (bf16[256,256]{1,0:T(8,128)(2,1)}, bf16[256,256]{1,0:T(8,128)(2,1)S(1)}, u32[]{:S(2)}, u32[]{:S(2)}) collective-permute-start(bf16[256,256]{1,0:T(8,128)(2,1)} %bitcast.9), channel_id=1, source_target_pairs={{0,4},{4,0},{8,12},{12,8},{16,20},{20,16},{24,28},{28,24},{1,5},{5... | collective-permute-start | bytes 393224 | tf_op jit(solution)/shard_map/ppermute | solution.py:387
  3.6 7.9 %collective-permute-start.1 = (bf16[256,256]{1,0:T(8,128)(2,1)}, bf16[256,256]{1,0:T(8,128)(2,1)S(1)}, u32[]{:S(2)}, u32[]{:S(2)}) collective-permute-start(bf16[256,256]{1,0:T(8,128)(2,1)} %bitcast.10), channel_id=1, source_target_pairs={{0,28},{4,8},{8,4},{12,16},{16,12},{20,24},{24,20},{28,0},{1,29},{... | collective-permute-start | bytes 393224 | tf_op jit(solution)/shard_map/ppermute | solution.py:391
  7.2 0.7 %copy-start = (s32[1,4]{1,0:T(1,128)S(1)}, s32[1,4]{1,0:T(1,128)}, u32[]{:S(2)}) copy-start(s32[1,4]{1,0:T(1,128)} %neighbour.1) | copy-start | bytes 52
  7.2 0.7 %copy-start.1 = (s32[1,4]{1,0:T(1,128)S(1)}, s32[1,4]{1,0:T(1,128)}, u32[]{:S(2)}) copy-start(s32[1,4]{1,0:T(1,128)} %code.1) | copy-start | bytes 52
  14.3 2.0 %collective-permute-start.2 = (bf16[4,256,256]{2,1,0:T(8,128)(2,1)S(1)}, bf16[4,256,256]{2,1,0:T(8,128)(2,1)S(1)}, u32[]{:S(2)}, u32[]{:S(2)}) collective-permute-start(bf16[4,256,256]{2,1,0:T(8,128)(2,1)S(1)} %get-tuple-element.45), channel_id=1, source_target_pairs={{0,1},{1,0},{2,3},{3,2},{4,5},{5,4},{6,7},{7,6},{8,9},{9,8},{10,11... | collective-permute-start | bytes 1572872 | tf_op jit(solution)/shard_map/ppermute | solution.py:400
  16.4 9.2 %collective-permute-start.3 = (bf16[272,256]{1,0:T(8,128)(2,1)S(1)}, bf16[272,256]{1,0:T(8,128)(2,1)S(1)}, u32[]{:S(2)}, u32[]{:S(2)}) collective-permute-start(bf16[272,256]{1,0:T(8,128)(2,1)S(1)} %get-tuple-element.48), channel_id=1, source_target_pairs={{0,6},{1,25},{2,4},{3,27},{4,2},{5,29},{6,0},{7,31},{8,14},{9,17},... | collective-permute-start | bytes 417800 | tf_op jit(solution)/shard_map/ppermute | solution.py:400
  18.0 7.6 %collective-permute-start.4 = (bf16[272,256]{1,0:T(8,128)(2,1)S(1)}, bf16[272,256]{1,0:T(8,128)(2,1)S(1)}, u32[]{:S(2)}, u32[]{:S(2)}) collective-permute-start(bf16[272,256]{1,0:T(8,128)(2,1)S(1)} %get-tuple-element.49), channel_id=1, source_target_pairs={{0,4},{1,17},{2,6},{3,19},{4,0},{5,21},{6,2},{7,23},{8,12},{9,25},... | collective-permute-start | bytes 417800 | tf_op jit(solution)/shard_map/ppermute | solution.py:400
  19.4 6.2 %collective-permute-start.5 = (bf16[272,256]{1,0:T(8,128)(2,1)S(1)}, bf16[272,256]{1,0:T(8,128)(2,1)S(1)}, u32[]{:S(2)}, u32[]{:S(2)}) collective-permute-start(bf16[272,256]{1,0:T(8,128)(2,1)S(1)} %get-tuple-element.50), channel_id=1, source_target_pairs={{0,2},{1,9},{2,0},{3,11},{4,6},{5,13},{6,4},{7,15},{8,10},{9,1},{1... | collective-permute-start | bytes 417800 | tf_op jit(solution)/shard_map/ppermute | solution.py:400
  21.3 8.8 %collective-permute-start.9 = (bf16[256,256]{1,0:T(8,128)(2,1)S(1)}, bf16[256,256]{1,0:T(8,128)(2,1)S(1)}, u32[]{:S(2)}, u32[]{:S(2)}) collective-permute-start(bf16[256,256]{1,0:T(8,128)(2,1)S(1)} %get-tuple-element.53), channel_id=1, source_target_pairs={{0,4},{4,0},{8,12},{12,8},{16,20},{20,16},{24,28},{28,24},{1,5},{5... | collective-permute-start | bytes 393224 | tf_op jit(solution)/shard_map/ppermute | solution.py:387
  22.0 17.2 %collective-permute-start.10 = (bf16[256,256]{1,0:T(8,128)(2,1)S(1)}, bf16[256,256]{1,0:T(8,128)(2,1)S(1)}, u32[]{:S(2)}, u32[]{:S(2)}) collective-permute-start(bf16[256,256]{1,0:T(8,128)(2,1)S(1)} %get-tuple-element.56), channel_id=1, source_target_pairs={{0,28},{4,8},{8,4},{12,16},{16,12},{20,24},{24,20},{28,0},{1,29},{... | collective-permute-start | bytes 393224 | tf_op jit(solution)/shard_map/ppermute | solution.py:391
  25.7 7.1 %collective-permute-start.8 = (bf16[272,256]{1,0:T(8,128)(2,1)S(1)}, bf16[272,256]{1,0:T(8,128)(2,1)S(1)}, u32[]{:S(2)}, u32[]{:S(2)}) collective-permute-start(bf16[272,256]{1,0:T(8,128)(2,1)S(1)} %add_convert_fusion.1), channel_id=1, source_target_pairs={{0,24},{1,7},{2,26},{3,5},{4,28},{5,3},{6,30},{7,1},{8,16},{9,15},... | collective-permute-start | bytes 417800 | tf_op jit(solution)/shard_map/ppermute | solution.py:400
  27.4 8.2 %collective-permute-start.7 = (bf16[272,256]{1,0:T(8,128)(2,1)S(1)}, bf16[272,256]{1,0:T(8,128)(2,1)S(1)}, u32[]{:S(2)}, u32[]{:S(2)}) collective-permute-start(bf16[272,256]{1,0:T(8,128)(2,1)S(1)} %add_convert_fusion.1), channel_id=1, source_target_pairs={{0,16},{1,5},{2,18},{3,7},{4,20},{5,1},{6,22},{7,3},{8,24},{9,13},... | collective-permute-start | bytes 417800 | tf_op jit(solution)/shard_map/ppermute | solution.py:400
  27.4 8.2 %collective-permute-start.6 = (bf16[272,256]{1,0:T(8,128)(2,1)S(1)}, bf16[272,256]{1,0:T(8,128)(2,1)S(1)}, u32[]{:S(2)}, u32[]{:S(2)}) collective-permute-start(bf16[272,256]{1,0:T(8,128)(2,1)S(1)} %add_convert_fusion.1), channel_id=1, source_target_pairs={{0,8},{1,3},{2,10},{3,1},{4,12},{5,7},{6,14},{7,5},{8,0},{9,11},{1... | collective-permute-start | bytes 417800 | tf_op jit(solution)/shard_map/ppermute | solution.py:400
  35.7 6.0 %collective-permute-start.16 = (bf16[272,256]{1,0:T(8,128)(2,1)S(1)}, bf16[272,256]{1,0:T(8,128)(2,1)S(1)}, u32[]{:S(2)}, u32[]{:S(2)}) collective-permute-start(bf16[272,256]{1,0:T(8,128)(2,1)S(1)} %add_convert_fusion.refs_0_.refs_4_), channel_id=1, source_target_pairs={{0,6},{1,25},{2,4},{3,27},{4,2},{5,29},{6,0},{7,31},{8,14},{9,17},... | collective-permute-start | bytes 417800 | tf_op jit(solution)/shard_map/ppermute | solution.py:400
  37.7 5.5 %collective-permute-start.14 = (bf16[272,256]{1,0:T(8,128)(2,1)S(1)}, bf16[272,256]{1,0:T(8,128)(2,1)S(1)}, u32[]{:S(2)}, u32[]{:S(2)}) collective-permute-start(bf16[272,256]{1,0:T(8,128)(2,1)S(1)} %add_convert_fusion.refs_0_.refs_4_), channel_id=1, source_target_pairs={{0,4},{1,17},{2,6},{3,19},{4,0},{5,21},{6,2},{7,23},{8,12},{9,25},... | collective-permute-start | bytes 417800 | tf_op jit(solution)/shard_map/ppermute | solution.py:400
  38.7 5.1 %collective-permute-start.12 = (bf16[272,256]{1,0:T(8,128)(2,1)S(1)}, bf16[272,256]{1,0:T(8,128)(2,1)S(1)}, u32[]{:S(2)}, u32[]{:S(2)}) collective-permute-start(bf16[272,256]{1,0:T(8,128)(2,1)S(1)} %add_convert_fusion.refs_0_.refs_4_), channel_id=1, source_target_pairs={{0,2},{1,9},{2,0},{3,11},{4,6},{5,13},{6,4},{7,15},{8,10},{9,1},{1... | collective-permute-start | bytes 417800 | tf_op jit(solution)/shard_map/ppermute | solution.py:400
  39.9 4.9 %collective-permute-start.11 = (bf16[272,256]{1,0:T(8,128)(2,1)S(1)}, bf16[272,256]{1,0:T(8,128)(2,1)S(1)}, u32[]{:S(2)}, u32[]{:S(2)}) collective-permute-start(bf16[272,256]{1,0:T(8,128)(2,1)S(1)} %add_convert_fusion.refs_0_.refs_4_), channel_id=1, source_target_pairs={{0,1},{1,0},{2,3},{3,2},{4,5},{5,4},{6,7},{7,6},{8,9},{9,8},{10,11... | collective-permute-start | bytes 417800 | tf_op jit(solution)/shard_map/ppermute | solution.py:400
  41.7 3.1 %collective-permute-start.17 = (bf16[272,256]{1,0:T(8,128)(2,1)S(1)}, bf16[272,256]{1,0:T(8,128)(2,1)S(1)}, u32[]{:S(2)}, u32[]{:S(2)}) collective-permute-start(bf16[272,256]{1,0:T(8,128)(2,1)S(1)} %collective-permute-done.16.refs_3_.refs_7_), channel_id=1, source_target_pairs={{0,1},{1,0},{2,3},{3,2},{4,5},{5,4},{6,7},{7,6},{8,9},{9,8},{10,11... | collective-permute-start | bytes 417800 | tf_op jit(solution)/shard_map/ppermute | solution.py:400
  43.2 1.6 %collective-permute-start.15 = (bf16[272,256]{1,0:T(8,128)(2,1)S(1)}, bf16[272,256]{1,0:T(8,128)(2,1)S(1)}, u32[]{:S(2)}, u32[]{:S(2)}) collective-permute-start(bf16[272,256]{1,0:T(8,128)(2,1)S(1)} %collective-permute-done.14.refs_2_.refs_6_), channel_id=1, source_target_pairs={{0,1},{1,0},{2,3},{3,2},{4,5},{5,4},{6,7},{7,6},{8,9},{9,8},{10,11... | collective-permute-start | bytes 417800 | tf_op jit(solution)/shard_map/ppermute | solution.py:400
  43.8 1.4 %collective-permute-start.13 = (bf16[272,256]{1,0:T(8,128)(2,1)S(1)}, bf16[272,256]{1,0:T(8,128)(2,1)S(1)}, u32[]{:S(2)}, u32[]{:S(2)}) collective-permute-start(bf16[272,256]{1,0:T(8,128)(2,1)S(1)} %collective-permute-done.12.refs_1_.refs_5_), channel_id=1, source_target_pairs={{0,1},{1,0},{2,3},{3,2},{4,5},{5,4},{6,7},{7,6},{8,9},{9,8},{10,11... | collective-permute-start | bytes 417800 | tf_op jit(solution)/shard_map/ppermute | solution.py:400

commit v6 on v5

--- a/solution.py
+++ b/solution.py
@@ -348,8 +348,8 @@
         pl.when(jnp.logical_not(to_in))(into_out.wait)
 
 
-def join_kernel(own_ref, other_ref, out_ref):
-    out_ref[...] = (own_ref[...] + other_ref[...].astype(F32)).astype(out_ref.dtype)
+def join_kernel(own_ref, one_ref, two_ref, out_ref):
+    out_ref[...] = (own_ref[...] + one_ref[...].astype(F32) + two_ref[...].astype(F32)).astype(BF16)
 
 
 def in_hbm(x):
@@ -488,15 +488,11 @@
         if len(even) == 3:
             summed = summed + (got[2] + got[3])
         total = summed.astype(BF16)
-    joined = call(
-        join_kernel, pltpu.VMEM((N * N, C), F32), (), [VMEM] * 2, flops=JOIN_COST
-    )(grad_own, back_one)
-    total, joined = lax.optimization_barrier((total, joined))
     mine = {d: swap(total, combos[0][d - 1], combos[1][d - 1]) for d in reversed(STARTS[2])}
     mine = [total, mine[1], mine[2], mine[3]]
     grad_features = call(
-        join_kernel, struct((N * N, C), BF16), (), [VMEM] * 2, flops=JOIN_COST
-    )(joined, back_two)
+        join_kernel, struct((N * N, C), BF16), (), [VMEM] * 3, flops=JOIN_COST
+    )(grad_own, back_one, back_two)
     mine[0], grad_features = lax.optimization_barrier((mine[0], grad_features))
     theirs = [swap(x, 1, 1) for x in mine]
     grads = (struct((C, HID), F32), struct((HID, C), F32))

time: 46.4 us -> 45.8 us (0.987)
  waiting for transfers between devices: 10.7 us -> 9.58 us
  starting transfers between devices: 22.5 us -> 23.1 us
    ppermute x14, waiting for transfers between devices: 10.5 us -> 7.86 us  [swap(): lax.ppermute(x, both, [(i, i ^ (odd if i % 2 else even)) for i in range(d...]
    ppermute x2, waiting for transfers between devices: 0.18 us -> 1.71 us  [two_over(): return lax.ppermute(x, 'tile', moves)]
    ppermute x14, starting transfers between devices: 11.6 us -> 12.2 us  [swap(): lax.ppermute(x, both, [(i, i ^ (odd if i % 2 else even)) for i in range(d...]
  transfers between devices with their start and end apart: 18 -> 18, of which waited for: 8 -> 11; matrix products, arithmetic and copies ran while one was open for 0% -> 0% of each run, Pallas kernels for 16% -> 16%
where the time goes in v6:
time: 45.8 us; the launch traced here: 45.7 us
  starting transfers between devices  23.1 us (50%)
  Pallas kernels  11.4 us (25%)
  waiting for transfers between devices  9.58 us (21%)
  between operations  0.78 us (2%)
  local copies, waits for them, and re-layouts  0.67 us (1%)
    ppermute x14, starting transfers between devices, swap(): lax.ppermute(x, both, [(i, i ^ (odd if i % 2 else even)) for i in range(d...  12.2 us
    ppermute x14, waiting for transfers between devices, swap(): lax.ppermute(x, both, [(i, i ^ (odd if i % 2 else even)) for i in range(d...  7.86 us
    ppermute x2, starting transfers between devices, two_over(): return lax.ppermute(x, 'tile', moves)  7.14 us
    ppermute x2, starting transfers between devices, one_over(): return lax.ppermute(x, 'tile', [(i, i ^ 1) for i in range(owners)])  3.69 us
    pallas_call x1, Pallas kernels, body(): call(functools.partial(prepare_kernel, owners), (pltpu.VMEM((SIDE_CELLS,...  3.21 us
    pallas_call x1, Pallas kernels, body(): call(forward_kernel, (half, half, cells, frame, cells), [frame], [SMEM] +...  2.76 us
    pallas_call x2, Pallas kernels, store(): call(functools.partial(store_kernel, scale, picks, len(given), last), (*g...  2.08 us
    ppermute x2, waiting for transfers between devices, two_over(): return lax.ppermute(x, 'tile', moves)  1.71 us
  transfers between devices with their start and end apart: 18, of which 11 were waited for; matrix products, arithmetic and copies ran while one was open for 0% of the time, Pallas kernels for 16%

profile of v6, /device:TPU:0, one launch (start us, length us, event | category | flops | bytes accessed | tf_op | source)
XLA Modules:
  0.0 45.7 jit_solution(4424855090781128617)
XLA Ops:
  0.6 3.0 %collective-permute-start = (bf16[256,256]{1,0:T(8,128)(2,1)}, bf16[256,256]{1,0:T(8,128)(2,1)S(1)}, u32[]{:S(2)}, u32[]{:S(2)}) collective-permute-start(bf16[256,256]{1,0:T(8,128)(2,1)} %bitcast.9), channel_id=1, source_target_pairs={{0,4},{4,0},{8,12},{12,8},{16,20},{20,16},{24,28},{28,24},{1,5},{5... | collective-permute-start | bytes 393224 | tf_op jit(solution)/shard_map/ppermute | solution.py:387
  3.6 3.6 %collective-permute-start.1 = (bf16[256,256]{1,0:T(8,128)(2,1)}, bf16[256,256]{1,0:T(8,128)(2,1)S(1)}, u32[]{:S(2)}, u32[]{:S(2)}) collective-permute-start(bf16[256,256]{1,0:T(8,128)(2,1)} %bitcast.10), channel_id=1, source_target_pairs={{0,28},{4,8},{8,4},{12,16},{16,12},{20,24},{24,20},{28,0},{1,29},{... | collective-permute-start | bytes 393224 | tf_op jit(solution)/shard_map/ppermute | solution.py:391
  7.2 0.0 copy-start
  7.2 0.0 copy-start.1
  7.2 0.7 %copy-done = s32[1,4]{1,0:T(1,128)S(1)} copy-done((s32[1,4]{1,0:T(1,128)S(1)}, s32[1,4]{1,0:T(1,128)}, u32[]{:S(2)}) %copy-start) | copy-done | bytes 40
  7.9 0.0 copy-done.1
  7.9 3.2 %shard_map.102 = (bf16[448,768]{1,0:T(8,128)(2,1)S(1)}, f32[2,28,32,128]{3,2,1,0:T(8,128)S(1)}, f32[256,256]{1,0:T(8,128)S(1)}, f32[256,1024]{1,0:T(8,128)S(1)},...) custom-call(s32[1]{0:T(128)} %bitcast.2.position, s32[1,4]{1,0:T(1,128)S(1)} %copy-done, ...), custom_call_target="tpu_custom_call" | custom-call | flops 300000000 | bytes 4000000 | tf_op jit(solution)/shard_map/pallas_call | solution.py:419
  11.1 0.0 collective-permute-done.one_ref
  11.1 0.2 shard_map.103.rims_ref
  11.3 0.2 collective-permute-done.1.two_ref
  11.5 2.8 %shard_map.104 = (bf16[4,256,256]{2,1,0:T(8,128)(2,1)S(1)}, bf16[4,256,256]{2,1,0:T(8,128)(2,1)S(1)}, f32[256,256]{1,0:T(8,128)S(1)}, f32[2,28,32,128]{3,2,1,0:T(8,128)S(1)}, f32[256,256]{1,0:T(8,128)S(1)}) custom-call(s32[1]{0:T(128)} %bitcast.1.core, ...), custom_call_target="tpu_custom_call", output_to_operand_aliasing={{3}: (1, {}), {4}: (2, {})} | custom-call | flops 1000000000 | bytes 4000000 | tf_op jit(solution)/shard_map/pallas_call | solution.py:444
  14.3 0.1 collective-permute-start.2
  14.4 0.9 %shard_map.105 = (f32[4,16,256]{2,1,0:T(8,128)S(1)}, f32[256,256]{1,0:T(8,128)S(1)}, bf16[4,256,256]{2,1,0:T(8,128)(2,1)S(1)}) custom-call(f32[2,28,32,128]{3,2,1,0:T(8,128)S(1)} %get-tuple-element.39.frame, f32[256,256]{1,0:T(8,128)S(1)} %get-tuple-element.40.dconv_in, ...), custom_call_target="tpu_custom_call", output_to_operand_aliasing={{1}: (1, {}), {2}: (2, {})} | custom-call | flops 300000000 | bytes 4000000 | tf_op jit(solution)/shard_map/pallas_call | solution.py:453
  15.3 0.9 %collective-permute-done.2.got_ref = bf16[4,256,256]{2,1,0:T(8,128)(2,1)S(1)} collective-permute-done((bf16[4,256,256]{2,1,0:T(8,128)(2,1)S(1)}, bf16[4,256,256]{2,1,0:T(8,128)(2,1)S(1)}, u32[]{:S(2)}, u32[]{:S(2)}) %collective-permute-start.2) | collective-permute-done | bytes 524320 | tf_op jit(solution)/shard_map/ppermute | solution.py:400
  16.3 0.1 shard_map.106
  16.4 1.6 %collective-permute-start.3 = (bf16[272,256]{1,0:T(8,128)(2,1)S(1)}, bf16[272,256]{1,0:T(8,128)(2,1)S(1)}, u32[]{:S(2)}, u32[]{:S(2)}) collective-permute-start(bf16[272,256]{1,0:T(8,128)(2,1)S(1)} %get-tuple-element.46), channel_id=1, source_target_pairs={{0,6},{1,25},{2,4},{3,27},{4,2},{5,29},{6,0},{7,31},{8,14},{9,17},... | collective-permute-start | bytes 417800 | tf_op jit(solution)/shard_map/ppermute | solution.py:400
  18.0 1.4 %collective-permute-start.4 = (bf16[272,256]{1,0:T(8,128)(2,1)S(1)}, bf16[272,256]{1,0:T(8,128)(2,1)S(1)}, u32[]{:S(2)}, u32[]{:S(2)}) collective-permute-start(bf16[272,256]{1,0:T(8,128)(2,1)S(1)} %get-tuple-element.47), channel_id=1, source_target_pairs={{0,4},{1,17},{2,6},{3,19},{4,0},{5,21},{6,2},{7,23},{8,12},{9,25},... | collective-permute-start | bytes 417800 | tf_op jit(solution)/shard_map/ppermute | solution.py:400
  19.4 0.5 %collective-permute-start.5 = (bf16[272,256]{1,0:T(8,128)(2,1)S(1)}, bf16[272,256]{1,0:T(8,128)(2,1)S(1)}, u32[]{:S(2)}, u32[]{:S(2)}) collective-permute-start(bf16[272,256]{1,0:T(8,128)(2,1)S(1)} %get-tuple-element.48), channel_id=1, source_target_pairs={{0,2},{1,9},{2,0},{3,11},{4,6},{5,13},{6,4},{7,15},{8,10},{9,1},{1... | collective-permute-start | bytes 417800 | tf_op jit(solution)/shard_map/ppermute | solution.py:400
  19.9 2.5 %collective-permute-done.3 = bf16[272,256]{1,0:T(8,128)(2,1)S(1)} collective-permute-done((bf16[272,256]{1,0:T(8,128)(2,1)S(1)}, bf16[272,256]{1,0:T(8,128)(2,1)S(1)}, u32[]{:S(2)}, u32[]{:S(2)}) %collective-permute-start.3) | collective-permute-done | bytes 139296 | tf_op jit(solution)/shard_map/ppermute | solution.py:400
  22.4 1.6 %collective-permute-done.4 = bf16[272,256]{1,0:T(8,128)(2,1)S(1)} collective-permute-done((bf16[272,256]{1,0:T(8,128)(2,1)S(1)}, bf16[272,256]{1,0:T(8,128)(2,1)S(1)}, u32[]{:S(2)}, u32[]{:S(2)}) %collective-permute-start.4) | collective-permute-done | bytes 139296 | tf_op jit(solution)/shard_map/ppermute | solution.py:400
  24.0 0.5 %collective-permute-done.5 = bf16[272,256]{1,0:T(8,128)(2,1)S(1)} collective-permute-done((bf16[272,256]{1,0:T(8,128)(2,1)S(1)}, bf16[272,256]{1,0:T(8,128)(2,1)S(1)}, u32[]{:S(2)}, u32[]{:S(2)}) %collective-permute-start.5) | collective-permute-done | bytes 139296 | tf_op jit(solution)/shard_map/ppermute | solution.py:400
  24.5 0.1 add_convert_fusion.1
  24.6 2.8 %collective-permute-start.8 = (bf16[272,256]{1,0:T(8,128)(2,1)S(1)}, bf16[272,256]{1,0:T(8,128)(2,1)S(1)}, u32[]{:S(2)}, u32[]{:S(2)}) collective-permute-start(bf16[272,256]{1,0:T(8,128)(2,1)S(1)} %add_convert_fusion.1), channel_id=1, source_target_pairs={{0,24},{1,7},{2,26},{3,5},{4,28},{5,3},{6,30},{7,1},{8,16},{9,15},... | collective-permute-start | bytes 417800 | tf_op jit(solution)/shard_map/ppermute | solution.py:400
  27.4 0.0 collective-permute-start.7
  27.4 1.7 %collective-permute-start.6 = (bf16[272,256]{1,0:T(8,128)(2,1)S(1)}, bf16[272,256]{1,0:T(8,128)(2,1)S(1)}, u32[]{:S(2)}, u32[]{:S(2)}) collective-permute-start(bf16[272,256]{1,0:T(8,128)(2,1)S(1)} %add_convert_fusion.1), channel_id=1, source_target_pairs={{0,8},{1,3},{2,10},{3,1},{4,12},{5,7},{6,14},{7,5},{8,0},{9,11},{1... | collective-permute-start | bytes 417800 | tf_op jit(solution)/shard_map/ppermute | solution.py:400
  29.0 1.4 %shard_map.107 = (f32[256,256]{1,0:T(8,128)S(1)}, bf16[256,256]{1,0:T(8,128)(2,1)S(1)}, bf16[256,256]{1,0:T(8,128)(2,1)S(1)}) custom-call(bf16[448,768]{1,0:T(8,128)(2,1)S(1)} %get-tuple-element.34.onehot, f32[256,256]{1,0:T(8,128)S(1)} %get-tuple-element.49.dconv_ref, f32[49,256]{1,0:T(8,128)S(1)} %get-tuple-element.37.taps_ref, bf16[256,256]{1,0:T(8,128)(2,1)} %bitcast.8), custom_call_target="tpu_custom_call" | custom-call | flops 300000000 | bytes 4000000 | tf_op jit(solution)/shard_map/pallas_call | solution.py:469
  30.4 0.7 %collective-permute-start.9 = (bf16[256,256]{1,0:T(8,128)(2,1)S(1)}, bf16[256,256]{1,0:T(8,128)(2,1)S(1)}, u32[]{:S(2)}, u32[]{:S(2)}) collective-permute-start(bf16[256,256]{1,0:T(8,128)(2,1)S(1)} %get-tuple-element.51), channel_id=1, source_target_pairs={{0,4},{4,0},{8,12},{12,8},{16,20},{20,16},{24,28},{28,24},{1,5},{5... | collective-permute-start | bytes 393224 | tf_op jit(solution)/shard_map/ppermute | solution.py:387
  31.1 3.6 %collective-permute-start.10 = (bf16[256,256]{1,0:T(8,128)(2,1)S(1)}, bf16[256,256]{1,0:T(8,128)(2,1)S(1)}, u32[]{:S(2)}, u32[]{:S(2)}) collective-permute-start(bf16[256,256]{1,0:T(8,128)(2,1)S(1)} %get-tuple-element.52), channel_id=1, source_target_pairs={{0,28},{4,8},{8,4},{12,16},{16,12},{20,24},{24,20},{28,0},{1,29},{... | collective-permute-start | bytes 393224 | tf_op jit(solution)/shard_map/ppermute | solution.py:391
  34.7 0.0 collective-permute-done.8
  34.7 0.5 %collective-permute-done.7 = bf16[272,256]{1,0:T(8,128)(2,1)S(1)} collective-permute-done((bf16[272,256]{1,0:T(8,128)(2,1)S(1)}, bf16[272,256]{1,0:T(8,128)(2,1)S(1)}, u32[]{:S(2)}, u32[]{:S(2)}) %collective-permute-start.7) | collective-permute-done | bytes 139296 | tf_op jit(solution)/shard_map/ppermute | solution.py:400
  35.2 0.0 collective-permute-done.6
  35.2 0.1 add_convert_fusion.refs_0_.refs_4_
  35.2 1.1 %collective-permute-start.16 = (bf16[272,256]{1,0:T(8,128)(2,1)S(1)}, bf16[272,256]{1,0:T(8,128)(2,1)S(1)}, u32[]{:S(2)}, u32[]{:S(2)}) collective-permute-start(bf16[272,256]{1,0:T(8,128)(2,1)S(1)} %add_convert_fusion.refs_0_.refs_4_), channel_id=1, source_target_pairs={{0,6},{1,25},{2,4},{3,27},{4,2},{5,29},{6,0},{7,31},{8,14},{9,17},... | collective-permute-start | bytes 417800 | tf_op jit(solution)/shard_map/ppermute | solution.py:400
  36.3 0.9 %collective-permute-start.14 = (bf16[272,256]{1,0:T(8,128)(2,1)S(1)}, bf16[272,256]{1,0:T(8,128)(2,1)S(1)}, u32[]{:S(2)}, u32[]{:S(2)}) collective-permute-start(bf16[272,256]{1,0:T(8,128)(2,1)S(1)} %add_convert_fusion.refs_0_.refs_4_), channel_id=1, source_target_pairs={{0,4},{1,17},{2,6},{3,19},{4,0},{5,21},{6,2},{7,23},{8,12},{9,25},... | collective-permute-start | bytes 417800 | tf_op jit(solution)/shard_map/ppermute | solution.py:400
  37.2 1.6 %collective-permute-start.12 = (bf16[272,256]{1,0:T(8,128)(2,1)S(1)}, bf16[272,256]{1,0:T(8,128)(2,1)S(1)}, u32[]{:S(2)}, u32[]{:S(2)}) collective-permute-start(bf16[272,256]{1,0:T(8,128)(2,1)S(1)} %add_convert_fusion.refs_0_.refs_4_), channel_id=1, source_target_pairs={{0,2},{1,9},{2,0},{3,11},{4,6},{5,13},{6,4},{7,15},{8,10},{9,1},{1... | collective-permute-start | bytes 417800 | tf_op jit(solution)/shard_map/ppermute | solution.py:400
  38.8 0.0 collective-permute-done.9.one_ref
  38.8 1.5 %collective-permute-done.10.two_ref = bf16[256,256]{1,0:T(8,128)(2,1)S(1)} collective-permute-done((bf16[256,256]{1,0:T(8,128)(2,1)S(1)}, bf16[256,256]{1,0:T(8,128)(2,1)S(1)}, u32[]{:S(2)}, u32[]{:S(2)}) %collective-permute-start.10) | collective-permute-done | bytes 131104 | tf_op jit(solution)/shard_map/ppermute | solution.py:391
  40.3 0.7 %shard_map.108 = bf16[256,256]{1,0:T(8,128)(2,1)} custom-call(f32[256,256]{1,0:T(8,128)S(1)} %get-tuple-element.50.own_ref, bf16[256,256]{1,0:T(8,128)(2,1)S(1)} %collective-permute-done.9.one_ref, bf16[256,256]{1,0:T(8,128)(2,1)S(1)} %collective-permute-done.10.two_ref), custom_call_target="tpu_custom_call" | custom-call | flops 30000001024 | bytes 4000000 | tf_op jit(solution)/shard_map/pallas_call | solution.py:493
  41.0 0.0 collective-permute-start.11
  41.0 0.8 %collective-permute-done.16.refs_3_.refs_7_ = bf16[272,256]{1,0:T(8,128)(2,1)S(1)} collective-permute-done((bf16[272,256]{1,0:T(8,128)(2,1)S(1)}, bf16[272,256]{1,0:T(8,128)(2,1)S(1)}, u32[]{:S(2)}, u32[]{:S(2)}) %collective-permute-start.16) | collective-permute-done | bytes 139296 | tf_op jit(solution)/shard_map/ppermute | solution.py:400
  41.9 0.0 collective-permute-start.17
  41.9 0.7 %collective-permute-done.14.refs_2_.refs_6_ = bf16[272,256]{1,0:T(8,128)(2,1)S(1)} collective-permute-done((bf16[272,256]{1,0:T(8,128)(2,1)S(1)}, bf16[272,256]{1,0:T(8,128)(2,1)S(1)}, u32[]{:S(2)}, u32[]{:S(2)}) %collective-permute-start.14) | collective-permute-done | bytes 139296 | tf_op jit(solution)/shard_map/ppermute | solution.py:400
  42.5 0.6 %collective-permute-start.15 = (bf16[272,256]{1,0:T(8,128)(2,1)S(1)}, bf16[272,256]{1,0:T(8,128)(2,1)S(1)}, u32[]{:S(2)}, u32[]{:S(2)}) collective-permute-start(bf16[272,256]{1,0:T(8,128)(2,1)S(1)} %collective-permute-done.14.refs_2_.refs_6_), channel_id=1, source_target_pairs={{0,1},{1,0},{2,3},{3,2},{4,5},{5,4},{6,7},{7,6},{8,9},{9,8},{10,11... | collective-permute-start | bytes 417800 | tf_op jit(solution)/shard_map/ppermute | solution.py:400
  43.1 0.1 collective-permute-done.12.refs_1_.refs_5_
  43.2 0.0 collective-permute-start.13
  43.2 1.0 %shard_map.109 = (f32[256,1024]{1,0:T(8,128)}, f32[1024,256]{1,0:T(8,128)}) custom-call(s32[1]{0:T(128)} %bitcast.1.core, s32[1]{0:T(128)} %bitcast.place.mine_at, s32[1]{0:T(128)} %bitcast.6.theirs_at, bf16[272,256]{1,0:T(8,128)(2,1)S(1)} %add_convert_fusion.refs_0_.refs_4_, bf16[272,256]{1,0:T(8,128)(2,1)S(1)} %collective-permute-done.12.refs_1_.refs_5_, ...), custom_call_target="tpu_custom_call" | custom-call | flops 300000000 | bytes 4000000 | tf_op jit(solution)/shard_map/pallas_call | solution.py:505
  44.3 0.0 collective-permute-done.11.refs_0_.refs_8_
  44.3 0.0 collective-permute-done.17.refs_3_.refs_11_
  44.3 0.0 collective-permute-done.15.refs_2_.refs_10_
  44.3 0.3 collective-permute-done.13.refs_1_.refs_9_
  44.6 1.1 %shard_map.110 = (f32[256,1024]{1,0:T(8,128)}, f32[1024,256]{1,0:T(8,128)}, f32[49,256]{1,0:T(8,128)}) custom-call(s32[1]{0:T(128)} %bitcast.1.core, s32[1]{0:T(128)} %bitcast.place.mine_at, s32[1]{0:T(128)} %bitcast.6.theirs_at, bf16[272,256]{1,0:T(8,128)(2,1)S(1)} %collective-permute-done.11.refs_0_.refs_8_, ...), custom_call_target="tpu_custom_call", output_to_operand_aliasing={{0}: (15, {}), {1}: (16, {})} | custom-call | flops 300000000 | bytes 4000000 | tf_op jit(solution)/shard_map/pallas_call | solution.py:505
Async XLA Ops:
  0.6 10.5 %collective-permute-start = (bf16[256,256]{1,0:T(8,128)(2,1)}, bf16[256,256]{1,0:T(8,128)(2,1)S(1)}, u32[]{:S(2)}, u32[]{:S(2)}) collective-permute-start(bf16[256,256]{1,0:T(8,128)(2,1)} %bitcast.9), channel_id=1, source_target_pairs={{0,4},{4,0},{8,12},{12,8},{16,20},{20,16},{24,28},{28,24},{1,5},{5... | collective-permute-start | bytes 393224 | tf_op jit(solution)/shard_map/ppermute | solution.py:387
  3.6 7.9 %collective-permute-start.1 = (bf16[256,256]{1,0:T(8,128)(2,1)}, bf16[256,256]{1,0:T(8,128)(2,1)S(1)}, u32[]{:S(2)}, u32[]{:S(2)}) collective-permute-start(bf16[256,256]{1,0:T(8,128)(2,1)} %bitcast.10), channel_id=1, source_target_pairs={{0,28},{4,8},{8,4},{12,16},{16,12},{20,24},{24,20},{28,0},{1,29},{... | collective-permute-start | bytes 393224 | tf_op jit(solution)/shard_map/ppermute | solution.py:391
  7.2 0.7 %copy-start = (s32[1,4]{1,0:T(1,128)S(1)}, s32[1,4]{1,0:T(1,128)}, u32[]{:S(2)}) copy-start(s32[1,4]{1,0:T(1,128)} %neighbour.1) | copy-start | bytes 52
  7.2 0.7 %copy-start.1 = (s32[1,4]{1,0:T(1,128)S(1)}, s32[1,4]{1,0:T(1,128)}, u32[]{:S(2)}) copy-start(s32[1,4]{1,0:T(1,128)} %code.1) | copy-start | bytes 52
  14.3 2.0 %collective-permute-start.2 = (bf16[4,256,256]{2,1,0:T(8,128)(2,1)S(1)}, bf16[4,256,256]{2,1,0:T(8,128)(2,1)S(1)}, u32[]{:S(2)}, u32[]{:S(2)}) collective-permute-start(bf16[4,256,256]{2,1,0:T(8,128)(2,1)S(1)} %get-tuple-element.43), channel_id=1, source_target_pairs={{0,1},{1,0},{2,3},{3,2},{4,5},{5,4},{6,7},{7,6},{8,9},{9,8},{10,11... | collective-permute-start | bytes 1572872 | tf_op jit(solution)/shard_map/ppermute | solution.py:400
  16.4 6.0 %collective-permute-start.3 = (bf16[272,256]{1,0:T(8,128)(2,1)S(1)}, bf16[272,256]{1,0:T(8,128)(2,1)S(1)}, u32[]{:S(2)}, u32[]{:S(2)}) collective-permute-start(bf16[272,256]{1,0:T(8,128)(2,1)S(1)} %get-tuple-element.46), channel_id=1, source_target_pairs={{0,6},{1,25},{2,4},{3,27},{4,2},{5,29},{6,0},{7,31},{8,14},{9,17},... | collective-permute-start | bytes 417800 | tf_op jit(solution)/shard_map/ppermute | solution.py:400
  18.0 5.9 %collective-permute-start.4 = (bf16[272,256]{1,0:T(8,128)(2,1)S(1)}, bf16[272,256]{1,0:T(8,128)(2,1)S(1)}, u32[]{:S(2)}, u32[]{:S(2)}) collective-permute-start(bf16[272,256]{1,0:T(8,128)(2,1)S(1)} %get-tuple-element.47), channel_id=1, source_target_pairs={{0,4},{1,17},{2,6},{3,19},{4,0},{5,21},{6,2},{7,23},{8,12},{9,25},... | collective-permute-start | bytes 417800 | tf_op jit(solution)/shard_map/ppermute | solution.py:400
  19.4 5.1 %collective-permute-start.5 = (bf16[272,256]{1,0:T(8,128)(2,1)S(1)}, bf16[272,256]{1,0:T(8,128)(2,1)S(1)}, u32[]{:S(2)}, u32[]{:S(2)}) collective-permute-start(bf16[272,256]{1,0:T(8,128)(2,1)S(1)} %get-tuple-element.48), channel_id=1, source_target_pairs={{0,2},{1,9},{2,0},{3,11},{4,6},{5,13},{6,4},{7,15},{8,10},{9,1},{1... | collective-permute-start | bytes 417800 | tf_op jit(solution)/shard_map/ppermute | solution.py:400
  24.6 10.1 %collective-permute-start.8 = (bf16[272,256]{1,0:T(8,128)(2,1)S(1)}, bf16[272,256]{1,0:T(8,128)(2,1)S(1)}, u32[]{:S(2)}, u32[]{:S(2)}) collective-permute-start(bf16[272,256]{1,0:T(8,128)(2,1)S(1)} %add_convert_fusion.1), channel_id=1, source_target_pairs={{0,24},{1,7},{2,26},{3,5},{4,28},{5,3},{6,30},{7,1},{8,16},{9,15},... | collective-permute-start | bytes 417800 | tf_op jit(solution)/shard_map/ppermute | solution.py:400
  27.4 7.8 %collective-permute-start.7 = (bf16[272,256]{1,0:T(8,128)(2,1)S(1)}, bf16[272,256]{1,0:T(8,128)(2,1)S(1)}, u32[]{:S(2)}, u32[]{:S(2)}) collective-permute-start(bf16[272,256]{1,0:T(8,128)(2,1)S(1)} %add_convert_fusion.1), channel_id=1, source_target_pairs={{0,16},{1,5},{2,18},{3,7},{4,20},{5,1},{6,22},{7,3},{8,24},{9,13},... | collective-permute-start | bytes 417800 | tf_op jit(solution)/shard_map/ppermute | solution.py:400
  27.4 7.8 %collective-permute-start.6 = (bf16[272,256]{1,0:T(8,128)(2,1)S(1)}, bf16[272,256]{1,0:T(8,128)(2,1)S(1)}, u32[]{:S(2)}, u32[]{:S(2)}) collective-permute-start(bf16[272,256]{1,0:T(8,128)(2,1)S(1)} %add_convert_fusion.1), channel_id=1, source_target_pairs={{0,8},{1,3},{2,10},{3,1},{4,12},{5,7},{6,14},{7,5},{8,0},{9,11},{1... | collective-permute-start | bytes 417800 | tf_op jit(solution)/shard_map/ppermute | solution.py:400
  30.4 8.4 %collective-permute-start.9 = (bf16[256,256]{1,0:T(8,128)(2,1)S(1)}, bf16[256,256]{1,0:T(8,128)(2,1)S(1)}, u32[]{:S(2)}, u32[]{:S(2)}) collective-permute-start(bf16[256,256]{1,0:T(8,128)(2,1)S(1)} %get-tuple-element.51), channel_id=1, source_target_pairs={{0,4},{4,0},{8,12},{12,8},{16,20},{20,16},{24,28},{28,24},{1,5},{5... | collective-permute-start | bytes 393224 | tf_op jit(solution)/shard_map/ppermute | solution.py:387
  31.1 9.2 %collective-permute-start.10 = (bf16[256,256]{1,0:T(8,128)(2,1)S(1)}, bf16[256,256]{1,0:T(8,128)(2,1)S(1)}, u32[]{:S(2)}, u32[]{:S(2)}) collective-permute-start(bf16[256,256]{1,0:T(8,128)(2,1)S(1)} %get-tuple-element.52), channel_id=1, source_target_pairs={{0,28},{4,8},{8,4},{12,16},{16,12},{20,24},{24,20},{28,0},{1,29},{... | collective-permute-start | bytes 393224 | tf_op jit(solution)/shard_map/ppermute | solution.py:391
  35.2 6.6 %collective-permute-start.16 = (bf16[272,256]{1,0:T(8,128)(2,1)S(1)}, bf16[272,256]{1,0:T(8,128)(2,1)S(1)}, u32[]{:S(2)}, u32[]{:S(2)}) collective-permute-start(bf16[272,256]{1,0:T(8,128)(2,1)S(1)} %add_convert_fusion.refs_0_.refs_4_), channel_id=1, source_target_pairs={{0,6},{1,25},{2,4},{3,27},{4,2},{5,29},{6,0},{7,31},{8,14},{9,17},... | collective-permute-start | bytes 417800 | tf_op jit(solution)/shard_map/ppermute | solution.py:400
  36.3 6.2 %collective-permute-start.14 = (bf16[272,256]{1,0:T(8,128)(2,1)S(1)}, bf16[272,256]{1,0:T(8,128)(2,1)S(1)}, u32[]{:S(2)}, u32[]{:S(2)}) collective-permute-start(bf16[272,256]{1,0:T(8,128)(2,1)S(1)} %add_convert_fusion.refs_0_.refs_4_), channel_id=1, source_target_pairs={{0,4},{1,17},{2,6},{3,19},{4,0},{5,21},{6,2},{7,23},{8,12},{9,25},... | collective-permute-start | bytes 417800 | tf_op jit(solution)/shard_map/ppermute | solution.py:400
  37.2 6.0 %collective-permute-start.12 = (bf16[272,256]{1,0:T(8,128)(2,1)S(1)}, bf16[272,256]{1,0:T(8,128)(2,1)S(1)}, u32[]{:S(2)}, u32[]{:S(2)}) collective-permute-start(bf16[272,256]{1,0:T(8,128)(2,1)S(1)} %add_convert_fusion.refs_0_.refs_4_), channel_id=1, source_target_pairs={{0,2},{1,9},{2,0},{3,11},{4,6},{5,13},{6,4},{7,15},{8,10},{9,1},{1... | collective-permute-start | bytes 417800 | tf_op jit(solution)/shard_map/ppermute | solution.py:400
  41.0 3.3 %collective-permute-start.11 = (bf16[272,256]{1,0:T(8,128)(2,1)S(1)}, bf16[272,256]{1,0:T(8,128)(2,1)S(1)}, u32[]{:S(2)}, u32[]{:S(2)}) collective-permute-start(bf16[272,256]{1,0:T(8,128)(2,1)S(1)} %add_convert_fusion.refs_0_.refs_4_), channel_id=1, source_target_pairs={{0,1},{1,0},{2,3},{3,2},{4,5},{5,4},{6,7},{7,6},{8,9},{9,8},{10,11... | collective-permute-start | bytes 417800 | tf_op jit(solution)/shard_map/ppermute | solution.py:400
  41.9 2.4 %collective-permute-start.17 = (bf16[272,256]{1,0:T(8,128)(2,1)S(1)}, bf16[272,256]{1,0:T(8,128)(2,1)S(1)}, u32[]{:S(2)}, u32[]{:S(2)}) collective-permute-start(bf16[272,256]{1,0:T(8,128)(2,1)S(1)} %collective-permute-done.16.refs_3_.refs_7_), channel_id=1, source_target_pairs={{0,1},{1,0},{2,3},{3,2},{4,5},{5,4},{6,7},{7,6},{8,9},{9,8},{10,11... | collective-permute-start | bytes 417800 | tf_op jit(solution)/shard_map/ppermute | solution.py:400
  42.5 1.8 %collective-permute-start.15 = (bf16[272,256]{1,0:T(8,128)(2,1)S(1)}, bf16[272,256]{1,0:T(8,128)(2,1)S(1)}, u32[]{:S(2)}, u32[]{:S(2)}) collective-permute-start(bf16[272,256]{1,0:T(8,128)(2,1)S(1)} %collective-permute-done.14.refs_2_.refs_6_), channel_id=1, source_target_pairs={{0,1},{1,0},{2,3},{3,2},{4,5},{5,4},{6,7},{7,6},{8,9},{9,8},{10,11... | collective-permute-start | bytes 417800 | tf_op jit(solution)/shard_map/ppermute | solution.py:400
  43.2 1.4 %collective-permute-start.13 = (bf16[272,256]{1,0:T(8,128)(2,1)S(1)}, bf16[272,256]{1,0:T(8,128)(2,1)S(1)}, u32[]{:S(2)}, u32[]{:S(2)}) collective-permute-start(bf16[272,256]{1,0:T(8,128)(2,1)S(1)} %collective-permute-done.12.refs_1_.refs_5_), channel_id=1, source_target_pairs={{0,1},{1,0},{2,3},{3,2},{4,5},{5,4},{6,7},{7,6},{8,9},{9,8},{10,11... | collective-permute-start | bytes 417800 | tf_op jit(solution)/shard_map/ppermute | solution.py:400
